TPU v7x, 512 devices: a whole 4x4x16 slice. The times are simulated.
512 devices in a mesh: seq: 64 (over z, x), expert: 8 (over y, core).
Axes of the slice: x: 4, y: 4, z: 16, core: 2. Of those that a mesh axis runs over, the one named last changes fastest.
Arguments:
- queries: bfloat16 [2, 16384, 4096], P(None, 'seq', 'expert'), may hold values from -6 to 6
- keys: bfloat16 [2, 16384, 4096], P(None, 'seq', 'expert'), may hold values from -6 to 6
- values: bfloat16 [2, 16384, 4096], P(None, 'seq', 'expert'), may hold values from -6 to 6
- log_decay: float32 [2, 16384, 32], P(None, 'seq', 'expert'), may hold values from -1 to 0
- norm_gain: float32 [4096], P('expert'), may hold values from 0.25 to 1.75
- expert_ids: int32 [512, 2], P('seq'), may hold values from 0 to 7, as said below
- gate_weights: float32 [512, 2], P('seq'), may hold values from 0.2 to 1
- w_gate: bfloat16 [8, 4096, 8192], P('expert', None, 'seq'), may hold values from -0.09375 to 0.09375
- w_up: bfloat16 [8, 4096, 8192], P('expert', None, 'seq'), may hold values from -0.09375 to 0.09375
- w_down: bfloat16 [8, 8192, 4096], P('expert', 'seq'), may hold values from -0.1875 to 0.1875
Outputs:
- attn_out: bfloat16 [2, 16384, 4096], P(None, 'seq', 'expert')
- moe_out: bfloat16 [512, 4096], P('seq', 'expert')
Inputs may be any that keep to these rules, and one draw needn't show every extreme that they name: `expert_ids`: in each aligned block of 8 rows the two experts of a row differ and each expert is named at most 4 times; one expert, the same in every block, is named exactly 4 times in every block.
All inputs are finite; a program needn't handle non-finite values.
Results may differ from a plain program's by a relative error of at most 0.012.
Values may be sent and summed in bfloat16 or wider, within the bound.
No kernel may reach another device: no remote copies, remote signals or barrier semaphores. Data moves between devices by JAX's collectives and lax.ppermute only.
A program may use at most 128 MiB of HBM per device.

v0:
```python
import jax
import jax.numpy as jnp
from jax import lax
from jax.sharding import PartitionSpec as P

EXPERTS = 8
MROWS = 8
CAP = 4


def carried_in(value, axis, combine, identity):
    length, here = (lax.axis_size(axis), lax.axis_index(axis))
    everything = jax.tree.map(lambda part: lax.all_gather(part, axis), value)
    start = jax.tree.map(
        lambda part, zero: jnp.broadcast_to(jnp.asarray(zero, part.dtype), part.shape),
        value,
        identity,
    )

    def hop(k, before):
        reached = k < here
        new = combine(before, jax.tree.map(lambda part: part[k], everything))
        return jax.tree.map(lambda a, b: jnp.where(reached, a, b), new, before)

    return lax.fori_loop(0, length, hop, start)


def carry_join(earlier, later):
    return (earlier[0] * later[0], later[0][:, :, None, None] * earlier[1] + later[1])


def body(
    queries, keys, values, log_decay, norm_gain, expert_ids, gate_weights, w_gate, w_up, w_down
):
    length = queries.shape[1]
    head_count = log_decay.shape[2]
    head_width = queries.shape[2] // head_count
    query_heads = queries.reshape(2, length, head_count, head_width)
    key_heads = keys.reshape(2, length, head_count, head_width)
    value_heads = values.reshape(2, length, head_count, head_width)
    running = jnp.cumsum(log_decay, axis=1)
    block_end = running[:, -1:, :]
    decayed_keys = (key_heads * jnp.exp(block_end - running)[:, :, :, None]).astype(jnp.bfloat16)
    update = jnp.einsum(
        "bshd,bshe->bhde", decayed_keys, value_heads, preferred_element_type=jnp.float32
    )
    factor = jnp.exp(block_end[:, 0, :])
    prefix_factor, prefix_state = carried_in(
        (factor, update), "seq", carry_join, (jnp.ones_like(factor), jnp.zeros_like(update))
    )
    entering = prefix_state.astype(jnp.bfloat16)
    scores = jnp.einsum(
        "bthd,bshd->bhts", query_heads, key_heads, preferred_element_type=jnp.float32
    )
    run_heads = jnp.transpose(running, (0, 2, 1))
    spread_log = run_heads[:, :, :, None] - run_heads[:, :, None, :]
    causal = lax.broadcasted_iota(jnp.int32, (length, length), 0) >= lax.broadcasted_iota(
        jnp.int32, (length, length), 1
    )
    fading = jnp.where(causal[None, None, :, :], jnp.exp(jnp.minimum(spread_log, 0.0)), 0.0)
    weights = (scores * fading).astype(jnp.bfloat16)
    local_part = jnp.einsum(
        "bhts,bshd->bthd", weights, value_heads, preferred_element_type=jnp.float32
    )
    decayed_queries = (query_heads * jnp.exp(running)[:, :, :, None]).astype(jnp.bfloat16)
    carried_part = jnp.einsum(
        "bthd,bhde->bthe", decayed_queries, entering, preferred_element_type=jnp.float32
    )
    combined = local_part + carried_part
    inverse_rms = lax.rsqrt(jnp.mean(combined * combined, axis=-1, keepdims=True) + 1e-06)
    attn_out = (
        (combined * inverse_rms * norm_gain.reshape(head_count, head_width))
        .astype(jnp.bfloat16)
        .reshape(2, length, head_count * head_width)
    )
    column_count = attn_out.shape[2]
    moe_rows = attn_out[:, : MROWS // 2].reshape(MROWS, column_count)
    pair_ids = expert_ids.reshape(-1)
    onehot = (pair_ids[:, None] == jnp.arange(EXPERTS, dtype=jnp.int32)[None, :]).astype(jnp.int32)
    before = jnp.cumsum(onehot, axis=0) - onehot
    slot_index = jnp.sum(before * onehot, axis=1)
    slot_row = slot_index * EXPERTS + pair_ids
    row_pairs = slot_row.reshape(MROWS, 2)
    row_iota = jnp.arange(CAP * EXPERTS, dtype=jnp.int32)[:, None]
    dispatch_matrix = (
        (row_pairs[:, 0][None, :] == row_iota) | (row_pairs[:, 1][None, :] == row_iota)
    ).astype(jnp.bfloat16)
    dispatch = (
        jnp.dot(dispatch_matrix, moe_rows, preferred_element_type=jnp.float32)
        .astype(jnp.bfloat16)
        .reshape(CAP, EXPERTS, column_count)
    )
    arrived = lax.all_to_all(dispatch, "expert", split_axis=1, concat_axis=2, tiled=True)
    piece = lax.all_gather(arrived, "seq", axis=0, tiled=True)
    gate_act = jnp.einsum("rid,idf->rif", piece, w_gate, preferred_element_type=jnp.float32)
    up_act = jnp.einsum("rid,idf->rif", piece, w_up, preferred_element_type=jnp.float32)
    hidden = (jax.nn.silu(gate_act) * up_act).astype(jnp.bfloat16)
    summed = lax.psum(
        jnp.einsum("rif,ifd->rid", hidden, w_down, preferred_element_type=jnp.float32), "seq"
    )
    own_rows = lax.dynamic_slice_in_dim(summed, lax.axis_index("seq") * CAP, CAP, 0)
    expert_out = own_rows.astype(jnp.bfloat16)
    returned = lax.all_to_all(expert_out, "expert", split_axis=2, concat_axis=1, tiled=True)
    flattened = returned.reshape(CAP * EXPERTS, column_count)
    picked = flattened[slot_row].astype(jnp.float32)
    weighted = picked * gate_weights.reshape(-1)[:, None]
    moe_out = weighted.reshape(MROWS, 2, column_count).sum(axis=1).astype(jnp.bfloat16)
    return (attn_out, moe_out)


def solution(mesh):
    placed = (
        P(None, "seq", "expert"),
        P(None, "seq", "expert"),
        P(None, "seq", "expert"),
        P(None, "seq", "expert"),
        P("expert"),
        P("seq", None),
        P("seq", None),
        P("expert", None, "seq"),
        P("expert", None, "seq"),
        P("expert", "seq", None),
    )
    return jax.shard_map(
        body,
        mesh=mesh,
        in_specs=placed,
        out_specs=(P(None, "seq", "expert"), P("seq", "expert")),
        check_vma=False,
    )
```

profile of v0, /device:TPU:1, one launch (start us, length us, event | category | flops | bytes accessed | tf_op | source)
XLA Modules:
  0.0 940.6 jit_solution(16258411254586844181)
XLA Ops:
  8.0 2.4 reduce-window.6
  11.1 1.3 copy.128
  12.4 2.1 fusion.37
  15.2 77.8 %all-gather = f32[128,1,4]{2,1,0:T(1,128)S(1)} all-gather(f32[2,1,4]{2,1,0:T(1,128)S(1)} %copy.111), channel_id=2, replica_groups=mesh['seq'=64,'expert'=8] {'seq'}, dimensions={0}, use_global_device_ids=true | all-gather | bytes 2080 | tf_op jit(solution)/shard_map/all_gather | solution.py:13
  93.3 220.7 %all-gather.7.cloned.1.call-done = f32[128,4,128,128]{3,2,1,0:T(8,128)} async-done(((f32[2,4,128,128]{3,2,1,0:T(8,128)}), f32[128,4,128,128]{3,2,1,0:T(8,128)}) %all-gather.7.cloned.1.call-update) | async-done | bytes 33554448 | tf_op jit(solution)/shard_map/all_gather | solution.py:13
  314.0 77.6 %while.14 = (s32[]{:T(128)}, f32[2,4,128,128]{3,2,1,0:T(8,128)S(1)}, s32[]{:T(128)}, f32[64,2,4]{2,1,0:T(2,128)S(1)}, f32[64,2,4,128,128]{4,3,2,1,0:T(8,128)}, /*index=5*/s32[]{:T(128)}, s32[]{:T(128)}) while((s32[]{:T(128)}, f32[2,4,128,128]{3,2,1,0:T(8,128)S(1)}, s32[]{:T(128)}, f32[64,2,4]{2,1,0:T(2,128)S(1)}, ...), condition=%wide.region_3.4_spmd.clone, body=%wide.region_2.3_spmd.clone.sunk | while | flops 524292 | bytes 1573065 | solution.py:25
  314.0 1.2 fusion.74
  316.5 1.2 fusion.74
  317.7 1.2 fusion.74
  321.3 1.2 fusion.74
  322.5 1.2 fusion.74
  325.0 1.2 fusion.74
  326.2 1.2 fusion.74
  327.4 1.2 fusion.74
  329.8 1.2 fusion.74
  331.0 1.2 fusion.74
  334.7 1.2 fusion.74
  335.9 1.2 fusion.74
  391.6 1.6 convolution_bitcast_fusion.1
  393.2 2.4 multiply_reduce_fusion
  396.9 10.0 %all_to_all.21 = bf16[4,8,512]{2,0,1:T(4,128)(2,1)S(1)} all-to-all(bf16[4,8,512]{2,0,1:T(4,128)(2,1)S(1)} %copy.119), channel_id=1, replica_groups=mesh['seq'=64,'expert'=8] {'expert'}, dimensions={1} | all-to-all | bytes 65536 | tf_op jit(solution)/shard_map/all_to_all | solution.py:93
  407.7 133.1 %all-gather.5.cloned.1.call-done = bf16[256,1,4096]{2,1,0:T(2,128)(2,1)} async-done(((bf16[4,1,4096]{2,1,0:T(2,128)(2,1)}), bf16[256,1,4096]{2,1,0:T(2,128)(2,1)}) %all-gather.5.cloned.1.call-update) | async-done | bytes 2097168 | tf_op jit(solution)/shard_map/all_gather | solution.py:94
  540.8 5.0 fusion.8
  545.8 7.2 convolution_bitcast_fusion
  553.0 276.2 %all-reduce.1 = bf16[256,1,4096]{2,0,1:T(8,128)(2,1)S(1)} all-reduce(f32[256,1,4096]{2,0,1:T(8,128)} %convolution_bitcast_fusion), channel_id=1, replica_groups=mesh['seq'=64,'expert'=8] {'seq'}, use_global_device_ids=true, to_apply=%region_7.8 | all-reduce | flops 1048576 | bytes 6291456 | tf_op jit(solution)/shard_map/psum | solution.py:98
  829.2 2.8 copy.121
  832.6 23.4 %reduce.6 = bf16[4096,4]{1,0:T(8,128)(2,1)} reduce(bf16[4096,1,4]{2,1,0:T(2,128)(2,1)S(1)} %bitcast.131, bf16[]{:T(256)} %broadcast.87), dimensions={1}, to_apply=%bitcast.106.reduce_sub_computation | reduce | bytes 65538
  856.0 3.7 reshape.189
  859.7 63.2 %all-to-all-start.1 = ((bf16[8,2,1024]{2,1,0:T(2,128)(2,1)}), bf16[8,2,1024]{2,1,0:T(2,128)(2,1)S(1)}, u32[]{:S(2)}, u32[]{:S(2)}) async-start(bf16[8,2,1024]{2,1,0:T(2,128)(2,1)} %reshape.189), calls=%async_computation.1 | async-start | bytes 65536 | tf_op jit(solution)/shard_map/all_to_all | solution.py:103
  923.0 4.6 all-to-all-done.1
  927.6 2.7 reshape.190
  930.3 2.0 copy.122
  (176 shorter events, 67.8 us)
Async XLA Ops:
  7.2 538.6 %copy-start = (bf16[1,128,4096]{2,1,0:T(8,128)(2,1)S(1)}, bf16[1,128,4096]{2,1,0:T(8,128)(2,1)}, u32[]{:S(2)}) copy-start(bf16[1,128,4096]{2,1,0:T(8,128)(2,1)} %param.21) | copy-start | bytes 3145732
  7.2 7.5 copy-start.6
  7.2 306.8 %all-gather.7.cloned.1.call-start = ((), (), s32[]{:S(2)}) async-start(), calls=%async_computation.3 | async-start | bytes 34078720 | tf_op jit(solution)/shard_map/all_gather | solution.py:13
  14.5 526.3 %all-gather.5.cloned.1.call-start = ((), (), s32[]{:S(2)}) async-start(), calls=%async_computation.2 | async-start | bytes 4259840 | tf_op jit(solution)/shard_map/all_gather | solution.py:94
  314.0 77.6 %copy-start.4 = (bf16[2,256,512]{2,1,0:T(8,128)(2,1)S(1)}, bf16[2,256,512]{2,1,0:T(8,128)(2,1)}, u32[]{:S(2)}) copy-start(bf16[2,256,512]{2,1,0:T(8,128)(2,1)} %param.12) | copy-start | bytes 1572868
  391.6 1.6 copy-start.3
  393.2 2.5 copy-start.5
  396.0 0.8 copy-start.2
  396.9 148.9 %copy-start.1 = (bf16[1,4096,128]{2,1,0:T(8,128)(2,1)S(1)}, bf16[1,4096,128]{2,1,0:T(8,128)(2,1)}, u32[]{:S(2)}) copy-start(bf16[1,4096,128]{2,1,0:T(8,128)(2,1)} %param.20) | copy-start | bytes 3145732
  832.6 90.3 %copy-start.7 = (f32[8,2]{0,1:T(2,128)S(1)}, f32[8,2]{0,1:T(2,128)}, u32[]{:S(2)}) copy-start(f32[8,2]{0,1:T(2,128)} %param.18) | copy-start | bytes 196
  859.7 67.9 %all-to-all-start.1 = ((bf16[8,2,1024]{2,1,0:T(2,128)(2,1)}), bf16[8,2,1024]{2,1,0:T(2,128)(2,1)S(1)}, u32[]{:S(2)}, u32[]{:S(2)}) async-start(bf16[8,2,1024]{2,1,0:T(2,128)(2,1)} %reshape.189), calls=%async_computation.1 | async-start | bytes 65536 | tf_op jit(solution)/shard_map/all_to_all | solution.py:103
Sparse Core Ops, SparseCore 0:
  14.6 299.3 all-gather.6
  407.7 133.0 all-gather.4
where the time goes:
time: 944 us; the launch traced here: 941 us
  blocking collectives  364 us (39%)
  waiting for transfers between devices  359 us (38%)
  other arithmetic  102 us (11%)
  starting transfers between devices  63.3 us (7%)
  matrix products  18.4 us (2%)
  local copies, waits for them, and re-layouts  17.7 us (2%)
  between operations  14.3 us (2%)
    psum x1, blocking collectives, body(): lax.psum(jnp.einsum('rif,ifd->rid', hidden, w_down, preferred_element_typ...  276 us
    all_gather x1, waiting for transfers between devices, carried_in(): everything = jax.tree.map(lambda part: lax.all_gather(part, axis), value)  221 us
    all_gather x1, waiting for transfers between devices, body(): piece = lax.all_gather(arrived, 'seq', axis=0, tiled=True)  133 us
    all_gather x1, blocking collectives, carried_in(): everything = jax.tree.map(lambda part: lax.all_gather(part, axis), value)  77.8 us
    select_n x64, other arithmetic, hop(): return jax.tree.map(lambda a, b: jnp.where(reached, a, b), new, before)  75.1 us
    all_to_all x1, starting transfers between devices, body(): lax.all_to_all(expert_out, 'expert', split_axis=2, concat_axis=1, tiled=T...  63.2 us
    unnamed x2, other arithmetic  23.4 us
  transfers between devices with their start and end apart: 3, of which 3 were waited for; matrix products, arithmetic and copies ran while one was open for 0% of the time, Pallas kernels for 0%

commit v1 on v0

v1 whole, which is shorter than its diff:
```python
import jax
import jax.numpy as jnp
from jax import lax
from jax.experimental import pallas as pl
from jax.experimental.pallas import tpu as pltpu
from jax.sharding import Mesh
from jax.sharding import PartitionSpec as P

HD = 128
HEADS = 4
PAIRS = 8
TOK = 256
Z, X, Y, CORE = 16, 4, 4, 2
EXPERTS = Y * CORE
MROWS = 8
CAP = 4
COLS = HEADS * HD
OWN = PAIRS // X
PART = OWN * HD // Z
SLOTS = Z * CAP
GROUP = Z * MROWS
INFO = 128
F32 = jnp.float32
BF16 = jnp.bfloat16


def call(kernel, out, name):
    vmem = pl.BlockSpec(memory_space=pltpu.VMEM)
    return pl.pallas_call(
        kernel,
        out_shape=out,
        out_specs=jax.tree.map(lambda _: vmem, out),
        compiler_params=pltpu.CompilerParams(vmem_limit_bytes=40 * 2**20),
        name=name,
    )


def split_log(log):
    first = jnp.floor(log * 0.125) * 8.0
    rest = log - first
    second = jnp.floor(rest * 32.0) * (1.0 / 32.0)
    rest = rest - second
    third = jnp.floor(rest * 8192.0) * (1.0 / 8192.0)
    return first, second, third, rest - third


def stacked_rows(rows):
    index = lax.broadcasted_iota(jnp.int32, (8, HD), 0)
    total = jnp.zeros((8, HD), F32)
    for i, row in enumerate(rows):
        total = jnp.where(index == i, jnp.broadcast_to(row, (8, HD)), total)
    return total


def joined_log(rows, first):
    return (rows[first : first + 1] + rows[first + 1 : first + 2]) + (
        rows[first + 2 : first + 3] + rows[first + 3 : first + 4]
    )


def update_kernel(decay_ref, k_ref, v_ref, run_ref, msg_ref):
    running = decay_ref[...]
    lane = lax.broadcasted_iota(jnp.int32, (PAIRS, TOK), 1)
    shift = 1
    while shift < TOK:
        running = running + jnp.where(lane >= shift, pltpu.roll(running, shift, 1), 0.0)
        shift *= 2
    run_ref[...] = running
    end = running[:, TOK - 1 :]
    to_end = jnp.exp(end - running).T
    for owner in range(X):
        parts, logs = [], []
        for i in range(OWN):
            pair = owner * OWN + i
            b, cols = pair // HEADS, pl.ds(pair % HEADS * HD, HD)
            decayed = (k_ref[b, :, cols].astype(F32) * to_end[:, pair : pair + 1]).astype(BF16)
            parts.append(
                lax.dot_general(
                    decayed, v_ref[b, :, cols], (((0,), (0,)), ((), ())), preferred_element_type=F32
                )
            )
            logs += [jnp.broadcast_to(p, (1, HD)) for p in split_log(end[pair : pair + 1])]
        msg_ref[owner] = jnp.concatenate(parts + [stacked_rows(logs)], axis=0).astype(BF16)


def group_kernel(msg_ref, out_ref):
    total = [None] * OWN
    logs = [None] * OWN
    for x in range(X):
        part = msg_ref[x].astype(F32)
        for i in range(OWN):
            update = part[i * HD : (i + 1) * HD]
            log = joined_log(part, OWN * HD + 4 * i)
            if x == 0:
                total[i], logs[i] = update, log
            else:
                total[i], logs[i] = jnp.exp(log) * total[i] + update, logs[i] + log
    for i in range(OWN):
        info = stacked_rows(split_log(logs[i]))
        for g in range(HD // PART):
            out_ref[i * (HD // PART) + g] = jnp.concatenate(
                [total[i][g * PART : (g + 1) * PART], info], axis=0
            ).astype(BF16)


def scan_kernel(msg_ref, out_ref):
    state = jnp.zeros((PART, HD), F32)
    for z in range(Z):
        out_ref[z] = state.astype(BF16)
        part = msg_ref[z].astype(F32)
        state = jnp.exp(joined_log(part, PART)) * state + part[:PART]


def expand_kernel(prefix_ref, msg_ref, out_ref):
    prefix = prefix_ref[...].astype(F32)
    state = [prefix[i * HD : (i + 1) * HD] for i in range(OWN)]
    for x in range(X):
        out_ref[x] = jnp.concatenate(state, axis=0).astype(BF16)
        if x < X - 1:
            part = msg_ref[x].astype(F32)
            for i in range(OWN):
                factor = jnp.exp(joined_log(part, OWN * HD + 4 * i))
                state[i] = factor * state[i] + part[i * HD : (i + 1) * HD]


def attention_kernel(
    q_ref, k_ref, v_ref, run_ref, state_ref, gain_ref, ids_ref, gates_ref, out_ref, rows_ref
):
    running = run_ref[...]
    columns = running.T
    causal = lax.broadcasted_iota(jnp.int32, (TOK, TOK), 0) >= lax.broadcasted_iota(
        jnp.int32, (TOK, TOK), 1
    )
    for pair in range(PAIRS):
        b, cols = pair // HEADS, pl.ds(pair % HEADS * HD, HD)
        q, v = q_ref[b, :, cols], v_ref[b, :, cols]
        scores = lax.dot_general(
            q, k_ref[b, :, cols], (((1,), (1,)), ((), ())), preferred_element_type=F32
        )
        column = columns[:, pair : pair + 1]
        spread = jnp.minimum(column - running[pair : pair + 1], 0.0)
        weights = jnp.where(causal, scores * jnp.exp(spread), 0.0).astype(BF16)
        decayed = (q.astype(F32) * jnp.exp(column)).astype(BF16)
        o = jnp.dot(weights, v, preferred_element_type=F32) + jnp.dot(
            decayed, state_ref[pair], preferred_element_type=F32
        )
        scale = lax.rsqrt(jnp.mean(o * o, axis=1, keepdims=True) + 1e-6)
        out_ref[b, :, cols] = (o * scale * gain_ref[:, cols]).astype(BF16)
    half = MROWS // 2
    one = out_ref[0, :16].astype(F32)[:MROWS]
    two = out_ref[1, :16].astype(F32)[:MROWS]
    token = lax.broadcasted_iota(jnp.int32, (MROWS, COLS), 0)
    routed = jnp.where(token < half, one, pltpu.roll(two, half, 0))
    ids = ids_ref[...]
    names = [ids[:, 0:1], ids[:, 1:2]]
    earlier = lax.broadcasted_iota(jnp.int32, (MROWS, 1), 0)
    slots = [jnp.zeros((MROWS, 1), jnp.int32), (names[0] == names[1]).astype(jnp.int32)]
    for t in range(MROWS - 1):
        for c in range(2):
            other = jnp.broadcast_to(names[c][t : t + 1], (MROWS, 1))
            for j in range(2):
                same = (other == names[j]) & (earlier > t)
                slots[j] = slots[j] + same.astype(jnp.int32)
    gates = gates_ref[...]
    lane = lax.broadcasted_iota(jnp.int32, (MROWS, INFO), 1)
    info = jnp.zeros((MROWS, INFO), F32)
    facts = [names[0].astype(F32), slots[0].astype(F32), names[1].astype(F32), slots[1].astype(F32)]
    facts += [gates[:, 0:1], gates[:, 1:2]]
    for i, fact in enumerate(facts):
        info = jnp.where(lane == i, jnp.broadcast_to(fact, (MROWS, INFO)), info)
    message = jnp.concatenate([routed, info], axis=1).astype(BF16)
    for z in range(Z):
        rows_ref[z] = message


def slot_lanes(info):
    place = (lax.broadcasted_iota(jnp.int32, (GROUP, 1), 0) // MROWS) * CAP
    lanes = []
    for j in range(2):
        name, slot = info[:, 2 * j : 2 * j + 1], info[:, 2 * j + 1 : 2 * j + 2]
        lanes.append((name * float(SLOTS) + slot).astype(jnp.int32) + place)
    return lanes


def dispatch_kernel(rows_ref, out_ref):
    lane = lax.broadcasted_iota(jnp.int32, (GROUP, EXPERTS * SLOTS), 1)
    for x in range(X):
        first, second = slot_lanes(rows_ref[x, :, COLS:].astype(F32))
        chosen = jnp.where((lane == first) | (lane == second), 1.0, 0.0).astype(BF16)
        sent = lax.dot_general(
            chosen, rows_ref[x, :, :COLS], (((0,), (0,)), ((), ())), preferred_element_type=F32
        ).astype(BF16)
        for e in range(EXPERTS):
            out_ref[e, x * SLOTS : (x + 1) * SLOTS] = sent[e * SLOTS : (e + 1) * SLOTS]


def expert_kernel(rows_ref, gate_ref, up_ref, down_ref, out_ref):
    total = None
    for j in range(EXPERTS):
        part = pl.ds(j * COLS, COLS)
        both = jnp.concatenate([gate_ref[part, :], up_ref[part, :]], axis=1)
        term = jnp.dot(rows_ref[j], both, preferred_element_type=F32)
        total = term if total is None else total + term
    width = gate_ref.shape[1]
    gate, up = total[:, :width], total[:, width:]
    hidden = (gate / (1.0 + jnp.exp(-gate)) * up).astype(BF16)
    for j in range(EXPERTS):
        out_ref[j] = jnp.dot(
            hidden, down_ref[:, pl.ds(j * COLS, COLS)], preferred_element_type=F32
        ).astype(BF16)


def combine_kernel(rows_ref, info_ref, out_ref):
    lane = lax.broadcasted_iota(jnp.int32, (GROUP, EXPERTS * SLOTS), 1)
    for x in range(X):
        info = info_ref[x, :, COLS:].astype(F32)
        first, second = slot_lanes(info)
        mix = jnp.where(lane == first, info[:, 4:5], 0.0) + jnp.where(
            lane == second, info[:, 5:6], 0.0
        )
        own = jnp.concatenate(
            [rows_ref[e, x * SLOTS : (x + 1) * SLOTS] for e in range(EXPERTS)], axis=0
        )
        out_ref[x] = jnp.dot(mix.astype(BF16), own, preferred_element_type=F32).astype(BF16)


def sum_kernel(parts_ref, out_ref):
    total = parts_ref[0].astype(F32)
    for i in range(1, parts_ref.shape[0]):
        total = total + parts_ref[i].astype(F32)
    out_ref[...] = total.astype(BF16)


def swap(array, axis):
    return lax.all_to_all(array, axis, 0, 0, tiled=True)


def body(
    queries, keys, values, log_decay, norm_gain, expert_ids, gate_weights, w_gate, w_up, w_down
):
    shape = jax.ShapeDtypeStruct
    decay = jnp.transpose(log_decay, (0, 2, 1)).reshape(PAIRS, TOK)
    running, message = call(
        update_kernel,
        (shape((PAIRS, TOK), F32), shape((X, OWN * HD + 8, HD), BF16)),
        "update",
    )(decay, keys, values)
    message = swap(message, "x")
    groups = call(group_kernel, shape((Z, PART + 8, HD), BF16), "group")(message)
    groups = swap(groups, "z")
    prefix = call(scan_kernel, shape((Z, PART, HD), BF16), "scan")(groups)
    prefix = swap(prefix, "z").reshape(OWN * HD, HD)
    states = call(expand_kernel, shape((X, OWN * HD, HD), BF16), "expand")(prefix, message)
    states = swap(states, "x").reshape(PAIRS, HD, HD)
    attn_out, rows = call(
        attention_kernel,
        (shape((2, TOK, COLS), BF16), shape((Z, MROWS, COLS + INFO), BF16)),
        "attention",
    )(
        queries, keys, values, running, states, norm_gain.reshape(1, COLS), expert_ids, gate_weights
    )
    rows = swap(rows, "z").reshape(GROUP, COLS + INFO)
    rows = lax.all_gather(rows, "x", axis=0)
    slots = call(dispatch_kernel, shape((EXPERTS, X * SLOTS, COLS), BF16), "dispatch")(rows)
    slots = swap(slots, ("y", "core"))
    slots = call(expert_kernel, shape((EXPERTS, X * SLOTS, COLS), BF16), "experts")(
        slots, w_gate[0], w_up[0], w_down[0]
    )
    slots = swap(slots, ("y", "core"))
    share = call(combine_kernel, shape((X, GROUP, COLS), BF16), "combine")(slots, rows)
    share = swap(share, "x")
    share = call(sum_kernel, shape((GROUP, COLS), BF16), "sum_x")(share)
    share = swap(share.reshape(Z, MROWS, COLS), "z")
    moe_out = call(sum_kernel, shape((MROWS, COLS), BF16), "sum_z")(share)
    return (attn_out, moe_out)


def solution(mesh):
    fine = Mesh(mesh.devices.reshape(Z, X, Y, CORE), ("z", "x", "y", "core"))
    seq, expert = ("z", "x"), ("y", "core")
    placed = (
        P(None, seq, expert),
        P(None, seq, expert),
        P(None, seq, expert),
        P(None, seq, expert),
        P(expert),
        P(seq, None),
        P(seq, None),
        P(expert, None, seq),
        P(expert, None, seq),
        P(expert, seq, None),
    )
    return jax.shard_map(
        body,
        mesh=fine,
        in_specs=placed,
        out_specs=(P(None, seq, expert), P(seq, expert)),
        check_vma=False,
    )
```

time: 944 us -> 200 us (0.21)
  waiting for transfers between devices: 359 us -> 5.32 us
  blocking collectives: 364 us -> 174 us
  other arithmetic: 102 us -> 0 us
  starting transfers between devices: 63.3 us -> 3.41 us
  matrix products: 18.4 us -> 0 us
  local copies, waits for them, and re-layouts: 17.7 us -> 3.01 us
  between operations: 14.3 us -> 0.75 us
  Pallas kernels: 0 us -> 10.8 us
    all_gather x2 -> x0, waiting for transfers between devices: 354 us -> none  [the longest x1 221 us: carried_in(): everything = jax.tree.map(lambda part: lax.all_gather(part, axis), value)]
    psum x1 -> x0, blocking collectives: 276 us -> none  [body(): lax.psum(jnp.einsum('rif,ifd->rid', hidden, w_down, preferred_element_typ...]
    all_to_all x1 -> x8, blocking collectives: 10 us -> 164 us  [swap(): return lax.all_to_all(array, axis, 0, 0, tiled=True)]
    select_n x65 -> x0, other arithmetic: 75.1 us -> none  [the longest x64 75.1 us: hop(): return jax.tree.map(lambda a, b: jnp.where(reached, a, b), new, before)]
    all_gather x1, blocking collectives: 77.8 us -> 10.4 us  [body(): rows = lax.all_gather(rows, 'x', axis=0)]
    all_to_all x1, starting transfers between devices: 63.2 us -> 3.41 us  [swap(): return lax.all_to_all(array, axis, 0, 0, tiled=True)]
    unnamed x2 -> x0, other arithmetic: 23.4 us -> none
    dot_general x6 -> x0, matrix products: 18.4 us -> none  [the longest x1 7.21 us: body(): jnp.einsum('rif,ifd->rid', hidden, w_down, preferred_element_type=jnp.flo...]
  transfers between devices with their start and end apart: 3 -> 1, of which waited for: 3 -> 1; matrix products, arithmetic and copies ran while one was open for 0% -> 0% of each run, Pallas kernels for 0% -> 0%
where the time goes in v1:
time: 200 us; the launch traced here: 198 us
  blocking collectives  174 us (87%)
  Pallas kernels  10.8 us (5%)
  waiting for transfers between devices  5.32 us (3%)
  starting transfers between devices  3.41 us (2%)
  local copies, waits for them, and re-layouts  3.01 us (2%)
    all_to_all x8, blocking collectives, swap(): return lax.all_to_all(array, axis, 0, 0, tiled=True)  164 us
    all_gather x1, blocking collectives, body(): rows = lax.all_gather(rows, 'x', axis=0)  10.4 us
    all_to_all x1, waiting for transfers between devices, swap(): return lax.all_to_all(array, axis, 0, 0, tiled=True)  5.32 us
  transfers between devices with their start and end apart: 1, of which 1 were waited for; matrix products, arithmetic and copies ran while one was open for 0% of the time, Pallas kernels for 0%

profile of v1, /device:TPU:1, one launch (start us, length us, event | category | flops | bytes accessed | tf_op | source)
XLA Modules:
  0.0 197.6 jit_solution(7599933674885844271)
XLA Ops:
  0.6 0.0 copy-start.9
  0.6 0.0 copy-start.10
  0.7 0.7 reshape.19.decay_ref
  1.4 1.0 copy-done
  2.4 1.0 copy-done.2
  3.5 1.4 update.1
  4.9 10.2 %all_to_all.45.msg_ref = bf16[4,264,128]{2,1,0:T(8,128)(2,1)S(1)} all-to-all(bf16[4,264,128]{2,1,0:T(8,128)(2,1)S(1)} %get-tuple-element.7), channel_id=1, replica_groups=mesh['z'=16,'x'=4,'y'=4,'core'=2] {'x'}, dimensions={0} | all-to-all | bytes 540672 | tf_op jit(solution)/shard_map/all_to_all | solution.py:235
  15.1 0.1 group.1
  15.2 26.6 %all_to_all.46.msg_ref = bf16[16,24,128]{2,1,0:T(8,128)(2,1)S(1)} all-to-all(bf16[16,24,128]{2,1,0:T(8,128)(2,1)S(1)} %group.1), channel_id=1, replica_groups=mesh['z'=16,'x'=4,'y'=4,'core'=2] {'z'}, dimensions={0} | all-to-all | bytes 196608 | tf_op jit(solution)/shard_map/all_to_all | solution.py:235
  41.8 14.8 %all_to_all.47 = bf16[16,16,128]{2,1,0:T(8,128)(2,1)S(1)} all-to-all(bf16[16,16,128]{2,1,0:T(8,128)(2,1)S(1)} %scan.1), channel_id=1, replica_groups=mesh['z'=16,'x'=4,'y'=4,'core'=2] {'z'}, dimensions={0} | all-to-all | bytes 131072 | tf_op jit(solution)/shard_map/all_to_all | solution.py:235
  56.6 0.8 expand.1
  57.4 3.4 %all-to-all-start.3 = ((bf16[4,256,128]{2,1,0:T(8,128)(2,1)}), bf16[4,256,128]{2,1,0:T(8,128)(2,1)S(1)}, u32[]{:S(2)}, u32[]{:S(2)}) async-start(bf16[4,256,128]{2,1,0:T(8,128)(2,1)} %expand.1), calls=%async_computation.3 | async-start | bytes 524288 | tf_op jit(solution)/shard_map/all_to_all | solution.py:235
  60.8 0.1 copy.14.ids_ref
  60.9 0.0 copy-done.10
  60.9 0.1 copy.15.gates_ref
  61.0 5.3 %all-to-all-done.3 = bf16[4,256,128]{2,1,0:T(8,128)(2,1)S(1)} async-done(((bf16[4,256,128]{2,1,0:T(8,128)(2,1)}), bf16[4,256,128]{2,1,0:T(8,128)(2,1)S(1)}, u32[]{:S(2)}, u32[]{:S(2)}) %all-to-all-start.3) | async-done | bytes 262176 | tf_op jit(solution)/shard_map/all_to_all | solution.py:235
  66.3 3.3 %attention.1 = (bf16[2,256,512]{2,1,0:T(8,128)(2,1)}, bf16[16,8,640]{2,1,0:T(8,128)(2,1)S(1)}) custom-call(bf16[2,256,512]{2,1,0:T(8,128)(2,1)S(1)} %copy-done.7, bf16[2,256,512]{2,1,0:T(8,128)(2,1)S(1)} %copy-done.1, bf16[2,256,512]{2,1,0:T(8,128)(2,1)S(1)} %copy-done.3, f32[8,256]{1,0:T(8,128)S(1)} %get-tuple-element.6.run_ref, ...), custom_call_target="tpu_custom_call" | custom-call | tf_op jit(solution)/shard_map/attention/pallas_call | solution.py:255
  69.7 15.1 %all_to_all.48 = bf16[16,8,640]{2,1,0:T(8,128)(2,1)S(1)} all-to-all(bf16[16,8,640]{2,1,0:T(8,128)(2,1)S(1)} %get-tuple-element.9), channel_id=1, replica_groups=mesh['z'=16,'x'=4,'y'=4,'core'=2] {'z'}, dimensions={0} | all-to-all | bytes 327680 | tf_op jit(solution)/shard_map/all_to_all | solution.py:235
  84.7 10.4 %all_gather.3.rows_ref.info_ref = bf16[4,128,640]{2,1,0:T(8,128)(2,1)S(1)} all-gather(bf16[1,128,640]{2,1,0:T(8,128)(2,1)S(1)} %bitcast.16), channel_id=1, replica_groups=mesh['z'=16,'x'=4,'y'=4,'core'=2] {'x'}, dimensions={0}, use_global_device_ids=true | all-gather | bytes 819200 | tf_op jit(solution)/shard_map/all_gather | solution.py:263
  95.2 1.2 dispatch.1
  96.4 0.0 copy-start.4
  96.4 0.0 copy-start.5
  96.4 0.0 copy-start.6
  96.4 40.5 %all_to_all.49.rows_ref = bf16[8,256,512]{2,1,0:T(8,128)(2,1)S(1)} all-to-all(bf16[8,256,512]{2,1,0:T(8,128)(2,1)S(1)} %dispatch.1), channel_id=1, replica_groups=mesh['z'=16,'x'=4,'y'=4,'core'=2] {'y','core'}, dimensions={0} | all-to-all | bytes 4194304 | tf_op jit(solution)/shard_map/all_to_all | solution.py:235
  136.9 0.0 copy-done.4
  136.9 2.4 %experts.1 = bf16[8,256,512]{2,1,0:T(8,128)(2,1)S(1)} custom-call(bf16[8,256,512]{2,1,0:T(8,128)(2,1)S(1)} %all_to_all.49.rows_ref, bf16[4096,128]{1,0:T(8,128)(2,1)S(1)} %bitcast.9, bf16[4096,128]{1,0:T(8,128)(2,1)S(1)} %bitcast.10, bf16[128,4096]{1,0:T(8,128)(2,1)S(1)} %bitcast.11), custom_call_target="tpu_custom_call" | custom-call | tf_op jit(solution)/shard_map/experts/pallas_call | solution.py:266
  139.3 29.9 %all_to_all.50.rows_ref = bf16[8,256,512]{2,1,0:T(8,128)(2,1)S(1)} all-to-all(bf16[8,256,512]{2,1,0:T(8,128)(2,1)S(1)} %experts.1), channel_id=1, replica_groups=mesh['z'=16,'x'=4,'y'=4,'core'=2] {'y','core'}, dimensions={0} | all-to-all | bytes 4194304 | tf_op jit(solution)/shard_map/all_to_all | solution.py:235
  169.3 0.9 combine.1
  170.2 10.7 %all_to_all.51.parts_ref = bf16[4,128,512]{2,1,0:T(8,128)(2,1)S(1)} all-to-all(bf16[4,128,512]{2,1,0:T(8,128)(2,1)S(1)} %combine.1), channel_id=1, replica_groups=mesh['z'=16,'x'=4,'y'=4,'core'=2] {'x'}, dimensions={0} | all-to-all | bytes 1048576 | tf_op jit(solution)/shard_map/all_to_all | solution.py:235
  180.9 0.1 sum_x.1
  181.0 16.0 %all_to_all.52.parts_ref = bf16[16,8,512]{2,1,0:T(8,128)(2,1)S(1)} all-to-all(bf16[16,8,512]{2,1,0:T(8,128)(2,1)S(1)} %bitcast.13), channel_id=1, replica_groups=mesh['z'=16,'x'=4,'y'=4,'core'=2] {'z'}, dimensions={0} | all-to-all | bytes 262144 | tf_op jit(solution)/shard_map/all_to_all | solution.py:235
  197.0 0.6 sum_z.1
  (14 shorter events, 0.1 us)
Async XLA Ops:
  0.6 60.2 %copy-start.9 = (s32[8,2]{0,1:T(2,128)S(1)}, s32[8,2]{0,1:T(2,128)}, u32[]{:S(2)}) copy-start(s32[8,2]{0,1:T(2,128)} %param.15) | copy-start | bytes 196
  0.6 60.3 %copy-start.10 = (f32[8,2]{0,1:T(2,128)S(1)}, f32[8,2]{0,1:T(2,128)}, u32[]{:S(2)}) copy-start(f32[8,2]{0,1:T(2,128)} %param.16) | copy-start | bytes 196
  0.7 65.7 %copy-start.8 = (f32[512]{0:T(512)S(1)}, f32[512]{0:T(512)}, u32[]{:S(2)}) copy-start(f32[512]{0:T(512)} %param.14) | copy-start | bytes 6148
  1.4 1.0 copy-start
  2.4 1.0 copy-start.2
  3.5 62.8 %copy-start.1 = (bf16[2,256,512]{2,1,0:T(8,128)(2,1)S(1)}, bf16[2,256,512]{2,1,0:T(8,128)(2,1)}, u32[]{:S(2)}) copy-start(bf16[2,256,512]{2,1,0:T(8,128)(2,1)} %k_ref.3) | copy-start | bytes 1572868
  3.5 62.8 %copy-start.3 = (bf16[2,256,512]{2,1,0:T(8,128)(2,1)S(1)}, bf16[2,256,512]{2,1,0:T(8,128)(2,1)}, u32[]{:S(2)}) copy-start(bf16[2,256,512]{2,1,0:T(8,128)(2,1)} %v_ref.3) | copy-start | bytes 1572868
  3.5 62.8 %copy-start.7 = (bf16[2,256,512]{2,1,0:T(8,128)(2,1)S(1)}, bf16[2,256,512]{2,1,0:T(8,128)(2,1)}, u32[]{:S(2)}) copy-start(bf16[2,256,512]{2,1,0:T(8,128)(2,1)} %q_ref.1) | copy-start | bytes 1572868
  57.4 8.9 %all-to-all-start.3 = ((bf16[4,256,128]{2,1,0:T(8,128)(2,1)}), bf16[4,256,128]{2,1,0:T(8,128)(2,1)S(1)}, u32[]{:S(2)}, u32[]{:S(2)}) async-start(bf16[4,256,128]{2,1,0:T(8,128)(2,1)} %expand.1), calls=%async_computation.3 | async-start | bytes 524288 | tf_op jit(solution)/shard_map/all_to_all | solution.py:235
  96.4 40.6 %copy-start.4 = (bf16[1,4096,128]{2,1,0:T(8,128)(2,1)S(1)}, bf16[1,4096,128]{2,1,0:T(8,128)(2,1)}, u32[]{:S(2)}) copy-start(bf16[1,4096,128]{2,1,0:T(8,128)(2,1)} %param.17) | copy-start | bytes 3145732
  96.4 40.6 %copy-start.5 = (bf16[1,4096,128]{2,1,0:T(8,128)(2,1)S(1)}, bf16[1,4096,128]{2,1,0:T(8,128)(2,1)}, u32[]{:S(2)}) copy-start(bf16[1,4096,128]{2,1,0:T(8,128)(2,1)} %param.18) | copy-start | bytes 3145732
  96.4 40.6 %copy-start.6 = (bf16[1,128,4096]{2,1,0:T(8,128)(2,1)S(1)}, bf16[1,128,4096]{2,1,0:T(8,128)(2,1)}, u32[]{:S(2)}) copy-start(bf16[1,128,4096]{2,1,0:T(8,128)(2,1)} %param.19) | copy-start | bytes 3145732

commit v2 on v1

v2 whole, which is shorter than its diff:
```python
import jax
import jax.numpy as jnp
from jax import lax
from jax.experimental import pallas as pl
from jax.experimental.pallas import tpu as pltpu
from jax.sharding import Mesh
from jax.sharding import PartitionSpec as P

HD = 128
HEADS = 4
PAIRS = 8
TOK = 256
Z, X, Y, CORE = 16, 4, 4, 2
EXPERTS = Y * CORE
MROWS = 8
CAP = 4
COLS = HEADS * HD
OWN = PAIRS // X
PART = OWN * HD // Z
HALF = MROWS // 2
FEW = 16
GROUP = Z * MROWS
AT_LOGS = OWN * HD
AT_Q = AT_LOGS + 8
AT_LOCAL = AT_Q + 8
AT_FACTS = AT_LOCAL + 16
F32 = jnp.float32
BF16 = jnp.bfloat16


def call(kernel, out, name, scratch=()):
    vmem = pl.BlockSpec(memory_space=pltpu.VMEM)
    return pl.pallas_call(
        kernel,
        out_shape=out,
        out_specs=jax.tree.map(lambda _: vmem, out),
        scratch_shapes=scratch,
        compiler_params=pltpu.CompilerParams(vmem_limit_bytes=40 * 2**20),
        name=name,
    )


def split_log(log):
    first = jnp.floor(log * 0.125) * 8.0
    rest = log - first
    second = jnp.floor(rest * 32.0) * (1.0 / 32.0)
    rest = rest - second
    third = jnp.floor(rest * 8192.0) * (1.0 / 8192.0)
    return first, second, third, rest - third


def stacked_rows(rows):
    index = lax.broadcasted_iota(jnp.int32, (8, HD), 0)
    total = jnp.zeros((8, HD), F32)
    for i, row in enumerate(rows):
        total = jnp.where(index == i, jnp.broadcast_to(row, (8, HD)), total)
    return total


def joined_log(rows, first):
    return (rows[first : first + 1] + rows[first + 1 : first + 2]) + (
        rows[first + 2 : first + 3] + rows[first + 3 : first + 4]
    )


def prefix_sums(rows):
    lane = lax.broadcasted_iota(jnp.int32, rows.shape, 1)
    shift = 1
    while shift < TOK:
        rows = rows + jnp.where(lane >= shift, pltpu.roll(rows, shift, 1), 0.0)
        shift *= 2
    return rows


def fading_scores(q, k, column, row):
    scores = lax.dot_general(q, k, (((1,), (1,)), ((), ())), preferred_element_type=F32)
    causal = lax.broadcasted_iota(jnp.int32, scores.shape, 0) >= lax.broadcasted_iota(
        jnp.int32, scores.shape, 1
    )
    fading = jnp.exp(jnp.minimum(column - row, 0.0))
    return jnp.where(causal, scores * fading, 0.0).astype(BF16)


def beside(one, two):
    row = lax.broadcasted_iota(jnp.int32, one.shape, 0)
    return jnp.where(row < HALF, one, pltpu.roll(two, HALF, 0))


def two_parts(array):
    coarse = array.astype(BF16).astype(F32)
    return coarse, array - coarse


def route_facts(ids_ref, gates_ref, facts_ref):
    facts_ref[...] = jnp.zeros((8, HD), F32)
    facts_ref[0:2, 0:MROWS] = ids_ref[...].astype(F32)
    facts_ref[6:8, 0:MROWS] = gates_ref[...]
    names = facts_ref[0:2, :]
    lane = lax.broadcasted_iota(jnp.int32, (2, HD), 1)
    choice = lax.broadcasted_iota(jnp.int32, (2, HD), 0)
    slots = jnp.where((choice == 1) & (names[0:1] == names[1:2]), 1.0, 0.0)
    for t in range(MROWS - 1):
        for c in range(2):
            same = (names[c : c + 1, t : t + 1] == names) & (lane > t)
            slots = slots + jnp.where(same, 1.0, 0.0)
    facts_ref[4:6, :] = jnp.where(lane < MROWS, names * float(CAP) + slots, 0.0)
    facts_ref[0:2, :] = jnp.zeros((2, HD), F32)


def update_kernel(
    decay_ref, q_ref, k_ref, v_ref, ids_ref, gates_ref, run_ref, msg_ref, facts_ref
):
    running = prefix_sums(decay_ref[...])
    run_ref[...] = running
    end = running[:, TOK - 1 :]
    to_end = jnp.exp(end - running).T
    columns = running.T[:FEW]
    route_facts(ids_ref, gates_ref, facts_ref)
    for owner in range(X):
        parts, logs, qs, locals_ = [], [], [], []
        for i in range(OWN):
            pair = owner * OWN + i
            b, cols = pair // HEADS, pl.ds(pair % HEADS * HD, HD)
            decayed = (k_ref[b, :, cols].astype(F32) * to_end[:, pair : pair + 1]).astype(BF16)
            parts.append(
                lax.dot_general(
                    v_ref[b, :, cols], decayed, (((0,), (0,)), ((), ())), preferred_element_type=F32
                )
            )
            logs += [jnp.broadcast_to(p, (1, HD)) for p in split_log(end[pair : pair + 1])]
            q, column = q_ref[b, :FEW, cols], columns[:, pair : pair + 1]
            weights = fading_scores(
                q, k_ref[b, :FEW, cols], column, running[pair : pair + 1, :FEW]
            )
            local = jnp.dot(weights, v_ref[b, :FEW, cols], preferred_element_type=F32)
            locals_.append(local[:8])
            qs.append((q.astype(F32) * jnp.exp(column))[:8])
        local = two_parts(beside(*locals_))
        msg_ref[owner] = jnp.concatenate(
            parts + [stacked_rows(logs), beside(*qs), local[0], local[1], facts_ref[...]], axis=0
        ).astype(BF16)


def placed(rows, i, x):
    row = lax.broadcasted_iota(jnp.int32, rows.shape, 0)
    moved = rows if i == x % 2 else pltpu.roll(rows, HALF, 0)
    moved = jnp.where(row // HALF == x % 2, moved, 0.0)
    zero = jnp.zeros_like(moved)
    return jnp.concatenate([moved, zero] if x < 2 else [zero, moved], axis=0)


def tall(rows):
    return jnp.concatenate([rows, jnp.zeros((HD - rows.shape[0], HD), F32)], axis=0)


def group_kernel(msg_ref, out_ref):
    lane = lax.broadcasted_iota(jnp.int32, (8, HD), 1)
    facts = jnp.zeros((8, HD), F32)
    for x in range(X):
        own = msg_ref[x].astype(F32)[AT_FACTS:]
        for b in range(2):
            only = jnp.where(lane // HALF == b, own, 0.0)
            shift = b * 16 + x * HALF - b * HALF
            facts = facts + (pltpu.roll(only, shift, 1) if shift else only)
    for i in range(OWN):
        total, log, queries, near, inner = None, None, 0.0, 0.0, 0.0
        for x in range(X):
            part = msg_ref[x].astype(F32)
            update = part[i * HD : (i + 1) * HD]
            own_log = joined_log(part, AT_LOGS + 4 * i)
            q = placed(part[AT_Q : AT_Q + 8], i, x)
            local = part[AT_LOCAL : AT_LOCAL + 8] + part[AT_LOCAL + 8 : AT_LOCAL + 16]
            near = near + placed(local, i, x)
            if x == 0:
                queries = q
                total, log = update, own_log
            else:
                inner = inner + lax.dot_general(
                    total.astype(BF16),
                    tall(q).astype(BF16),
                    (((1,), (1,)), ((), ())),
                    preferred_element_type=F32,
                )
                queries = queries + q * jnp.exp(log)
                total, log = jnp.exp(own_log) * total + update, log + own_log
        coarse, rest = two_parts(inner + tall(near).T)
        rows = coarse + pltpu.roll(rest, 16, 1)
        info = stacked_rows(split_log(log)) + facts
        for g in range(HD // PART):
            piece = slice(g * PART, (g + 1) * PART)
            out_ref[i * (HD // PART) + g] = jnp.concatenate(
                [total[piece], info, queries, rows[piece]], axis=0
            ).astype(BF16)


def scan_kernel(msg_ref, out_ref, facts_ref):
    state = jnp.zeros((PART, HD), F32)
    lane = lax.broadcasted_iota(jnp.int32, (16, HD), 1)
    states, queries = [], []
    near = [jnp.zeros((PART, HD), F32) for _ in range(2)]
    facts = [jnp.zeros((8, HD), F32) for _ in range(4)]
    for z in range(Z):
        states.append(state)
        part = msg_ref[z].astype(F32)
        info, query, rows = part[16:24], part[24:40], part[40:56]
        queries.append(query)
        half, shift = z // 8, z % 8 * 16
        rows = jnp.where(lane < 16, rows + pltpu.roll(rows, HD - 16, 1), 0.0)
        near[half] = near[half] + (pltpu.roll(rows, shift, 1) if shift else rows)
        for b in range(2):
            only = jnp.where(lane[:8] // 16 == b, info, 0.0)
            move = (shift - b * 16) % HD
            place = half * 2 + b
            facts[place] = facts[place] + (pltpu.roll(only, move, 1) if move else only)
        state = jnp.exp(joined_log(part, PART)) * state + part[:PART]
    far = lax.dot_general(
        jnp.concatenate(states, axis=0).astype(BF16),
        jnp.concatenate(queries, axis=0).astype(BF16),
        (((1,), (1,)), ((), ())),
        preferred_element_type=F32,
    )
    row = lax.broadcasted_iota(jnp.int32, far.shape, 0)
    column = lax.broadcasted_iota(jnp.int32, far.shape, 1)
    far = jnp.where(row // 16 == column // 16, far, 0.0)
    total = jnp.concatenate(near, axis=1)
    for z in range(Z):
        total = total + far[z * PART : (z + 1) * PART]
    for z in range(Z):
        out_ref[z] = jnp.concatenate(
            [states[z], total[:, :HD], total[:, HD:]], axis=0
        ).astype(BF16)
    facts_ref[...] = jnp.concatenate(facts, axis=1)


def expand_kernel(back_ref, msg_ref, gain_ref, out_ref):
    odd = lax.rem(lax.axis_index("x"), 2)
    gain = jnp.where(odd == 1, gain_ref[:, OWN * HD :], gain_ref[:, : OWN * HD])
    back = [back_ref[c].astype(F32) for c in range(Z)]
    each = Z // OWN
    state, rows = [], []
    for i in range(OWN):
        mine = back[i * each : (i + 1) * each]
        state.append(jnp.concatenate([part[:PART] for part in mine], axis=0))
        for half in range(2):
            first = PART * (1 + half)
            o = jnp.concatenate([part[first : first + PART] for part in mine], axis=0).T
            scale = lax.rsqrt(jnp.mean(o * o, axis=1, keepdims=True) + 1e-6)
            rows.append((o * scale * gain[:, i * HD : (i + 1) * HD]).astype(BF16))
    for x in range(X):
        out_ref[x] = jnp.concatenate([part.astype(BF16) for part in state] + rows, axis=0)
        if x < X - 1:
            part = msg_ref[x].astype(F32)
            for i in range(OWN):
                factor = jnp.exp(joined_log(part, AT_LOGS + 4 * i))
                state[i] = factor * state[i] + part[i * HD : (i + 1) * HD]


def attention_kernel(q_ref, k_ref, v_ref, run_ref, state_ref, gain_ref, out_ref):
    running = run_ref[...]
    columns = running.T
    for pair in range(PAIRS):
        b, cols = pair // HEADS, pl.ds(pair % HEADS * HD, HD)
        q, column = q_ref[b, :, cols], columns[:, pair : pair + 1]
        state = state_ref[pair // OWN, pair % OWN * HD : (pair % OWN + 1) * HD]
        weights = fading_scores(q, k_ref[b, :, cols], column, running[pair : pair + 1])
        decayed = (q.astype(F32) * jnp.exp(column)).astype(BF16)
        o = jnp.dot(
            weights, v_ref[b, :, cols], preferred_element_type=F32
        ) + lax.dot_general(
            decayed, state, (((1,), (1,)), ((), ())), preferred_element_type=F32
        )
        scale = lax.rsqrt(jnp.mean(o * o, axis=1, keepdims=True) + 1e-6)
        out_ref[b, :, cols] = (o * scale * gain_ref[:, cols]).astype(BF16)


def slot_rows(facts_ref, half):
    facts = facts_ref[:, half * 2 * HD : (half + 1) * 2 * HD]
    lane = lax.broadcasted_iota(jnp.int32, (1, 2 * HD), 1)
    place = lane % HD // CAP * CAP
    rows = []
    for j in range(2):
        code = facts[4 + j : 5 + j].astype(jnp.int32)
        rows.append(code // CAP * HD + code % CAP + place)
    return rows, [facts[6:7], facts[7:8]]


def dispatch_kernel(rows_ref, facts_ref, out_ref):
    index = lax.broadcasted_iota(jnp.int32, (EXPERTS * HD, 2 * HD), 0)
    for half in range(2):
        (first, second), _ = slot_rows(facts_ref, half)
        chosen = jnp.where((index == first) | (index == second), 1.0, 0.0).astype(BF16)
        tokens = pl.ds(half * HD, HD)
        rows = jnp.concatenate(
            [
                jnp.concatenate(
                    [
                        rows_ref[2 * b + h // OWN, pl.ds((OWN + h % OWN * 2 + half) * HD, HD)]
                        for h in range(HEADS)
                    ],
                    axis=1,
                )
                for b in range(2)
            ],
            axis=0,
        )
        sent = jnp.dot(chosen, rows, preferred_element_type=F32).astype(BF16)
        for e in range(EXPERTS):
            out_ref[e, tokens] = sent[e * HD : (e + 1) * HD]


def expert_kernel(rows_ref, gate_ref, up_ref, down_ref, out_ref):
    total = None
    for j in range(EXPERTS):
        part = pl.ds(j * COLS, COLS)
        both = jnp.concatenate([gate_ref[part, :], up_ref[part, :]], axis=1)
        term = jnp.dot(rows_ref[j], both, preferred_element_type=F32)
        total = term if total is None else total + term
    width = gate_ref.shape[1]
    gate, up = total[:, :width], total[:, width:]
    hidden = (gate / (1.0 + jnp.exp(-gate)) * up).astype(BF16)
    for j in range(EXPERTS):
        out_ref[j] = jnp.dot(
            hidden, down_ref[:, pl.ds(j * COLS, COLS)], preferred_element_type=F32
        ).astype(BF16)


def combine_kernel(rows_ref, facts_ref, out_ref):
    index = lax.broadcasted_iota(jnp.int32, (EXPERTS * HD, 2 * HD), 0)
    for half in range(2):
        (first, second), gates = slot_rows(facts_ref, half)
        mix = jnp.where(index == first, gates[0], 0.0) + jnp.where(index == second, gates[1], 0.0)
        own = jnp.concatenate(
            [rows_ref[e, half * HD : (half + 1) * HD] for e in range(EXPERTS)], axis=0
        )
        total = lax.dot_general(
            mix.astype(BF16), own, (((0,), (0,)), ((), ())), preferred_element_type=F32
        )
        for k in range(16):
            one, two = total[k * 8 : (k + 1) * 8], total[HD + k * 8 : HD + (k + 1) * 8]
            row = lax.broadcasted_iota(jnp.int32, one.shape, 0)
            even = jnp.where(row < HALF, one, pltpu.roll(two, HALF, 0))
            odd = jnp.where(row < HALF, pltpu.roll(one, HALF, 0), two)
            z, x = half * 8 + k // 2, k % 2 * 2
            out_ref[x, z] = even.astype(BF16)
            out_ref[x + 1, z] = odd.astype(BF16)


def sum_kernel(parts_ref, out_ref):
    total = parts_ref[0].astype(F32)
    for i in range(1, parts_ref.shape[0]):
        total = total + parts_ref[i].astype(F32)
    out_ref[...] = total.astype(BF16)


def swap(array, axis):
    return lax.all_to_all(array, axis, 0, 0, tiled=True)


def body(
    queries, keys, values, log_decay, norm_gain, expert_ids, gate_weights, w_gate, w_up, w_down
):
    shape = jax.ShapeDtypeStruct
    decay = jnp.transpose(log_decay, (0, 2, 1)).reshape(PAIRS, TOK)
    gain = norm_gain.reshape(1, COLS)
    running, message = call(
        update_kernel,
        (shape((PAIRS, TOK), F32), shape((X, AT_FACTS + 8, HD), BF16)),
        "update",
        [pltpu.VMEM((8, HD), F32)],
    )(decay, queries, keys, values, expert_ids.T, gate_weights.T)
    message = swap(message, "x")
    groups = call(group_kernel, shape((Z, PART + 40, HD), BF16), "group")(message)
    groups = swap(groups, "z")
    back, facts = call(
        scan_kernel,
        (shape((Z, 3 * PART, HD), BF16), shape((8, 4 * HD), F32)),
        "scan",
    )(groups)
    back = swap(back, "z")
    back = call(expand_kernel, shape((X, 3 * OWN * HD, HD), BF16), "expand")(back, message, gain)
    rows = swap(back, "x")
    attn_out = call(attention_kernel, shape((2, TOK, COLS), BF16), "attention")(
        queries, keys, values, running, rows, gain
    )
    slots = call(dispatch_kernel, shape((EXPERTS, 2 * HD, COLS), BF16), "dispatch")(rows, facts)
    slots = swap(slots, ("y", "core"))
    slots = call(expert_kernel, shape((EXPERTS, 2 * HD, COLS), BF16), "experts")(
        slots, w_gate[0], w_up[0], w_down[0]
    )
    slots = swap(slots, ("y", "core"))
    share = call(combine_kernel, shape((X, Z, MROWS, COLS), BF16), "combine")(slots, facts)
    share = swap(share.reshape(X, GROUP, COLS), "x")
    share = call(sum_kernel, shape((GROUP, COLS), BF16), "sum_x")(share)
    share = swap(share.reshape(Z, MROWS, COLS), "z")
    moe_out = call(sum_kernel, shape((MROWS, COLS), BF16), "sum_z")(share)
    return (attn_out, moe_out)


def solution(mesh):
    fine = Mesh(mesh.devices.reshape(Z, X, Y, CORE), ("z", "x", "y", "core"))
    seq, expert = ("z", "x"), ("y", "core")
    placed = (
        P(None, seq, expert),
        P(None, seq, expert),
        P(None, seq, expert),
        P(None, seq, expert),
        P(expert),
        P(seq, None),
        P(seq, None),
        P(expert, None, seq),
        P(expert, None, seq),
        P(expert, seq, None),
    )
    return jax.shard_map(
        body,
        mesh=fine,
        in_specs=placed,
        out_specs=(P(None, seq, expert), P(seq, expert)),
        check_vma=False,
    )
```

time: 200 us -> 181 us (0.905)
  blocking collectives: 174 us -> 148 us
  waiting for transfers between devices: 5.32 us -> 8.98 us
  local copies, waits for them, and re-layouts: 3.01 us -> 5.23 us
    all_to_all x8 -> x7, blocking collectives: 164 us -> 148 us  [swap(): return lax.all_to_all(array, axis, 0, 0, tiled=True)]
    all_gather x1 -> x0, blocking collectives: 10.4 us -> none  [body(): rows = lax.all_gather(rows, 'x', axis=0)]
    all_to_all x1, waiting for transfers between devices: 5.32 us -> 8.98 us  [swap(): return lax.all_to_all(array, axis, 0, 0, tiled=True)]
    unnamed x24, local copies, waits for them, and re-layouts: 2.29 us -> 4.51 us
  transfers between devices with their start and end apart: 1 -> 1, of which waited for: 1 -> 1; matrix products, arithmetic and copies ran while one was open for 0% -> 0% of each run, Pallas kernels for 0% -> 2%
where the time goes in v2:
time: 181 us; the launch traced here: 179 us
  blocking collectives  148 us (82%)
  Pallas kernels  10.6 us (6%)
  waiting for transfers between devices  8.98 us (5%)
  starting transfers between devices  5.27 us (3%)
  local copies, waits for them, and re-layouts  5.23 us (3%)
    all_to_all x7, blocking collectives, swap(): return lax.all_to_all(array, axis, 0, 0, tiled=True)  148 us
    all_to_all x1, waiting for transfers between devices, swap(): return lax.all_to_all(array, axis, 0, 0, tiled=True)  8.98 us
    all_to_all x1, starting transfers between devices, swap(): return lax.all_to_all(array, axis, 0, 0, tiled=True)  5.27 us
    unnamed x24, local copies, waits for them, and re-layouts  4.51 us
  transfers between devices with their start and end apart: 1, of which 1 were waited for; matrix products, arithmetic and copies ran while one was open for 0% of the time, Pallas kernels for 2%

profile of v2, /device:TPU:1, one launch (start us, length us, event | category | flops | bytes accessed | tf_op | source)
XLA Modules:
  0.0 178.6 jit_solution(7053683492097864228)
XLA Ops:
  0.6 0.0 copy-start.9
  0.6 0.7 reshape.16.decay_ref
  1.4 1.0 copy-done
  2.4 1.0 copy-done.2
  3.4 1.0 copy-done.4
  4.5 0.7 copy-done.10
  5.2 0.7 copy-done.11
  5.8 1.5 update.1
  7.4 10.4 %all_to_all.40.msg_ref = bf16[4,296,128]{2,1,0:T(8,128)(2,1)S(1)} all-to-all(bf16[4,296,128]{2,1,0:T(8,128)(2,1)S(1)} %get-tuple-element.7), channel_id=1, replica_groups=mesh['z'=16,'x'=4,'y'=4,'core'=2] {'x'}, dimensions={0} | all-to-all | bytes 606208 | tf_op jit(solution)/shard_map/all_to_all | solution.py:356
  17.8 0.3 group.1
  18.1 27.5 %all_to_all.41.msg_ref = bf16[16,56,128]{2,1,0:T(8,128)(2,1)S(1)} all-to-all(bf16[16,56,128]{2,1,0:T(8,128)(2,1)S(1)} %group.1), channel_id=1, replica_groups=mesh['z'=16,'x'=4,'y'=4,'core'=2] {'z'}, dimensions={0} | all-to-all | bytes 458752 | tf_op jit(solution)/shard_map/all_to_all | solution.py:356
  45.5 0.2 scan.1
  45.7 20.5 %all_to_all.42.back_ref = bf16[16,48,128]{2,1,0:T(8,128)(2,1)S(1)} all-to-all(bf16[16,48,128]{2,1,0:T(8,128)(2,1)S(1)} %get-tuple-element.8), channel_id=1, replica_groups=mesh['z'=16,'x'=4,'y'=4,'core'=2] {'z'}, dimensions={0} | all-to-all | bytes 393216 | tf_op jit(solution)/shard_map/all_to_all | solution.py:356
  66.3 0.0 copy-done.9
  66.3 0.3 expand.1
  66.6 10.7 %all_to_all.43.state_ref.rows_ref = bf16[4,768,128]{2,1,0:T(8,128)(2,1)S(1)} all-to-all(bf16[4,768,128]{2,1,0:T(8,128)(2,1)S(1)} %expand.1), channel_id=1, replica_groups=mesh['z'=16,'x'=4,'y'=4,'core'=2] {'x'}, dimensions={0} | all-to-all | bytes 1572864 | tf_op jit(solution)/shard_map/all_to_all | solution.py:356
  77.4 0.7 dispatch.1
  78.1 0.0 copy-start.6
  78.1 0.0 copy-start.7
  78.1 0.0 copy-start.8
  78.1 37.8 %all_to_all.44.rows_ref = bf16[8,256,512]{2,1,0:T(8,128)(2,1)S(1)} all-to-all(bf16[8,256,512]{2,1,0:T(8,128)(2,1)S(1)} %dispatch.1), channel_id=1, replica_groups=mesh['z'=16,'x'=4,'y'=4,'core'=2] {'y','core'}, dimensions={0} | all-to-all | bytes 4194304 | tf_op jit(solution)/shard_map/all_to_all | solution.py:356
  115.9 0.0 copy-done.6
  115.9 0.0 copy-done.8
  115.9 2.4 %experts.1 = bf16[8,256,512]{2,1,0:T(8,128)(2,1)S(1)} custom-call(bf16[8,256,512]{2,1,0:T(8,128)(2,1)S(1)} %all_to_all.44.rows_ref, bf16[4096,128]{1,0:T(8,128)(2,1)S(1)} %bitcast.10, bf16[4096,128]{1,0:T(8,128)(2,1)S(1)} %bitcast.11, bf16[128,4096]{1,0:T(8,128)(2,1)S(1)} %bitcast.12), custom_call_target="tpu_custom_call" | custom-call | tf_op jit(solution)/shard_map/experts/pallas_call | solution.py:387
  118.3 30.0 %all_to_all.45.rows_ref = bf16[8,256,512]{2,1,0:T(8,128)(2,1)S(1)} all-to-all(bf16[8,256,512]{2,1,0:T(8,128)(2,1)S(1)} %experts.1), channel_id=1, replica_groups=mesh['z'=16,'x'=4,'y'=4,'core'=2] {'y','core'}, dimensions={0} | all-to-all | bytes 4194304 | tf_op jit(solution)/shard_map/all_to_all | solution.py:356
  148.3 0.8 combine.1
  149.1 10.9 %all_to_all.46.parts_ref = bf16[4,128,512]{2,1,0:T(8,128)(2,1)S(1)} all-to-all(bf16[4,128,512]{2,1,0:T(8,128)(2,1)S(1)} %bitcast.9), channel_id=1, replica_groups=mesh['z'=16,'x'=4,'y'=4,'core'=2] {'x'}, dimensions={0} | all-to-all | bytes 1048576 | tf_op jit(solution)/shard_map/all_to_all | solution.py:356
  159.9 0.7 sum_x.1
  160.7 5.3 %all-to-all-start.7 = ((bf16[16,8,512]{2,1,0:T(8,128)(2,1)}), bf16[16,8,512]{2,1,0:T(8,128)(2,1)S(1)}, u32[]{:S(2)}, u32[]{:S(2)}) async-start(bf16[16,8,512]{2,1,0:T(8,128)(2,1)} %bitcast.8), calls=%async_computation.7 | async-start | bytes 262144 | tf_op jit(solution)/shard_map/all_to_all | solution.py:356
  166.0 3.0 %attention.1 = bf16[2,256,512]{2,1,0:T(8,128)(2,1)} custom-call(bf16[2,256,512]{2,1,0:T(8,128)(2,1)S(1)} %copy-done.1, bf16[2,256,512]{2,1,0:T(8,128)(2,1)S(1)} %copy-done.3, bf16[2,256,512]{2,1,0:T(8,128)(2,1)S(1)} %copy-done.5, f32[8,256]{1,0:T(8,128)S(1)} %get-tuple-element.6.run_ref, bf16[4,768,128]{2,1,0:T(8,128)(2,1)S(1)} %all_to_all.43.state_ref.rows_ref, ...), custom_call_target="tpu_custom_call" | custom-call | tf_op jit(solution)/shard_map/attention/pallas_call | solution.py:382
  168.9 9.0 %all-to-all-done.7.parts_ref = bf16[16,8,512]{2,1,0:T(8,128)(2,1)S(1)} async-done(((bf16[16,8,512]{2,1,0:T(8,128)(2,1)}), bf16[16,8,512]{2,1,0:T(8,128)(2,1)S(1)}, u32[]{:S(2)}, u32[]{:S(2)}) %all-to-all-start.7) | async-done | bytes 131104 | tf_op jit(solution)/shard_map/all_to_all | solution.py:356
  177.9 0.6 sum_z.1
  (12 shorter events, 0.0 us)
Async XLA Ops:
  0.6 65.7 %copy-start.9 = (f32[512]{0:T(512)S(1)}, f32[512]{0:T(512)}, u32[]{:S(2)}) copy-start(f32[512]{0:T(512)} %param.14) | copy-start | bytes 6148
  1.4 1.0 copy-start
  2.4 1.0 copy-start.2
  3.4 1.0 copy-start.4
  4.5 0.7 copy-start.10
  5.2 0.7 copy-start.11
  78.1 37.8 %copy-start.6 = (bf16[1,4096,128]{2,1,0:T(8,128)(2,1)S(1)}, bf16[1,4096,128]{2,1,0:T(8,128)(2,1)}, u32[]{:S(2)}) copy-start(bf16[1,4096,128]{2,1,0:T(8,128)(2,1)} %param.17) | copy-start | bytes 3145732
  78.1 37.8 %copy-start.7 = (bf16[1,4096,128]{2,1,0:T(8,128)(2,1)S(1)}, bf16[1,4096,128]{2,1,0:T(8,128)(2,1)}, u32[]{:S(2)}) copy-start(bf16[1,4096,128]{2,1,0:T(8,128)(2,1)} %param.18) | copy-start | bytes 3145732
  78.1 37.8 %copy-start.8 = (bf16[1,128,4096]{2,1,0:T(8,128)(2,1)S(1)}, bf16[1,128,4096]{2,1,0:T(8,128)(2,1)}, u32[]{:S(2)}) copy-start(bf16[1,128,4096]{2,1,0:T(8,128)(2,1)} %param.19) | copy-start | bytes 3145732
  148.3 17.7 %copy-start.1 = (bf16[2,256,512]{2,1,0:T(8,128)(2,1)S(1)}, bf16[2,256,512]{2,1,0:T(8,128)(2,1)}, u32[]{:S(2)}) copy-start(bf16[2,256,512]{2,1,0:T(8,128)(2,1)} %q_ref.3) | copy-start | bytes 1572868
  148.3 17.7 %copy-start.3 = (bf16[2,256,512]{2,1,0:T(8,128)(2,1)S(1)}, bf16[2,256,512]{2,1,0:T(8,128)(2,1)}, u32[]{:S(2)}) copy-start(bf16[2,256,512]{2,1,0:T(8,128)(2,1)} %k_ref.3) | copy-start | bytes 1572868
  148.3 17.7 %copy-start.5 = (bf16[2,256,512]{2,1,0:T(8,128)(2,1)S(1)}, bf16[2,256,512]{2,1,0:T(8,128)(2,1)}, u32[]{:S(2)}) copy-start(bf16[2,256,512]{2,1,0:T(8,128)(2,1)} %v_ref.3) | copy-start | bytes 1572868
  160.7 17.3 %all-to-all-start.7 = ((bf16[16,8,512]{2,1,0:T(8,128)(2,1)}), bf16[16,8,512]{2,1,0:T(8,128)(2,1)S(1)}, u32[]{:S(2)}, u32[]{:S(2)}) async-start(bf16[16,8,512]{2,1,0:T(8,128)(2,1)} %bitcast.8), calls=%async_computation.7 | async-start | bytes 262144 | tf_op jit(solution)/shard_map/all_to_all | solution.py:356

commit v3 on v2

--- a/solution.py
+++ b/solution.py
@@ -17,6 +17,7 @@
 COLS = HEADS * HD
 OWN = PAIRS // X
 PART = OWN * HD // Z
+SLOTS = Z * CAP
 HALF = MROWS // 2
 FEW = 16
 GROUP = Z * MROWS
@@ -24,19 +25,23 @@
 AT_Q = AT_LOGS + 8
 AT_LOCAL = AT_Q + 8
 AT_FACTS = AT_LOCAL + 16
+AT_ROUTE = 64
+AT_MINE = 96
 F32 = jnp.float32
 BF16 = jnp.bfloat16
 
 
-def call(kernel, out, name, scratch=()):
+def call(kernel, out, name, scratch=(), fetch=False):
     vmem = pl.BlockSpec(memory_space=pltpu.VMEM)
+    specs = {"in_specs": [pl.BlockSpec(memory_space=pl.ANY)] * 6} if fetch else {}
     return pl.pallas_call(
         kernel,
         out_shape=out,
         out_specs=jax.tree.map(lambda _: vmem, out),
         scratch_shapes=scratch,
-        compiler_params=pltpu.CompilerParams(vmem_limit_bytes=40 * 2**20),
+        compiler_params=pltpu.CompilerParams(vmem_limit_bytes=(60 if fetch else 40) * 2**20),
         name=name,
+        **specs,
     )
 
 
@@ -107,10 +112,19 @@
     facts_ref[0:2, :] = jnp.zeros((2, HD), F32)
 
 
-def update_kernel(
-    decay_ref, q_ref, k_ref, v_ref, ids_ref, gates_ref, run_ref, msg_ref, facts_ref
-):
-    running = prefix_sums(decay_ref[...])
+def update_kernel(*refs):
+    sources, (run_ref, msg_ref), fetched = refs[:6], refs[6:8], refs[8:14]
+    facts_ref, semaphores = refs[14:]
+    copies = []
+    for i, (source, target) in enumerate(zip(sources, fetched)):
+        part = source.at[:, pl.ds(0, FEW)] if i == 1 else source
+        copies.append(pltpu.make_async_copy(part, target, semaphores.at[i]))
+    for copy in copies:
+        copy.start()
+    for copy in copies:
+        copy.wait()
+    decay_ref, q_ref, k_ref, v_ref, ids_ref, gates_ref = fetched
+    running = prefix_sums(jnp.concatenate([decay_ref[0], decay_ref[1]], axis=0))
     run_ref[...] = running
     end = running[:, TOK - 1 :]
     to_end = jnp.exp(end - running).T
@@ -161,7 +175,9 @@
         for b in range(2):
             only = jnp.where(lane // HALF == b, own, 0.0)
             shift = b * 16 + x * HALF - b * HALF
-            facts = facts + (pltpu.roll(only, shift, 1) if shift else only)
+            facts = facts + pltpu.roll(only, AT_ROUTE + shift, 1)
+        mine = jnp.where((lane < MROWS) & (lax.axis_index("x") == x), own, 0.0)
+        facts = facts + pltpu.roll(mine, AT_MINE, 1)
     for i in range(OWN):
         total, log, queries, near, inner = None, None, 0.0, 0.0, 0.0
         for x in range(X):
@@ -185,11 +201,12 @@
                 total, log = jnp.exp(own_log) * total + update, log + own_log
         coarse, rest = two_parts(inner + tall(near).T)
         rows = coarse + pltpu.roll(rest, 16, 1)
-        info = stacked_rows(split_log(log)) + facts
+        info = jnp.where(lane < AT_ROUTE, 0.0, stacked_rows(split_log(log)) + facts)
         for g in range(HD // PART):
-            piece = slice(g * PART, (g + 1) * PART)
+            at = g * PART
+            near = rows[at : at + 8] + pltpu.roll(rows[at + 8 : at + PART], 32, 1)
             out_ref[i * (HD // PART) + g] = jnp.concatenate(
-                [total[piece], info, queries, rows[piece]], axis=0
+                [total[at : at + PART], info + near, queries], axis=0
             ).astype(BF16)
 
 
@@ -198,21 +215,26 @@
     lane = lax.broadcasted_iota(jnp.int32, (16, HD), 1)
     states, queries = [], []
     near = [jnp.zeros((PART, HD), F32) for _ in range(2)]
-    facts = [jnp.zeros((8, HD), F32) for _ in range(4)]
+    facts = [jnp.zeros((8, HD), F32) for _ in range(5)]
     for z in range(Z):
         states.append(state)
         part = msg_ref[z].astype(F32)
-        info, query, rows = part[16:24], part[24:40], part[40:56]
-        queries.append(query)
+        info = part[16:24]
+        queries.append(part[24:40])
         half, shift = z // 8, z % 8 * 16
+        rows = jnp.concatenate([info, pltpu.roll(info, HD - 32, 1)], axis=0)
         rows = jnp.where(lane < 16, rows + pltpu.roll(rows, HD - 16, 1), 0.0)
         near[half] = near[half] + (pltpu.roll(rows, shift, 1) if shift else rows)
         for b in range(2):
-            only = jnp.where(lane[:8] // 16 == b, info, 0.0)
-            move = (shift - b * 16) % HD
+            only = jnp.where(lane[:8] // 16 == AT_ROUTE // 16 + b, info, 0.0)
+            move = (shift - AT_ROUTE - b * 16) % HD
             place = half * 2 + b
             facts[place] = facts[place] + (pltpu.roll(only, move, 1) if move else only)
-        state = jnp.exp(joined_log(part, PART)) * state + part[:PART]
+        only = jnp.where(lane[:8] // MROWS == AT_MINE // MROWS, info, 0.0)
+        move = (z * MROWS - AT_MINE) % HD
+        facts[4] = facts[4] + (pltpu.roll(only, move, 1) if move else only)
+        factor = jnp.exp(joined_log(part, PART))[:, AT_ROUTE : AT_ROUTE + 1]
+        state = factor * state + part[:PART]
     far = lax.dot_general(
         jnp.concatenate(states, axis=0).astype(BF16),
         jnp.concatenate(queries, axis=0).astype(BF16),
@@ -273,21 +295,22 @@
         out_ref[b, :, cols] = (o * scale * gain_ref[:, cols]).astype(BF16)
 
 
-def slot_rows(facts_ref, half):
-    facts = facts_ref[:, half * 2 * HD : (half + 1) * 2 * HD]
-    lane = lax.broadcasted_iota(jnp.int32, (1, 2 * HD), 1)
-    place = lane % HD // CAP * CAP
+def slot_rows(facts, place, slots):
     rows = []
     for j in range(2):
         code = facts[4 + j : 5 + j].astype(jnp.int32)
-        rows.append(code // CAP * HD + code % CAP + place)
+        rows.append(code // CAP * slots + code % CAP + place)
     return rows, [facts[6:7], facts[7:8]]
 
 
 def dispatch_kernel(rows_ref, facts_ref, out_ref):
     index = lax.broadcasted_iota(jnp.int32, (EXPERTS * HD, 2 * HD), 0)
+    lane = lax.broadcasted_iota(jnp.int32, (1, 2 * HD), 1)
+    place = lane // HALF % X * 32 + lane % HD // 16 * CAP
     for half in range(2):
-        (first, second), _ = slot_rows(facts_ref, half)
+        (first, second), _ = slot_rows(
+            facts_ref[:, half * 2 * HD : (half + 1) * 2 * HD], place, HD
+        )
         chosen = jnp.where((index == first) | (index == second), 1.0, 0.0).astype(BF16)
         tokens = pl.ds(half * HD, HD)
         rows = jnp.concatenate(
@@ -305,7 +328,9 @@
         )
         sent = jnp.dot(chosen, rows, preferred_element_type=F32).astype(BF16)
         for e in range(EXPERTS):
-            out_ref[e, tokens] = sent[e * HD : (e + 1) * HD]
+            for x in range(X):
+                at = e * HD + x * 32
+                out_ref[e, pl.ds(x * SLOTS + half * 32, 32)] = sent[at : at + 32]
 
 
 def expert_kernel(rows_ref, gate_ref, up_ref, down_ref, out_ref):
@@ -319,30 +344,28 @@
     gate, up = total[:, :width], total[:, width:]
     hidden = (gate / (1.0 + jnp.exp(-gate)) * up).astype(BF16)
     for j in range(EXPERTS):
-        out_ref[j] = jnp.dot(
-            hidden, down_ref[:, pl.ds(j * COLS, COLS)], preferred_element_type=F32
-        ).astype(BF16)
-
-
-def combine_kernel(rows_ref, facts_ref, out_ref):
-    index = lax.broadcasted_iota(jnp.int32, (EXPERTS * HD, 2 * HD), 0)
-    for half in range(2):
-        (first, second), gates = slot_rows(facts_ref, half)
-        mix = jnp.where(index == first, gates[0], 0.0) + jnp.where(index == second, gates[1], 0.0)
-        own = jnp.concatenate(
-            [rows_ref[e, half * HD : (half + 1) * HD] for e in range(EXPERTS)], axis=0
-        )
-        total = lax.dot_general(
-            mix.astype(BF16), own, (((0,), (0,)), ((), ())), preferred_element_type=F32
-        )
-        for k in range(16):
-            one, two = total[k * 8 : (k + 1) * 8], total[HD + k * 8 : HD + (k + 1) * 8]
-            row = lax.broadcasted_iota(jnp.int32, one.shape, 0)
-            even = jnp.where(row < HALF, one, pltpu.roll(two, HALF, 0))
-            odd = jnp.where(row < HALF, pltpu.roll(one, HALF, 0), two)
-            z, x = half * 8 + k // 2, k % 2 * 2
-            out_ref[x, z] = even.astype(BF16)
-            out_ref[x + 1, z] = odd.astype(BF16)
+        out = jnp.dot(hidden, down_ref[:, pl.ds(j * COLS, COLS)], preferred_element_type=F32)
+        for x in range(X):
+            out_ref[x * EXPERTS + j] = out[x * SLOTS : (x + 1) * SLOTS].astype(BF16)
+
+
+def combine_kernel(parts_ref, facts_ref, out_ref):
+    index = lax.broadcasted_iota(jnp.int32, (EXPERTS * SLOTS, GROUP), 0)
+    place = lax.broadcasted_iota(jnp.int32, (1, GROUP), 1) // MROWS * CAP
+    (first, second), gates = slot_rows(facts_ref[:, 4 * HD :], place, SLOTS)
+    mix = jnp.where(index == first, gates[0], 0.0) + jnp.where(index == second, gates[1], 0.0)
+    rows = []
+    for e in range(EXPERTS):
+        total = parts_ref[e].astype(F32)
+        for x in range(1, X):
+            total = total + parts_ref[x * EXPERTS + e].astype(F32)
+        rows.append(total.astype(BF16))
+    out_ref[...] = lax.dot_general(
+        mix.astype(BF16),
+        jnp.concatenate(rows, axis=0),
+        (((0,), (0,)), ((), ())),
+        preferred_element_type=F32,
+    ).astype(BF16)
 
 
 def sum_kernel(parts_ref, out_ref):
@@ -360,20 +383,30 @@
     queries, keys, values, log_decay, norm_gain, expert_ids, gate_weights, w_gate, w_up, w_down
 ):
     shape = jax.ShapeDtypeStruct
-    decay = jnp.transpose(log_decay, (0, 2, 1)).reshape(PAIRS, TOK)
+    decay = jnp.transpose(log_decay, (0, 2, 1))
     gain = norm_gain.reshape(1, COLS)
     running, message = call(
         update_kernel,
         (shape((PAIRS, TOK), F32), shape((X, AT_FACTS + 8, HD), BF16)),
         "update",
-        [pltpu.VMEM((8, HD), F32)],
+        [
+            pltpu.VMEM((2, HEADS, TOK), F32),
+            pltpu.VMEM((2, FEW, COLS), BF16),
+            pltpu.VMEM((2, TOK, COLS), BF16),
+            pltpu.VMEM((2, TOK, COLS), BF16),
+            pltpu.VMEM((2, MROWS), jnp.int32),
+            pltpu.VMEM((2, MROWS), F32),
+            pltpu.VMEM((8, HD), F32),
+            pltpu.SemaphoreType.DMA((6,)),
+        ],
+        True,
     )(decay, queries, keys, values, expert_ids.T, gate_weights.T)
     message = swap(message, "x")
-    groups = call(group_kernel, shape((Z, PART + 40, HD), BF16), "group")(message)
+    groups = call(group_kernel, shape((Z, PART + 24, HD), BF16), "group")(message)
     groups = swap(groups, "z")
     back, facts = call(
         scan_kernel,
-        (shape((Z, 3 * PART, HD), BF16), shape((8, 4 * HD), F32)),
+        (shape((Z, 3 * PART, HD), BF16), shape((8, 5 * HD), F32)),
         "scan",
     )(groups)
     back = swap(back, "z")
@@ -384,13 +417,11 @@
     )
     slots = call(dispatch_kernel, shape((EXPERTS, 2 * HD, COLS), BF16), "dispatch")(rows, facts)
     slots = swap(slots, ("y", "core"))
-    slots = call(expert_kernel, shape((EXPERTS, 2 * HD, COLS), BF16), "experts")(
+    parts = call(expert_kernel, shape((X * EXPERTS, SLOTS, COLS), BF16), "experts")(
         slots, w_gate[0], w_up[0], w_down[0]
     )
-    slots = swap(slots, ("y", "core"))
-    share = call(combine_kernel, shape((X, Z, MROWS, COLS), BF16), "combine")(slots, facts)
-    share = swap(share.reshape(X, GROUP, COLS), "x")
-    share = call(sum_kernel, shape((GROUP, COLS), BF16), "sum_x")(share)
+    parts = swap(parts, ("x", "y", "core"))
+    share = call(combine_kernel, shape((GROUP, COLS), BF16), "combine")(parts, facts)
     share = swap(share.reshape(Z, MROWS, COLS), "z")
     moe_out = call(sum_kernel, shape((MROWS, COLS), BF16), "sum_z")(share)
     return (attn_out, moe_out)

time: 181 us -> 165 us (0.912)
  blocking collectives: 148 us -> 137 us
  local copies, waits for them, and re-layouts: 5.23 us -> 0.04 us
    all_to_all x7 -> x6, blocking collectives: 148 us -> 137 us  [swap(): return lax.all_to_all(array, axis, 0, 0, tiled=True)]
    unnamed x24 -> x16, local copies, waits for them, and re-layouts: 4.51 us -> 0.04 us
    pallas_call x1, Pallas kernels: 1.53 us -> 3.56 us  [body(): call(update_kernel, (shape((PAIRS, TOK), F32), shape((X, AT_FACTS + 8, HD...]
    pallas_call x5 -> x4, Pallas kernels: 4.41 us -> 4.17 us  [the longest x1 2.38 us: body(): call(expert_kernel, shape((X * EXPERTS, SLOTS, COLS), BF16), 'experts')]
where the time goes in v3:
time: 165 us; the launch traced here: 164 us
  blocking collectives  137 us (83%)
  Pallas kernels  12.3 us (7%)
  waiting for transfers between devices  9.13 us (6%)
  starting transfers between devices  4.95 us (3%)
    all_to_all x6, blocking collectives, swap(): return lax.all_to_all(array, axis, 0, 0, tiled=True)  137 us
    all_to_all x1, waiting for transfers between devices, swap(): return lax.all_to_all(array, axis, 0, 0, tiled=True)  9.13 us
    all_to_all x1, starting transfers between devices, swap(): return lax.all_to_all(array, axis, 0, 0, tiled=True)  4.95 us
    pallas_call x1, Pallas kernels, body(): call(update_kernel, (shape((PAIRS, TOK), F32), shape((X, AT_FACTS + 8, HD...  3.56 us
  transfers between devices with their start and end apart: 1, of which 1 were waited for; matrix products, arithmetic and copies ran while one was open for 0% of the time, Pallas kernels for 2%

profile of v3, /device:TPU:1, one launch (start us, length us, event | category | flops | bytes accessed | tf_op | source)
XLA Modules:
  0.0 163.7 jit_solution(4451449796658387043)
XLA Ops:
  0.6 0.0 copy-start.7
  0.6 3.6 %update.1 = (f32[8,256]{1,0:T(8,128)}, bf16[4,296,128]{2,1,0:T(8,128)(2,1)}) custom-call(f32[2,4,256]{2,1,0:T(4,128)} %bitcast.13, bf16[2,256,512]{2,1,0:T(8,128)(2,1)} %q_ref.1, bf16[2,256,512]{2,1,0:T(8,128)(2,1)} %k_ref.1, bf16[2,256,512]{2,1,0:T(8,128)(2,1)} %v_ref.1, s32[2,8]{1,0:T(2,128)} %bitcast.14, f32[2,8]{1,0:T(2,128)} %bitcast.15), custom_call_target="tpu_custom_call" | custom-call | tf_op jit(solution)/shard_map/update/pallas_call | solution.py:388
  4.2 10.6 %all_to_all.35.msg_ref = bf16[4,296,128]{2,1,0:T(8,128)(2,1)S(1)} all-to-all(bf16[4,296,128]{2,1,0:T(8,128)(2,1)} %get-tuple-element.7), channel_id=1, replica_groups=mesh['z'=16,'x'=4,'y'=4,'core'=2] {'x'}, dimensions={0} | all-to-all | bytes 606208 | tf_op jit(solution)/shard_map/all_to_all | solution.py:379
  14.8 0.3 group.1
  15.2 27.1 %all_to_all.36.msg_ref = bf16[16,40,128]{2,1,0:T(8,128)(2,1)S(1)} all-to-all(bf16[16,40,128]{2,1,0:T(8,128)(2,1)S(1)} %group.1), channel_id=1, replica_groups=mesh['z'=16,'x'=4,'y'=4,'core'=2] {'z'}, dimensions={0} | all-to-all | bytes 327680 | tf_op jit(solution)/shard_map/all_to_all | solution.py:379
  42.2 0.3 scan.1
  42.5 18.2 %all_to_all.37.back_ref = bf16[16,48,128]{2,1,0:T(8,128)(2,1)S(1)} all-to-all(bf16[16,48,128]{2,1,0:T(8,128)(2,1)S(1)} %get-tuple-element.8), channel_id=1, replica_groups=mesh['z'=16,'x'=4,'y'=4,'core'=2] {'z'}, dimensions={0} | all-to-all | bytes 393216 | tf_op jit(solution)/shard_map/all_to_all | solution.py:379
  60.8 0.0 copy-done.7
  60.8 0.3 expand.1
  61.1 10.7 %all_to_all.38.state_ref.rows_ref = bf16[4,768,128]{2,1,0:T(8,128)(2,1)S(1)} all-to-all(bf16[4,768,128]{2,1,0:T(8,128)(2,1)S(1)} %expand.1), channel_id=1, replica_groups=mesh['z'=16,'x'=4,'y'=4,'core'=2] {'x'}, dimensions={0} | all-to-all | bytes 1572864 | tf_op jit(solution)/shard_map/all_to_all | solution.py:379
  71.8 0.7 dispatch.1
  72.6 0.0 copy-start.3
  72.6 0.0 copy-start.4
  72.6 0.0 copy-start.5
  72.6 37.7 %all_to_all.39.rows_ref = bf16[8,256,512]{2,1,0:T(8,128)(2,1)S(1)} all-to-all(bf16[8,256,512]{2,1,0:T(8,128)(2,1)S(1)} %dispatch.1), channel_id=1, replica_groups=mesh['z'=16,'x'=4,'y'=4,'core'=2] {'y','core'}, dimensions={0} | all-to-all | bytes 4194304 | tf_op jit(solution)/shard_map/all_to_all | solution.py:379
  110.3 0.0 copy-done.3
  110.3 0.0 copy-done.4
  110.3 0.0 copy-done.5
  110.3 2.4 %experts.1 = bf16[32,64,512]{2,1,0:T(8,128)(2,1)S(1)} custom-call(bf16[8,256,512]{2,1,0:T(8,128)(2,1)S(1)} %all_to_all.39.rows_ref, bf16[4096,128]{1,0:T(8,128)(2,1)S(1)} %bitcast.8, bf16[4096,128]{1,0:T(8,128)(2,1)S(1)} %bitcast.9, bf16[128,4096]{1,0:T(8,128)(2,1)S(1)} %bitcast.10), custom_call_target="tpu_custom_call" | custom-call | tf_op jit(solution)/shard_map/experts/pallas_call | solution.py:420
  112.7 32.1 %all_to_all.40.parts_ref = bf16[32,64,512]{2,1,0:T(8,128)(2,1)S(1)} all-to-all(bf16[32,64,512]{2,1,0:T(8,128)(2,1)S(1)} %experts.1), channel_id=1, replica_groups=mesh['z'=16,'x'=4,'y'=4,'core'=2] {'x','y','core'}, dimensions={0} | all-to-all | bytes 4194304 | tf_op jit(solution)/shard_map/all_to_all | solution.py:379
  144.9 0.0 copy-start
  144.9 0.0 copy-start.1
  144.9 0.0 copy-start.2
  144.9 1.1 combine.1
  146.0 4.9 %all-to-all-start.6 = ((bf16[16,8,512]{2,1,0:T(8,128)(2,1)}), bf16[16,8,512]{2,1,0:T(8,128)(2,1)S(1)}, u32[]{:S(2)}, u32[]{:S(2)}) async-start(bf16[16,8,512]{2,1,0:T(8,128)(2,1)} %bitcast.7), calls=%async_computation.6 | async-start | bytes 262144 | tf_op jit(solution)/shard_map/all_to_all | solution.py:379
  151.0 0.0 copy-done
  151.0 0.0 copy-done.1
  151.0 0.0 copy-done.2
  151.0 0.0 copy-done.6
  151.0 3.0 %attention.1 = bf16[2,256,512]{2,1,0:T(8,128)(2,1)} custom-call(bf16[2,256,512]{2,1,0:T(8,128)(2,1)S(1)} %copy-done, bf16[2,256,512]{2,1,0:T(8,128)(2,1)S(1)} %copy-done.1, bf16[2,256,512]{2,1,0:T(8,128)(2,1)S(1)} %copy-done.2, f32[8,256]{1,0:T(8,128)S(1)} %copy-done.6, bf16[4,768,128]{2,1,0:T(8,128)(2,1)S(1)} %all_to_all.38.state_ref.rows_ref, ...), custom_call_target="tpu_custom_call" | custom-call | tf_op jit(solution)/shard_map/attention/pallas_call | solution.py:415
  154.0 9.1 %all-to-all-done.6.parts_ref = bf16[16,8,512]{2,1,0:T(8,128)(2,1)S(1)} async-done(((bf16[16,8,512]{2,1,0:T(8,128)(2,1)}), bf16[16,8,512]{2,1,0:T(8,128)(2,1)S(1)}, u32[]{:S(2)}, u32[]{:S(2)}) %all-to-all-start.6) | async-done | bytes 131104 | tf_op jit(solution)/shard_map/all_to_all | solution.py:379
  163.1 0.6 sum_z.1
  (1 shorter events, 0.0 us)
Async XLA Ops:
  0.6 60.2 %copy-start.7 = (f32[512]{0:T(512)S(1)}, f32[512]{0:T(512)}, u32[]{:S(2)}) copy-start(f32[512]{0:T(512)} %param.14) | copy-start | bytes 6148
  72.6 37.8 %copy-start.3 = (bf16[1,4096,128]{2,1,0:T(8,128)(2,1)S(1)}, bf16[1,4096,128]{2,1,0:T(8,128)(2,1)}, u32[]{:S(2)}) copy-start(bf16[1,4096,128]{2,1,0:T(8,128)(2,1)} %param.17) | copy-start | bytes 3145732
  72.6 37.8 %copy-start.4 = (bf16[1,4096,128]{2,1,0:T(8,128)(2,1)S(1)}, bf16[1,4096,128]{2,1,0:T(8,128)(2,1)}, u32[]{:S(2)}) copy-start(bf16[1,4096,128]{2,1,0:T(8,128)(2,1)} %param.18) | copy-start | bytes 3145732
  72.6 37.7 %copy-start.5 = (bf16[1,128,4096]{2,1,0:T(8,128)(2,1)S(1)}, bf16[1,128,4096]{2,1,0:T(8,128)(2,1)}, u32[]{:S(2)}) copy-start(bf16[1,128,4096]{2,1,0:T(8,128)(2,1)} %param.19) | copy-start | bytes 3145732
  144.9 6.1 %copy-start = (bf16[2,256,512]{2,1,0:T(8,128)(2,1)S(1)}, bf16[2,256,512]{2,1,0:T(8,128)(2,1)}, u32[]{:S(2)}) copy-start(bf16[2,256,512]{2,1,0:T(8,128)(2,1)} %q_ref.1) | copy-start | bytes 1572868
  144.9 6.1 %copy-start.1 = (bf16[2,256,512]{2,1,0:T(8,128)(2,1)S(1)}, bf16[2,256,512]{2,1,0:T(8,128)(2,1)}, u32[]{:S(2)}) copy-start(bf16[2,256,512]{2,1,0:T(8,128)(2,1)} %k_ref.1) | copy-start | bytes 1572868
  144.9 6.1 %copy-start.2 = (bf16[2,256,512]{2,1,0:T(8,128)(2,1)S(1)}, bf16[2,256,512]{2,1,0:T(8,128)(2,1)}, u32[]{:S(2)}) copy-start(bf16[2,256,512]{2,1,0:T(8,128)(2,1)} %v_ref.1) | copy-start | bytes 1572868
  144.9 6.1 %copy-start.6 = (f32[8,256]{1,0:T(8,128)S(1)}, f32[8,256]{1,0:T(8,128)}, u32[]{:S(2)}) copy-start(f32[8,256]{1,0:T(8,128)} %get-tuple-element.6.run_ref) | copy-start | bytes 24580
  146.0 17.1 %all-to-all-start.6 = ((bf16[16,8,512]{2,1,0:T(8,128)(2,1)}), bf16[16,8,512]{2,1,0:T(8,128)(2,1)S(1)}, u32[]{:S(2)}, u32[]{:S(2)}) async-start(bf16[16,8,512]{2,1,0:T(8,128)(2,1)} %bitcast.7), calls=%async_computation.6 | async-start | bytes 262144 | tf_op jit(solution)/shard_map/all_to_all | solution.py:379

commit v4 on v3

--- a/solution.py
+++ b/solution.py
@@ -133,8 +133,7 @@
     for owner in range(X):
         parts, logs, qs, locals_ = [], [], [], []
         for i in range(OWN):
-            pair = owner * OWN + i
-            b, cols = pair // HEADS, pl.ds(pair % HEADS * HD, HD)
+            b, pair, cols = i, i * HEADS + owner, pl.ds(owner * HD, HD)
             decayed = (k_ref[b, :, cols].astype(F32) * to_end[:, pair : pair + 1]).astype(BF16)
             parts.append(
                 lax.dot_general(
@@ -254,9 +253,10 @@
     facts_ref[...] = jnp.concatenate(facts, axis=1)
 
 
-def expand_kernel(back_ref, msg_ref, gain_ref, out_ref):
-    odd = lax.rem(lax.axis_index("x"), 2)
-    gain = jnp.where(odd == 1, gain_ref[:, OWN * HD :], gain_ref[:, : OWN * HD])
+def expand_kernel(back_ref, msg_ref, gain_ref, facts_ref, state_ref, slots_ref):
+    gain = gain_ref[:, :HD]
+    for x in range(1, X):
+        gain = jnp.where(lax.axis_index("x") == x, gain_ref[:, x * HD : (x + 1) * HD], gain)
     back = [back_ref[c].astype(F32) for c in range(Z)]
     each = Z // OWN
     state, rows = [], []
@@ -267,9 +267,26 @@
             first = PART * (1 + half)
             o = jnp.concatenate([part[first : first + PART] for part in mine], axis=0).T
             scale = lax.rsqrt(jnp.mean(o * o, axis=1, keepdims=True) + 1e-6)
-            rows.append((o * scale * gain[:, i * HD : (i + 1) * HD]).astype(BF16))
+            rows.append((o * scale * gain).astype(BF16))
+    index = lax.broadcasted_iota(jnp.int32, (EXPERTS * HD, 2 * HD), 0)
+    lane = lax.broadcasted_iota(jnp.int32, (1, 2 * HD), 1)
+    place = lane // HALF % X * 32 + lane % HD // 16 * CAP
+    for half in range(2):
+        (first, second), _ = slot_rows(
+            facts_ref[:, half * 2 * HD : (half + 1) * 2 * HD], place, HD
+        )
+        chosen = jnp.where((index == first) | (index == second), 1.0, 0.0).astype(BF16)
+        both = jnp.concatenate([rows[half], rows[2 + half]], axis=0)
+        sent = jnp.dot(chosen, both, preferred_element_type=F32).astype(BF16)
+        for e in range(EXPERTS):
+            for x in range(X):
+                at = e * HD + x * 32
+                for target in range(X):
+                    slots_ref[target * EXPERTS + e, pl.ds(x * SLOTS + half * 32, 32)] = sent[
+                        at : at + 32
+                    ]
     for x in range(X):
-        out_ref[x] = jnp.concatenate([part.astype(BF16) for part in state] + rows, axis=0)
+        state_ref[x] = jnp.concatenate(state, axis=0).astype(BF16)
         if x < X - 1:
             part = msg_ref[x].astype(F32)
             for i in range(OWN):
@@ -278,12 +295,13 @@
 
 
 def attention_kernel(q_ref, k_ref, v_ref, run_ref, state_ref, gain_ref, out_ref):
+    here = lax.axis_index("x")
     running = run_ref[...]
     columns = running.T
     for pair in range(PAIRS):
         b, cols = pair // HEADS, pl.ds(pair % HEADS * HD, HD)
         q, column = q_ref[b, :, cols], columns[:, pair : pair + 1]
-        state = state_ref[pair // OWN, pair % OWN * HD : (pair % OWN + 1) * HD]
+        state = state_ref[pair % HEADS, here, b * HD : (b + 1) * HD]
         weights = fading_scores(q, k_ref[b, :, cols], column, running[pair : pair + 1])
         decayed = (q.astype(F32) * jnp.exp(column)).astype(BF16)
         o = jnp.dot(
@@ -303,42 +321,13 @@
     return rows, [facts[6:7], facts[7:8]]
 
 
-def dispatch_kernel(rows_ref, facts_ref, out_ref):
-    index = lax.broadcasted_iota(jnp.int32, (EXPERTS * HD, 2 * HD), 0)
-    lane = lax.broadcasted_iota(jnp.int32, (1, 2 * HD), 1)
-    place = lane // HALF % X * 32 + lane % HD // 16 * CAP
-    for half in range(2):
-        (first, second), _ = slot_rows(
-            facts_ref[:, half * 2 * HD : (half + 1) * 2 * HD], place, HD
-        )
-        chosen = jnp.where((index == first) | (index == second), 1.0, 0.0).astype(BF16)
-        tokens = pl.ds(half * HD, HD)
-        rows = jnp.concatenate(
-            [
-                jnp.concatenate(
-                    [
-                        rows_ref[2 * b + h // OWN, pl.ds((OWN + h % OWN * 2 + half) * HD, HD)]
-                        for h in range(HEADS)
-                    ],
-                    axis=1,
-                )
-                for b in range(2)
-            ],
-            axis=0,
-        )
-        sent = jnp.dot(chosen, rows, preferred_element_type=F32).astype(BF16)
-        for e in range(EXPERTS):
-            for x in range(X):
-                at = e * HD + x * 32
-                out_ref[e, pl.ds(x * SLOTS + half * 32, 32)] = sent[at : at + 32]
-
-
 def expert_kernel(rows_ref, gate_ref, up_ref, down_ref, out_ref):
     total = None
     for j in range(EXPERTS):
         part = pl.ds(j * COLS, COLS)
         both = jnp.concatenate([gate_ref[part, :], up_ref[part, :]], axis=1)
-        term = jnp.dot(rows_ref[j], both, preferred_element_type=F32)
+        rows = jnp.concatenate([rows_ref[x * EXPERTS + j] for x in range(X)], axis=1)
+        term = jnp.dot(rows, both, preferred_element_type=F32)
         total = term if total is None else total + term
     width = gate_ref.shape[1]
     gate, up = total[:, :width], total[:, width:]
@@ -410,13 +399,16 @@
         "scan",
     )(groups)
     back = swap(back, "z")
-    back = call(expand_kernel, shape((X, 3 * OWN * HD, HD), BF16), "expand")(back, message, gain)
-    rows = swap(back, "x")
+    states, slots = call(
+        expand_kernel,
+        (shape((X, OWN * HD, HD), BF16), shape((X * EXPERTS, X * SLOTS, HD), BF16)),
+        "expand",
+    )(back, message, gain, facts)
+    slots = swap(slots, ("x", "y", "core"))
+    states = lax.all_gather(states, "x", axis=0)
     attn_out = call(attention_kernel, shape((2, TOK, COLS), BF16), "attention")(
-        queries, keys, values, running, rows, gain
-    )
-    slots = call(dispatch_kernel, shape((EXPERTS, 2 * HD, COLS), BF16), "dispatch")(rows, facts)
-    slots = swap(slots, ("y", "core"))
+        queries, keys, values, running, states, gain
+    )
     parts = call(expert_kernel, shape((X * EXPERTS, SLOTS, COLS), BF16), "experts")(
         slots, w_gate[0], w_up[0], w_down[0]
     )

time: 165 us -> 176 us (1.067)
  blocking collectives: 137 us -> 95 us
  waiting for transfers between devices: 9.13 us -> 40.4 us
  between operations: 0.76 us -> 14.1 us
  starting transfers between devices: 4.95 us -> 7.51 us
  local copies, waits for them, and re-layouts: 0.04 us -> 2.3 us
  Pallas kernels: 12.3 us -> 14.2 us
    all_to_all x6 -> x4, blocking collectives: 137 us -> 95 us  [swap(): return lax.all_to_all(array, axis, 0, 0, tiled=True)]
    all_to_all x1 -> x2, waiting for transfers between devices: 9.13 us -> 39.7 us  [swap(): return lax.all_to_all(array, axis, 0, 0, tiled=True)]
    all_to_all x1 -> x2, starting transfers between devices: 4.95 us -> 7.47 us  [swap(): return lax.all_to_all(array, axis, 0, 0, tiled=True)]
    unnamed x16 -> x18, local copies, waits for them, and re-layouts: 0.04 us -> 2.3 us
  transfers between devices with their start and end apart: 1 -> 3, of which waited for: 1 -> 2; matrix products, arithmetic and copies ran while one was open for 0% -> 0% of each run, Pallas kernels for 2% -> 2%
where the time goes in v4:
time: 176 us; the launch traced here: 174 us
  blocking collectives  95 us (54%)
  waiting for transfers between devices  40.4 us (23%)
  Pallas kernels  14.2 us (8%)
  between operations  14.1 us (8%)
  starting transfers between devices  7.51 us (4%)
  local copies, waits for them, and re-layouts  2.3 us (1%)
    all_to_all x4, blocking collectives, swap(): return lax.all_to_all(array, axis, 0, 0, tiled=True)  95 us
    all_to_all x2, waiting for transfers between devices, swap(): return lax.all_to_all(array, axis, 0, 0, tiled=True)  39.7 us
    all_to_all x2, starting transfers between devices, swap(): return lax.all_to_all(array, axis, 0, 0, tiled=True)  7.47 us
    pallas_call x1, Pallas kernels, body(): call(expert_kernel, shape((X * EXPERTS, SLOTS, COLS), BF16), 'experts')  3.73 us
    pallas_call x1, Pallas kernels, body(): call(update_kernel, (shape((PAIRS, TOK), F32), shape((X, AT_FACTS + 8, HD...  3.56 us
  transfers between devices with their start and end apart: 3, of which 2 were waited for; matrix products, arithmetic and copies ran while one was open for 0% of the time, Pallas kernels for 2%

profile of v4, /device:TPU:1, one launch (start us, length us, event | category | flops | bytes accessed | tf_op | source)
XLA Modules:
  0.0 173.5 jit_solution(6880464731600267210)
XLA Ops:
  7.2 0.0 copy-start.8
  7.2 3.6 %update.1 = (f32[8,256]{1,0:T(8,128)}, bf16[4,296,128]{2,1,0:T(8,128)(2,1)}) custom-call(f32[2,4,256]{2,1,0:T(4,128)} %bitcast.15, bf16[2,256,512]{2,1,0:T(8,128)(2,1)} %q_ref.1, bf16[2,256,512]{2,1,0:T(8,128)(2,1)} %k_ref.1, bf16[2,256,512]{2,1,0:T(8,128)(2,1)} %v_ref.1, s32[2,8]{1,0:T(2,128)} %bitcast.16, f32[2,8]{1,0:T(2,128)} %bitcast.17), custom_call_target="tpu_custom_call" | custom-call | tf_op jit(solution)/shard_map/update/pallas_call | solution.py:377
  10.7 10.6 %all_to_all.30.msg_ref = bf16[4,296,128]{2,1,0:T(8,128)(2,1)S(1)} all-to-all(bf16[4,296,128]{2,1,0:T(8,128)(2,1)} %get-tuple-element.9), channel_id=1, replica_groups=mesh['z'=16,'x'=4,'y'=4,'core'=2] {'x'}, dimensions={0} | all-to-all | bytes 606208 | tf_op jit(solution)/shard_map/all_to_all | solution.py:368
  21.3 0.3 group.1
  21.7 27.1 %all_to_all.31.msg_ref = bf16[16,40,128]{2,1,0:T(8,128)(2,1)S(1)} all-to-all(bf16[16,40,128]{2,1,0:T(8,128)(2,1)S(1)} %group.1), channel_id=1, replica_groups=mesh['z'=16,'x'=4,'y'=4,'core'=2] {'z'}, dimensions={0} | all-to-all | bytes 327680 | tf_op jit(solution)/shard_map/all_to_all | solution.py:368
  48.8 0.3 scan.1
  49.1 18.2 %all_to_all.32.back_ref = bf16[16,48,128]{2,1,0:T(8,128)(2,1)S(1)} all-to-all(bf16[16,48,128]{2,1,0:T(8,128)(2,1)S(1)} %get-tuple-element.10), channel_id=1, replica_groups=mesh['z'=16,'x'=4,'y'=4,'core'=2] {'z'}, dimensions={0} | all-to-all | bytes 393216 | tf_op jit(solution)/shard_map/all_to_all | solution.py:368
  67.3 0.0 copy-done.8
  67.3 1.5 expand.1
  68.8 39.1 %all_to_all.33.rows_ref = bf16[32,256,128]{2,1,0:T(8,128)(2,1)S(1)} all-to-all(bf16[32,256,128]{2,1,0:T(8,128)(2,1)S(1)} %get-tuple-element.13), channel_id=1, replica_groups=mesh['z'=16,'x'=4,'y'=4,'core'=2] {'x','y','core'}, dimensions={0} | all-to-all | bytes 4194304 | tf_op jit(solution)/shard_map/all_to_all | solution.py:368
  107.9 0.0 copy-done.3
  107.9 0.0 copy-done.4
  107.9 0.0 copy-done.5
  107.9 3.7 %experts.1 = bf16[32,64,512]{2,1,0:T(8,128)(2,1)} custom-call(bf16[32,256,128]{2,1,0:T(8,128)(2,1)S(1)} %all_to_all.33.rows_ref, bf16[4096,128]{1,0:T(8,128)(2,1)S(1)} %bitcast.9, bf16[4096,128]{1,0:T(8,128)(2,1)S(1)} %bitcast.10, bf16[128,4096]{1,0:T(8,128)(2,1)S(1)} %bitcast.11), custom_call_target="tpu_custom_call" | custom-call | tf_op jit(solution)/shard_map/experts/pallas_call | solution.py:412
  111.7 4.0 %all-to-all-start.4 = ((bf16[32,64,512]{2,1,0:T(8,128)(2,1)}), bf16[32,64,512]{2,1,0:T(8,128)(2,1)S(1)}, u32[]{:S(2)}, u32[]{:S(2)}) async-start(bf16[32,64,512]{2,1,0:T(8,128)(2,1)} %experts.1), calls=%async_computation.4 | async-start | bytes 4194304 | tf_op jit(solution)/shard_map/all_to_all | solution.py:368
  115.6 0.0 copy-start
  115.6 0.0 copy-start.1
  115.6 0.0 copy-start.7
  115.7 0.0 all-gather.3.cloned.1.call-start
  115.7 0.7 all-gather.3.cloned.1.call-update
  116.4 33.1 %all-to-all-done.4.parts_ref = bf16[32,64,512]{2,1,0:T(8,128)(2,1)S(1)} async-done(((bf16[32,64,512]{2,1,0:T(8,128)(2,1)}), bf16[32,64,512]{2,1,0:T(8,128)(2,1)S(1)}, u32[]{:S(2)}, u32[]{:S(2)}) %all-to-all-start.4) | async-done | bytes 2097184 | tf_op jit(solution)/shard_map/all_to_all | solution.py:368
  149.5 1.2 combine.1
  150.6 3.5 %all-to-all-start.5 = ((bf16[16,8,512]{2,1,0:T(8,128)(2,1)}), bf16[16,8,512]{2,1,0:T(8,128)(2,1)S(1)}, u32[]{:S(2)}, u32[]{:S(2)}) async-start(bf16[16,8,512]{2,1,0:T(8,128)(2,1)} %bitcast.8), calls=%async_computation.5 | async-start | bytes 262144 | tf_op jit(solution)/shard_map/all_to_all | solution.py:368
  154.1 0.0 all-gather.3.cloned.1.call-done
  154.2 0.0 copy-done
  154.2 0.0 copy-done.1
  154.2 0.0 copy-start.2
  154.2 1.0 copy-done.2
  155.2 1.2 copy-done.6
  156.5 3.0 %attention.1 = bf16[2,256,512]{2,1,0:T(8,128)(2,1)} custom-call(bf16[2,256,512]{2,1,0:T(8,128)(2,1)S(1)} %copy-done, bf16[2,256,512]{2,1,0:T(8,128)(2,1)S(1)} %copy-done.1, bf16[2,256,512]{2,1,0:T(8,128)(2,1)S(1)} %copy-done.2, f32[8,256]{1,0:T(8,128)S(1)} %copy-done.7, bf16[4,4,256,128]{3,2,1,0:T(8,128)(2,1)S(1)} %bitcast.12, f32[1,512]{1,0:T(1,128)S(1)} %bitcast.14), custom_call_target="tpu_custom_call" | custom-call | tf_op jit(solution)/shard_map/attention/pallas_call | solution.py:409
  159.4 6.6 %all-to-all-done.5.parts_ref = bf16[16,8,512]{2,1,0:T(8,128)(2,1)S(1)} async-done(((bf16[16,8,512]{2,1,0:T(8,128)(2,1)}), bf16[16,8,512]{2,1,0:T(8,128)(2,1)S(1)}, u32[]{:S(2)}, u32[]{:S(2)}) %all-to-all-start.5) | async-done | bytes 131104 | tf_op jit(solution)/shard_map/all_to_all | solution.py:368
  166.1 0.6 sum_z.1
  (5 shorter events, 0.0 us)
Async XLA Ops:
  7.2 60.1 %copy-start.8 = (f32[512]{0:T(512)S(1)}, f32[512]{0:T(512)}, u32[]{:S(2)}) copy-start(f32[512]{0:T(512)} %param.14) | copy-start | bytes 6148
  68.8 39.2 %copy-start.3 = (bf16[1,4096,128]{2,1,0:T(8,128)(2,1)S(1)}, bf16[1,4096,128]{2,1,0:T(8,128)(2,1)}, u32[]{:S(2)}) copy-start(bf16[1,4096,128]{2,1,0:T(8,128)(2,1)} %param.17) | copy-start | bytes 3145732
  68.8 39.2 %copy-start.4 = (bf16[1,4096,128]{2,1,0:T(8,128)(2,1)S(1)}, bf16[1,4096,128]{2,1,0:T(8,128)(2,1)}, u32[]{:S(2)}) copy-start(bf16[1,4096,128]{2,1,0:T(8,128)(2,1)} %param.18) | copy-start | bytes 3145732
  68.8 39.2 %copy-start.5 = (bf16[1,128,4096]{2,1,0:T(8,128)(2,1)S(1)}, bf16[1,128,4096]{2,1,0:T(8,128)(2,1)}, u32[]{:S(2)}) copy-start(bf16[1,128,4096]{2,1,0:T(8,128)(2,1)} %param.19) | copy-start | bytes 3145732
  111.7 37.8 %all-to-all-start.4 = ((bf16[32,64,512]{2,1,0:T(8,128)(2,1)}), bf16[32,64,512]{2,1,0:T(8,128)(2,1)S(1)}, u32[]{:S(2)}, u32[]{:S(2)}) async-start(bf16[32,64,512]{2,1,0:T(8,128)(2,1)} %experts.1), calls=%async_computation.4 | async-start | bytes 4194304 | tf_op jit(solution)/shard_map/all_to_all | solution.py:368
  115.6 38.6 %copy-start = (bf16[2,256,512]{2,1,0:T(8,128)(2,1)S(1)}, bf16[2,256,512]{2,1,0:T(8,128)(2,1)}, u32[]{:S(2)}) copy-start(bf16[2,256,512]{2,1,0:T(8,128)(2,1)} %q_ref.1) | copy-start | bytes 1572868
  115.6 38.5 %copy-start.1 = (bf16[2,256,512]{2,1,0:T(8,128)(2,1)S(1)}, bf16[2,256,512]{2,1,0:T(8,128)(2,1)}, u32[]{:S(2)}) copy-start(bf16[2,256,512]{2,1,0:T(8,128)(2,1)} %k_ref.1) | copy-start | bytes 1572868
  115.6 38.5 %copy-start.7 = (f32[8,256]{1,0:T(8,128)S(1)}, f32[8,256]{1,0:T(8,128)}, u32[]{:S(2)}) copy-start(f32[8,256]{1,0:T(8,128)} %get-tuple-element.8.run_ref) | copy-start | bytes 24580
  115.7 38.5 %all-gather.3.cloned.1.call-start = ((), (), s32[]{:S(2)}) async-start(), calls=%async_computation.6 | async-start | bytes 1310720 | tf_op jit(solution)/shard_map/all_gather | solution.py:408
  150.6 15.5 %all-to-all-start.5 = ((bf16[16,8,512]{2,1,0:T(8,128)(2,1)}), bf16[16,8,512]{2,1,0:T(8,128)(2,1)S(1)}, u32[]{:S(2)}, u32[]{:S(2)}) async-start(bf16[16,8,512]{2,1,0:T(8,128)(2,1)} %bitcast.8), calls=%async_computation.5 | async-start | bytes 262144 | tf_op jit(solution)/shard_map/all_to_all | solution.py:368
  154.2 1.0 copy-start.2
  155.2 1.2 copy-start.6
Sparse Core Ops, SparseCore 0:
  119.2 31.4 all-gather.2

commit v5 on v4

--- a/solution.py
+++ b/solution.py
@@ -31,15 +31,17 @@
 BF16 = jnp.bfloat16
 
 
-def call(kernel, out, name, scratch=(), fetch=False):
+def call(kernel, out, name, scratch=(), places=None):
     vmem = pl.BlockSpec(memory_space=pltpu.VMEM)
-    specs = {"in_specs": [pl.BlockSpec(memory_space=pl.ANY)] * 6} if fetch else {}
+    specs = {}
+    if places:
+        specs["in_specs"] = [pl.BlockSpec(memory_space=pl.ANY) if p else vmem for p in places]
     return pl.pallas_call(
         kernel,
         out_shape=out,
         out_specs=jax.tree.map(lambda _: vmem, out),
         scratch_shapes=scratch,
-        compiler_params=pltpu.CompilerParams(vmem_limit_bytes=(60 if fetch else 40) * 2**20),
+        compiler_params=pltpu.CompilerParams(vmem_limit_bytes=(56 if places else 40) * 2**20),
         name=name,
         **specs,
     )
@@ -121,15 +123,17 @@
         copies.append(pltpu.make_async_copy(part, target, semaphores.at[i]))
     for copy in copies:
         copy.start()
-    for copy in copies:
-        copy.wait()
     decay_ref, q_ref, k_ref, v_ref, ids_ref, gates_ref = fetched
+    for i in (0, 4, 5):
+        copies[i].wait()
     running = prefix_sums(jnp.concatenate([decay_ref[0], decay_ref[1]], axis=0))
     run_ref[...] = running
     end = running[:, TOK - 1 :]
     to_end = jnp.exp(end - running).T
     columns = running.T[:FEW]
     route_facts(ids_ref, gates_ref, facts_ref)
+    for i in (1, 2, 3):
+        copies[i].wait()
     for owner in range(X):
         parts, logs, qs, locals_ = [], [], [], []
         for i in range(OWN):
@@ -295,13 +299,12 @@
 
 
 def attention_kernel(q_ref, k_ref, v_ref, run_ref, state_ref, gain_ref, out_ref):
-    here = lax.axis_index("x")
     running = run_ref[...]
     columns = running.T
     for pair in range(PAIRS):
         b, cols = pair // HEADS, pl.ds(pair % HEADS * HD, HD)
         q, column = q_ref[b, :, cols], columns[:, pair : pair + 1]
-        state = state_ref[pair % HEADS, here, b * HD : (b + 1) * HD]
+        state = state_ref[pair % HEADS, b * HD : (b + 1) * HD]
         weights = fading_scores(q, k_ref[b, :, cols], column, running[pair : pair + 1])
         decayed = (q.astype(F32) * jnp.exp(column)).astype(BF16)
         o = jnp.dot(
@@ -321,17 +324,43 @@
     return rows, [facts[6:7], facts[7:8]]
 
 
-def expert_kernel(rows_ref, gate_ref, up_ref, down_ref, out_ref):
+def expert_kernel(
+    rows_hbm,
+    gate_hbm,
+    up_hbm,
+    down_hbm,
+    out_ref,
+    rows_ref,
+    gate_ref,
+    up_ref,
+    down_ref,
+    semaphores,
+):
+    copies = []
+    for j in range(EXPERTS):
+        part = pl.ds(j * COLS, COLS)
+        for source, target in (
+            (rows_hbm.at[:, j], rows_ref.at[j]),
+            (gate_hbm.at[part], gate_ref.at[part]),
+            (up_hbm.at[part], up_ref.at[part]),
+        ):
+            copies.append(pltpu.make_async_copy(source, target, semaphores.at[len(copies)]))
+    copies.append(pltpu.make_async_copy(down_hbm, down_ref, semaphores.at[len(copies)]))
+    for copy in copies:
+        copy.start()
     total = None
     for j in range(EXPERTS):
         part = pl.ds(j * COLS, COLS)
+        for copy in copies[3 * j : 3 * j + 3]:
+            copy.wait()
         both = jnp.concatenate([gate_ref[part, :], up_ref[part, :]], axis=1)
-        rows = jnp.concatenate([rows_ref[x * EXPERTS + j] for x in range(X)], axis=1)
+        rows = jnp.concatenate([rows_ref[j, x] for x in range(X)], axis=1)
         term = jnp.dot(rows, both, preferred_element_type=F32)
         total = term if total is None else total + term
     width = gate_ref.shape[1]
     gate, up = total[:, :width], total[:, width:]
     hidden = (gate / (1.0 + jnp.exp(-gate)) * up).astype(BF16)
+    copies[-1].wait()
     for j in range(EXPERTS):
         out = jnp.dot(hidden, down_ref[:, pl.ds(j * COLS, COLS)], preferred_element_type=F32)
         for x in range(X):
@@ -388,7 +417,7 @@
             pltpu.VMEM((8, HD), F32),
             pltpu.SemaphoreType.DMA((6,)),
         ],
-        True,
+        [True] * 6,
     )(decay, queries, keys, values, expert_ids.T, gate_weights.T)
     message = swap(message, "x")
     groups = call(group_kernel, shape((Z, PART + 24, HD), BF16), "group")(message)
@@ -405,14 +434,22 @@
         "expand",
     )(back, message, gain, facts)
     slots = swap(slots, ("x", "y", "core"))
-    states = lax.all_gather(states, "x", axis=0)
+    states = swap(states, "x")
     attn_out = call(attention_kernel, shape((2, TOK, COLS), BF16), "attention")(
         queries, keys, values, running, states, gain
     )
-    parts = call(expert_kernel, shape((X * EXPERTS, SLOTS, COLS), BF16), "experts")(
-        slots, w_gate[0], w_up[0], w_down[0]
-    )
+    weights = (w_gate[0], w_up[0], w_down[0])
+    parts = call(
+        expert_kernel,
+        shape((X * EXPERTS, SLOTS, COLS), BF16),
+        "experts",
+        [pltpu.VMEM((EXPERTS, X, X * SLOTS, HD), BF16)]
+        + [pltpu.VMEM(w.shape, BF16) for w in weights]
+        + [pltpu.SemaphoreType.DMA((3 * EXPERTS + 1,))],
+        [True] * 4,
+    )(slots.reshape(X, EXPERTS, X * SLOTS, HD), *weights)
     parts = swap(parts, ("x", "y", "core"))
+    parts, attn_out = lax.optimization_barrier((parts, attn_out))
     share = call(combine_kernel, shape((GROUP, COLS), BF16), "combine")(parts, facts)
     share = swap(share.reshape(Z, MROWS, COLS), "z")
     moe_out = call(sum_kernel, shape((MROWS, COLS), BF16), "sum_z")(share)

time: 176 us -> 164 us (0.932)
  blocking collectives: 95 us -> 111 us
  waiting for transfers between devices: 40.4 us -> 25.4 us
  between operations: 14.1 us -> 0.75 us
    all_to_all x4 -> x5, blocking collectives: 95 us -> 111 us  [swap(): return lax.all_to_all(array, axis, 0, 0, tiled=True)]
    all_to_all x2, waiting for transfers between devices: 39.7 us -> 25.4 us  [swap(): return lax.all_to_all(array, axis, 0, 0, tiled=True)]
  transfers between devices with their start and end apart: 3 -> 2, of which waited for: 2 -> 2; matrix products, arithmetic and copies ran while one was open for 0% -> 0% of each run, Pallas kernels for 2% -> 5%
where the time goes in v5:
time: 164 us; the launch traced here: 162 us
  blocking collectives  111 us (68%)
  waiting for transfers between devices  25.4 us (15%)
  Pallas kernels  15 us (9%)
  starting transfers between devices  8.72 us (5%)
    all_to_all x5, blocking collectives, swap(): return lax.all_to_all(array, axis, 0, 0, tiled=True)  111 us
    all_to_all x2, waiting for transfers between devices, swap(): return lax.all_to_all(array, axis, 0, 0, tiled=True)  25.4 us
    all_to_all x2, starting transfers between devices, swap(): return lax.all_to_all(array, axis, 0, 0, tiled=True)  8.72 us
    pallas_call x1, Pallas kernels, body(): call(expert_kernel, shape((X * EXPERTS, SLOTS, COLS), BF16), 'experts', [...  5.46 us
    pallas_call x1, Pallas kernels, body(): call(update_kernel, (shape((PAIRS, TOK), F32), shape((X, AT_FACTS + 8, HD...  3.38 us
  transfers between devices with their start and end apart: 2, of which 2 were waited for; matrix products, arithmetic and copies ran while one was open for 0% of the time, Pallas kernels for 5%

profile of v5, /device:TPU:1, one launch (start us, length us, event | category | flops | bytes accessed | tf_op | source)
XLA Modules:
  0.0 161.8 jit_solution(1845391216683470181)
XLA Ops:
  0.6 0.0 copy-start.4
  0.6 3.4 %update.1 = (f32[8,256]{1,0:T(8,128)}, bf16[4,296,128]{2,1,0:T(8,128)(2,1)}) custom-call(f32[2,4,256]{2,1,0:T(4,128)} %bitcast.16, bf16[2,256,512]{2,1,0:T(8,128)(2,1)} %q_ref.1, bf16[2,256,512]{2,1,0:T(8,128)(2,1)} %k_ref.1, bf16[2,256,512]{2,1,0:T(8,128)(2,1)} %v_ref.1, s32[2,8]{1,0:T(2,128)} %bitcast.17, f32[2,8]{1,0:T(2,128)} %bitcast.18), custom_call_target="tpu_custom_call" | custom-call | tf_op jit(solution)/shard_map/update/pallas_call | solution.py:406
  4.0 10.6 %all_to_all.35.msg_ref = bf16[4,296,128]{2,1,0:T(8,128)(2,1)S(1)} all-to-all(bf16[4,296,128]{2,1,0:T(8,128)(2,1)} %get-tuple-element.10), channel_id=1, replica_groups=mesh['z'=16,'x'=4,'y'=4,'core'=2] {'x'}, dimensions={0} | all-to-all | bytes 606208 | tf_op jit(solution)/shard_map/all_to_all | solution.py:397
  14.6 0.3 group.1
  15.0 27.1 %all_to_all.36.msg_ref = bf16[16,40,128]{2,1,0:T(8,128)(2,1)S(1)} all-to-all(bf16[16,40,128]{2,1,0:T(8,128)(2,1)S(1)} %group.1), channel_id=1, replica_groups=mesh['z'=16,'x'=4,'y'=4,'core'=2] {'z'}, dimensions={0} | all-to-all | bytes 327680 | tf_op jit(solution)/shard_map/all_to_all | solution.py:397
  42.0 0.3 scan.1
  42.4 18.2 %all_to_all.37.back_ref = bf16[16,48,128]{2,1,0:T(8,128)(2,1)S(1)} all-to-all(bf16[16,48,128]{2,1,0:T(8,128)(2,1)S(1)} %get-tuple-element.11), channel_id=1, replica_groups=mesh['z'=16,'x'=4,'y'=4,'core'=2] {'z'}, dimensions={0} | all-to-all | bytes 393216 | tf_op jit(solution)/shard_map/all_to_all | solution.py:397
  60.6 0.0 copy-done.4
  60.6 1.5 expand.1
  62.0 39.0 %all_to_all.38 = bf16[32,256,128]{2,1,0:T(8,128)(2,1)} all-to-all(bf16[32,256,128]{2,1,0:T(8,128)(2,1)S(1)} %get-tuple-element.13), channel_id=1, replica_groups=mesh['z'=16,'x'=4,'y'=4,'core'=2] {'x','y','core'}, dimensions={0} | all-to-all | bytes 4194304 | tf_op jit(solution)/shard_map/all_to_all | solution.py:397
  101.0 3.4 %all-to-all-start.5 = ((bf16[4,256,128]{2,1,0:T(8,128)(2,1)}), bf16[4,256,128]{2,1,0:T(8,128)(2,1)S(1)}, u32[]{:S(2)}, u32[]{:S(2)}) async-start(bf16[4,256,128]{2,1,0:T(8,128)(2,1)} %get-tuple-element.15), calls=%async_computation.5 | async-start | bytes 524288 | tf_op jit(solution)/shard_map/all_to_all | solution.py:397
  104.4 5.5 %experts.1 = bf16[32,64,512]{2,1,0:T(8,128)(2,1)} custom-call(bf16[4,8,256,128]{3,2,1,0:T(8,128)(2,1)} %bitcast.12, bf16[4096,128]{1,0:T(8,128)(2,1)} %bitcast.13, bf16[4096,128]{1,0:T(8,128)(2,1)} %bitcast.14, bf16[128,4096]{1,0:T(8,128)(2,1)} %bitcast.15), custom_call_target="tpu_custom_call" | custom-call | tf_op jit(solution)/shard_map/experts/pallas_call | solution.py:442
  109.9 0.0 copy-start
  109.9 0.0 copy-start.1
  109.9 0.0 copy-start.3
  110.0 1.1 all-to-all-done.5.state_ref
  111.1 5.3 %all-to-all-start.4 = ((bf16[32,64,512]{2,1,0:T(8,128)(2,1)}), bf16[32,64,512]{2,1,0:T(8,128)(2,1)S(1)}, u32[]{:S(2)}, u32[]{:S(2)}) async-start(bf16[32,64,512]{2,1,0:T(8,128)(2,1)} %experts.1), calls=%async_computation.4 | async-start | bytes 4194304 | tf_op jit(solution)/shard_map/all_to_all | solution.py:397
  116.4 0.0 copy-done
  116.4 0.0 copy-done.1
  116.4 0.0 copy-done.3
  116.4 0.0 copy-start.2
  116.4 1.0 copy-done.2
  117.5 3.0 %attention.1 = bf16[2,256,512]{2,1,0:T(8,128)(2,1)} custom-call(bf16[2,256,512]{2,1,0:T(8,128)(2,1)S(1)} %copy-done, bf16[2,256,512]{2,1,0:T(8,128)(2,1)S(1)} %copy-done.1, bf16[2,256,512]{2,1,0:T(8,128)(2,1)S(1)} %copy-done.2, f32[8,256]{1,0:T(8,128)S(1)} %copy-done.3, bf16[4,256,128]{2,1,0:T(8,128)(2,1)S(1)} %all-to-all-done.5.state_ref, f32[1,512]{1,0:T(1,128)S(1)} %bitcast.11), custom_call_target="tpu_custom_call" | custom-call | tf_op jit(solution)/shard_map/attention/pallas_call | solution.py:438
  120.5 24.2 %all-to-all-done.4.parts_ref = bf16[32,64,512]{2,1,0:T(8,128)(2,1)S(1)} async-done(((bf16[32,64,512]{2,1,0:T(8,128)(2,1)}), bf16[32,64,512]{2,1,0:T(8,128)(2,1)S(1)}, u32[]{:S(2)}, u32[]{:S(2)}) %all-to-all-start.4) | async-done | bytes 2097184 | tf_op jit(solution)/shard_map/all_to_all | solution.py:397
  144.7 0.5 combine.1
  145.2 16.0 %all_to_all.39.parts_ref = bf16[16,8,512]{2,1,0:T(8,128)(2,1)S(1)} all-to-all(bf16[16,8,512]{2,1,0:T(8,128)(2,1)S(1)} %bitcast.9), channel_id=1, replica_groups=mesh['z'=16,'x'=4,'y'=4,'core'=2] {'z'}, dimensions={0} | all-to-all | bytes 262144 | tf_op jit(solution)/shard_map/all_to_all | solution.py:397
  161.2 0.6 sum_z.1
Async XLA Ops:
  0.6 60.0 %copy-start.4 = (f32[512]{0:T(512)S(1)}, f32[512]{0:T(512)}, u32[]{:S(2)}) copy-start(f32[512]{0:T(512)} %param.14) | copy-start | bytes 6148
  101.0 10.0 %all-to-all-start.5 = ((bf16[4,256,128]{2,1,0:T(8,128)(2,1)}), bf16[4,256,128]{2,1,0:T(8,128)(2,1)S(1)}, u32[]{:S(2)}, u32[]{:S(2)}) async-start(bf16[4,256,128]{2,1,0:T(8,128)(2,1)} %get-tuple-element.15), calls=%async_computation.5 | async-start | bytes 524288 | tf_op jit(solution)/shard_map/all_to_all | solution.py:397
  109.9 6.5 %copy-start = (bf16[2,256,512]{2,1,0:T(8,128)(2,1)S(1)}, bf16[2,256,512]{2,1,0:T(8,128)(2,1)}, u32[]{:S(2)}) copy-start(bf16[2,256,512]{2,1,0:T(8,128)(2,1)} %q_ref.1) | copy-start | bytes 1572868
  109.9 6.5 %copy-start.1 = (bf16[2,256,512]{2,1,0:T(8,128)(2,1)S(1)}, bf16[2,256,512]{2,1,0:T(8,128)(2,1)}, u32[]{:S(2)}) copy-start(bf16[2,256,512]{2,1,0:T(8,128)(2,1)} %k_ref.1) | copy-start | bytes 1572868
  109.9 6.5 %copy-start.3 = (f32[8,256]{1,0:T(8,128)S(1)}, f32[8,256]{1,0:T(8,128)}, u32[]{:S(2)}) copy-start(f32[8,256]{1,0:T(8,128)} %get-tuple-element.14.run_ref) | copy-start | bytes 24580
  111.1 33.6 %all-to-all-start.4 = ((bf16[32,64,512]{2,1,0:T(8,128)(2,1)}), bf16[32,64,512]{2,1,0:T(8,128)(2,1)S(1)}, u32[]{:S(2)}, u32[]{:S(2)}) async-start(bf16[32,64,512]{2,1,0:T(8,128)(2,1)} %experts.1), calls=%async_computation.4 | async-start | bytes 4194304 | tf_op jit(solution)/shard_map/all_to_all | solution.py:397
  116.4 1.0 copy-start.2

commit v6 on v5

--- a/solution.py
+++ b/solution.py
@@ -31,15 +31,16 @@
 BF16 = jnp.bfloat16
 
 
-def call(kernel, out, name, scratch=(), places=None):
-    vmem = pl.BlockSpec(memory_space=pltpu.VMEM)
-    specs = {}
+def call(kernel, out, name, scratch=(), places=None, results=None):
+    vmem, own = pl.BlockSpec(memory_space=pltpu.VMEM), pl.BlockSpec(memory_space=pl.ANY)
+    specs = {"out_specs": jax.tree.map(lambda _: vmem, out)}
     if places:
-        specs["in_specs"] = [pl.BlockSpec(memory_space=pl.ANY) if p else vmem for p in places]
+        specs["in_specs"] = [own if p else vmem for p in places]
+    if results:
+        specs["out_specs"] = tuple(own if p else vmem for p in results)
     return pl.pallas_call(
         kernel,
         out_shape=out,
-        out_specs=jax.tree.map(lambda _: vmem, out),
         scratch_shapes=scratch,
         compiler_params=pltpu.CompilerParams(vmem_limit_bytes=(56 if places else 40) * 2**20),
         name=name,
@@ -115,26 +116,34 @@
 
 
 def update_kernel(*refs):
-    sources, (run_ref, msg_ref), fetched = refs[:6], refs[6:8], refs[8:14]
-    facts_ref, semaphores = refs[14:]
-    copies = []
-    for i, (source, target) in enumerate(zip(sources, fetched)):
-        part = source.at[:, pl.ds(0, FEW)] if i == 1 else source
-        copies.append(pltpu.make_async_copy(part, target, semaphores.at[i]))
-    for copy in copies:
-        copy.start()
+    sources, (run_ref, msg_hbm), fetched = refs[:6], refs[6:8], refs[8:14]
+    msg_ref, facts_ref, semaphores = refs[14:]
+
+    def copy(i, source, target):
+        return pltpu.make_async_copy(source, target, semaphores.at[i])
+
     decay_ref, q_ref, k_ref, v_ref, ids_ref, gates_ref = fetched
-    for i in (0, 4, 5):
-        copies[i].wait()
+    first = [copy(i, sources[i], fetched[i]) for i in (0, 4, 5)]
+    first.append(copy(1, sources[1].at[:, pl.ds(0, FEW)], q_ref))
+    heads = []
+    for owner in range(X):
+        part = (slice(None), slice(None), pl.ds(owner * HD, HD))
+        for i in (2, 3):
+            heads.append(copy(6 + len(heads), sources[i].at[part], fetched[i].at[part]))
+    for fetch in first + heads:
+        fetch.start()
+    for fetch in first:
+        fetch.wait()
     running = prefix_sums(jnp.concatenate([decay_ref[0], decay_ref[1]], axis=0))
     run_ref[...] = running
     end = running[:, TOK - 1 :]
     to_end = jnp.exp(end - running).T
     columns = running.T[:FEW]
     route_facts(ids_ref, gates_ref, facts_ref)
-    for i in (1, 2, 3):
-        copies[i].wait()
+    sent = []
     for owner in range(X):
+        for fetch in heads[2 * owner : 2 * owner + 2]:
+            fetch.wait()
         parts, logs, qs, locals_ = [], [], [], []
         for i in range(OWN):
             b, pair, cols = i, i * HEADS + owner, pl.ds(owner * HD, HD)
@@ -156,6 +165,10 @@
         msg_ref[owner] = jnp.concatenate(
             parts + [stacked_rows(logs), beside(*qs), local[0], local[1], facts_ref[...]], axis=0
         ).astype(BF16)
+        sent.append(copy(14 + owner, msg_ref.at[owner], msg_hbm.at[owner]))
+        sent[-1].start()
+    for send in sent:
+        send.wait()
 
 
 def placed(rows, i, x):
@@ -414,10 +427,12 @@
             pltpu.VMEM((2, TOK, COLS), BF16),
             pltpu.VMEM((2, MROWS), jnp.int32),
             pltpu.VMEM((2, MROWS), F32),
+            pltpu.VMEM((X, AT_FACTS + 8, HD), BF16),
             pltpu.VMEM((8, HD), F32),
-            pltpu.SemaphoreType.DMA((6,)),
+            pltpu.SemaphoreType.DMA((18,)),
         ],
         [True] * 6,
+        [False, True],
     )(decay, queries, keys, values, expert_ids.T, gate_weights.T)
     message = swap(message, "x")
     groups = call(group_kernel, shape((Z, PART + 24, HD), BF16), "group")(message)
@@ -435,9 +450,6 @@
     )(back, message, gain, facts)
     slots = swap(slots, ("x", "y", "core"))
     states = swap(states, "x")
-    attn_out = call(attention_kernel, shape((2, TOK, COLS), BF16), "attention")(
-        queries, keys, values, running, states, gain
-    )
     weights = (w_gate[0], w_up[0], w_down[0])
     parts = call(
         expert_kernel,
@@ -448,8 +460,11 @@
         + [pltpu.SemaphoreType.DMA((3 * EXPERTS + 1,))],
         [True] * 4,
     )(slots.reshape(X, EXPERTS, X * SLOTS, HD), *weights)
+    parts, states = lax.optimization_barrier((parts, states))
+    attn_out = call(attention_kernel, shape((2, TOK, COLS), BF16), "attention")(
+        queries, keys, values, running, states, gain
+    )
     parts = swap(parts, ("x", "y", "core"))
-    parts, attn_out = lax.optimization_barrier((parts, attn_out))
     share = call(combine_kernel, shape((GROUP, COLS), BF16), "combine")(parts, facts)
     share = swap(share.reshape(Z, MROWS, COLS), "z")
     moe_out = call(sum_kernel, shape((MROWS, COLS), BF16), "sum_z")(share)

time: 164 us -> 165 us (level)
  blocking collectives: 111 us -> 128 us
  waiting for transfers between devices: 25.4 us -> 10.3 us
  Pallas kernels: 15 us -> 16.8 us
    all_to_all x5, blocking collectives: 111 us -> 128 us  [swap(): return lax.all_to_all(array, axis, 0, 0, tiled=True)]
    all_to_all x2, waiting for transfers between devices: 25.4 us -> 10.3 us  [swap(): return lax.all_to_all(array, axis, 0, 0, tiled=True)]
where the time goes in v6:
time: 165 us; the launch traced here: 164 us
  blocking collectives  128 us (78%)
  Pallas kernels  16.8 us (10%)
  waiting for transfers between devices  10.3 us (6%)
  starting transfers between devices  7.61 us (5%)
    all_to_all x5, blocking collectives, swap(): return lax.all_to_all(array, axis, 0, 0, tiled=True)  128 us
    all_to_all x2, waiting for transfers between devices, swap(): return lax.all_to_all(array, axis, 0, 0, tiled=True)  10.3 us
    all_to_all x2, starting transfers between devices, swap(): return lax.all_to_all(array, axis, 0, 0, tiled=True)  7.61 us
    pallas_call x1, Pallas kernels, body(): call(expert_kernel, shape((X * EXPERTS, SLOTS, COLS), BF16), 'experts', [...  5.46 us
    pallas_call x1, Pallas kernels, body(): call(update_kernel, (shape((PAIRS, TOK), F32), shape((X, AT_FACTS + 8, HD...  4.49 us
  transfers between devices with their start and end apart: 2, of which 2 were waited for; matrix products, arithmetic and copies ran while one was open for 0% of the time, Pallas kernels for 5%

profile of v6, /device:TPU:1, one launch (start us, length us, event | category | flops | bytes accessed | tf_op | source)
XLA Modules:
  0.0 163.6 jit_solution(11990214319206015881)
XLA Ops:
  0.6 0.0 copy-start.4
  0.6 4.5 %update.1 = (f32[8,256]{1,0:T(8,128)}, bf16[4,296,128]{2,1,0:T(8,128)(2,1)}) custom-call(f32[2,4,256]{2,1,0:T(4,128)} %bitcast.15, bf16[2,256,512]{2,1,0:T(8,128)(2,1)} %q_ref.1, bf16[2,256,512]{2,1,0:T(8,128)(2,1)} %k_ref.1, bf16[2,256,512]{2,1,0:T(8,128)(2,1)} %v_ref.1, s32[2,8]{1,0:T(2,128)} %bitcast.16, f32[2,8]{1,0:T(2,128)} %bitcast.17), custom_call_target="tpu_custom_call" | custom-call | tf_op jit(solution)/shard_map/update/pallas_call | solution.py:419
  5.1 10.6 %all_to_all.35.msg_ref = bf16[4,296,128]{2,1,0:T(8,128)(2,1)S(1)} all-to-all(bf16[4,296,128]{2,1,0:T(8,128)(2,1)} %get-tuple-element.11), channel_id=1, replica_groups=mesh['z'=16,'x'=4,'y'=4,'core'=2] {'x'}, dimensions={0} | all-to-all | bytes 606208 | tf_op jit(solution)/shard_map/all_to_all | solution.py:410
  15.7 0.3 group.1
  16.1 27.1 %all_to_all.36.msg_ref = bf16[16,40,128]{2,1,0:T(8,128)(2,1)S(1)} all-to-all(bf16[16,40,128]{2,1,0:T(8,128)(2,1)S(1)} %group.1), channel_id=1, replica_groups=mesh['z'=16,'x'=4,'y'=4,'core'=2] {'z'}, dimensions={0} | all-to-all | bytes 327680 | tf_op jit(solution)/shard_map/all_to_all | solution.py:410
  43.1 0.3 scan.1
  43.5 18.2 %all_to_all.37.back_ref = bf16[16,48,128]{2,1,0:T(8,128)(2,1)S(1)} all-to-all(bf16[16,48,128]{2,1,0:T(8,128)(2,1)S(1)} %get-tuple-element.12), channel_id=1, replica_groups=mesh['z'=16,'x'=4,'y'=4,'core'=2] {'z'}, dimensions={0} | all-to-all | bytes 393216 | tf_op jit(solution)/shard_map/all_to_all | solution.py:410
  61.7 0.0 copy-done.4
  61.7 1.5 expand.1
  63.1 39.0 %all_to_all.38 = bf16[32,256,128]{2,1,0:T(8,128)(2,1)} all-to-all(bf16[32,256,128]{2,1,0:T(8,128)(2,1)S(1)} %get-tuple-element.14), channel_id=1, replica_groups=mesh['z'=16,'x'=4,'y'=4,'core'=2] {'x','y','core'}, dimensions={0} | all-to-all | bytes 4194304 | tf_op jit(solution)/shard_map/all_to_all | solution.py:410
  102.1 3.4 %all-to-all-start.4 = ((bf16[4,256,128]{2,1,0:T(8,128)(2,1)}), bf16[4,256,128]{2,1,0:T(8,128)(2,1)S(1)}, u32[]{:S(2)}, u32[]{:S(2)}) async-start(bf16[4,256,128]{2,1,0:T(8,128)(2,1)} %get-tuple-element.15), calls=%async_computation.4 | async-start | bytes 524288 | tf_op jit(solution)/shard_map/all_to_all | solution.py:410
  105.6 5.5 %experts.1 = bf16[32,64,512]{2,1,0:T(8,128)(2,1)} custom-call(bf16[4,8,256,128]{3,2,1,0:T(8,128)(2,1)} %bitcast.11, bf16[4096,128]{1,0:T(8,128)(2,1)} %bitcast.12, bf16[4096,128]{1,0:T(8,128)(2,1)} %bitcast.13, bf16[128,4096]{1,0:T(8,128)(2,1)} %bitcast.14), custom_call_target="tpu_custom_call" | custom-call | tf_op jit(solution)/shard_map/experts/pallas_call | solution.py:454
  111.0 1.2 all-to-all-done.4.state_ref
  112.2 33.3 %all_to_all.39.parts_ref = bf16[32,64,512]{2,1,0:T(8,128)(2,1)S(1)} all-to-all(bf16[32,64,512]{2,1,0:T(8,128)(2,1)} %experts.1), channel_id=1, replica_groups=mesh['z'=16,'x'=4,'y'=4,'core'=2] {'x','y','core'}, dimensions={0} | all-to-all | bytes 4194304 | tf_op jit(solution)/shard_map/all_to_all | solution.py:410
  145.5 0.0 copy-start
  145.5 0.0 copy-start.1
  145.5 0.0 copy-start.2
  145.5 0.0 copy-start.3
  145.5 1.1 combine.1
  146.6 4.2 %all-to-all-start.6 = ((bf16[16,8,512]{2,1,0:T(8,128)(2,1)}), bf16[16,8,512]{2,1,0:T(8,128)(2,1)S(1)}, u32[]{:S(2)}, u32[]{:S(2)}) async-start(bf16[16,8,512]{2,1,0:T(8,128)(2,1)} %bitcast.8), calls=%async_computation.6 | async-start | bytes 262144 | tf_op jit(solution)/shard_map/all_to_all | solution.py:410
  150.8 0.0 copy-done
  150.8 0.0 copy-done.1
  150.9 0.0 copy-done.2
  150.9 0.0 copy-done.3
  150.9 3.0 %attention.1 = bf16[2,256,512]{2,1,0:T(8,128)(2,1)} custom-call(bf16[2,256,512]{2,1,0:T(8,128)(2,1)S(1)} %copy-done, bf16[2,256,512]{2,1,0:T(8,128)(2,1)S(1)} %copy-done.1, bf16[2,256,512]{2,1,0:T(8,128)(2,1)S(1)} %copy-done.2, f32[8,256]{1,0:T(8,128)S(1)} %copy-done.3, bf16[4,256,128]{2,1,0:T(8,128)(2,1)S(1)} %all-to-all-done.4.state_ref, f32[1,512]{1,0:T(1,128)S(1)} %bitcast.10), custom_call_target="tpu_custom_call" | custom-call | tf_op jit(solution)/shard_map/attention/pallas_call | solution.py:464
  153.9 9.1 %all-to-all-done.6.parts_ref = bf16[16,8,512]{2,1,0:T(8,128)(2,1)S(1)} async-done(((bf16[16,8,512]{2,1,0:T(8,128)(2,1)}), bf16[16,8,512]{2,1,0:T(8,128)(2,1)S(1)}, u32[]{:S(2)}, u32[]{:S(2)}) %all-to-all-start.6) | async-done | bytes 131104 | tf_op jit(solution)/shard_map/all_to_all | solution.py:410
  163.0 0.6 sum_z.1
Async XLA Ops:
  0.6 61.1 %copy-start.4 = (f32[512]{0:T(512)S(1)}, f32[512]{0:T(512)}, u32[]{:S(2)}) copy-start(f32[512]{0:T(512)} %param.14) | copy-start | bytes 6148
  102.1 10.0 %all-to-all-start.4 = ((bf16[4,256,128]{2,1,0:T(8,128)(2,1)}), bf16[4,256,128]{2,1,0:T(8,128)(2,1)S(1)}, u32[]{:S(2)}, u32[]{:S(2)}) async-start(bf16[4,256,128]{2,1,0:T(8,128)(2,1)} %get-tuple-element.15), calls=%async_computation.4 | async-start | bytes 524288 | tf_op jit(solution)/shard_map/all_to_all | solution.py:410
  145.5 5.4 %copy-start = (bf16[2,256,512]{2,1,0:T(8,128)(2,1)S(1)}, bf16[2,256,512]{2,1,0:T(8,128)(2,1)}, u32[]{:S(2)}) copy-start(bf16[2,256,512]{2,1,0:T(8,128)(2,1)} %q_ref.1) | copy-start | bytes 1572868
  145.5 5.4 %copy-start.1 = (bf16[2,256,512]{2,1,0:T(8,128)(2,1)S(1)}, bf16[2,256,512]{2,1,0:T(8,128)(2,1)}, u32[]{:S(2)}) copy-start(bf16[2,256,512]{2,1,0:T(8,128)(2,1)} %k_ref.1) | copy-start | bytes 1572868
  145.5 5.4 %copy-start.2 = (bf16[2,256,512]{2,1,0:T(8,128)(2,1)S(1)}, bf16[2,256,512]{2,1,0:T(8,128)(2,1)}, u32[]{:S(2)}) copy-start(bf16[2,256,512]{2,1,0:T(8,128)(2,1)} %v_ref.1) | copy-start | bytes 1572868
  145.5 5.4 %copy-start.3 = (f32[8,256]{1,0:T(8,128)S(1)}, f32[8,256]{1,0:T(8,128)}, u32[]{:S(2)}) copy-start(f32[8,256]{1,0:T(8,128)} %get-tuple-element.10.run_ref) | copy-start | bytes 24580
  146.6 16.4 %all-to-all-start.6 = ((bf16[16,8,512]{2,1,0:T(8,128)(2,1)}), bf16[16,8,512]{2,1,0:T(8,128)(2,1)S(1)}, u32[]{:S(2)}, u32[]{:S(2)}) async-start(bf16[16,8,512]{2,1,0:T(8,128)(2,1)} %bitcast.8), calls=%async_computation.6 | async-start | bytes 262144 | tf_op jit(solution)/shard_map/all_to_all | solution.py:410

commit v7 on v4

--- a/solution.py
+++ b/solution.py
@@ -31,15 +31,17 @@
 BF16 = jnp.bfloat16
 
 
-def call(kernel, out, name, scratch=(), fetch=False):
+def call(kernel, out, name, scratch=(), places=None):
     vmem = pl.BlockSpec(memory_space=pltpu.VMEM)
-    specs = {"in_specs": [pl.BlockSpec(memory_space=pl.ANY)] * 6} if fetch else {}
+    specs = {}
+    if places:
+        specs["in_specs"] = [pl.BlockSpec(memory_space=pl.ANY) if p else vmem for p in places]
     return pl.pallas_call(
         kernel,
         out_shape=out,
         out_specs=jax.tree.map(lambda _: vmem, out),
         scratch_shapes=scratch,
-        compiler_params=pltpu.CompilerParams(vmem_limit_bytes=(60 if fetch else 40) * 2**20),
+        compiler_params=pltpu.CompilerParams(vmem_limit_bytes=(56 if places else 40) * 2**20),
         name=name,
         **specs,
     )
@@ -121,15 +123,17 @@
         copies.append(pltpu.make_async_copy(part, target, semaphores.at[i]))
     for copy in copies:
         copy.start()
-    for copy in copies:
-        copy.wait()
     decay_ref, q_ref, k_ref, v_ref, ids_ref, gates_ref = fetched
+    for i in (0, 4, 5):
+        copies[i].wait()
     running = prefix_sums(jnp.concatenate([decay_ref[0], decay_ref[1]], axis=0))
     run_ref[...] = running
     end = running[:, TOK - 1 :]
     to_end = jnp.exp(end - running).T
     columns = running.T[:FEW]
     route_facts(ids_ref, gates_ref, facts_ref)
+    for i in (1, 2, 3):
+        copies[i].wait()
     for owner in range(X):
         parts, logs, qs, locals_ = [], [], [], []
         for i in range(OWN):
@@ -281,10 +285,7 @@
         for e in range(EXPERTS):
             for x in range(X):
                 at = e * HD + x * 32
-                for target in range(X):
-                    slots_ref[target * EXPERTS + e, pl.ds(x * SLOTS + half * 32, 32)] = sent[
-                        at : at + 32
-                    ]
+                slots_ref[e, pl.ds(x * SLOTS + half * 32, 32)] = sent[at : at + 32]
     for x in range(X):
         state_ref[x] = jnp.concatenate(state, axis=0).astype(BF16)
         if x < X - 1:
@@ -295,13 +296,12 @@
 
 
 def attention_kernel(q_ref, k_ref, v_ref, run_ref, state_ref, gain_ref, out_ref):
-    here = lax.axis_index("x")
     running = run_ref[...]
     columns = running.T
     for pair in range(PAIRS):
         b, cols = pair // HEADS, pl.ds(pair % HEADS * HD, HD)
         q, column = q_ref[b, :, cols], columns[:, pair : pair + 1]
-        state = state_ref[pair % HEADS, here, b * HD : (b + 1) * HD]
+        state = state_ref[pair % HEADS, b * HD : (b + 1) * HD]
         weights = fading_scores(q, k_ref[b, :, cols], column, running[pair : pair + 1])
         decayed = (q.astype(F32) * jnp.exp(column)).astype(BF16)
         o = jnp.dot(
@@ -321,14 +321,36 @@
     return rows, [facts[6:7], facts[7:8]]
 
 
-def expert_kernel(rows_ref, gate_ref, up_ref, down_ref, out_ref):
+def share_of_hidden(rows, where, step, gate_ref, up_ref):
+    x = lax.rem(lax.axis_index("x") + step, X)
     total = None
-    for j in range(EXPERTS):
-        part = pl.ds(j * COLS, COLS)
-        both = jnp.concatenate([gate_ref[part, :], up_ref[part, :]], axis=1)
-        rows = jnp.concatenate([rows_ref[x * EXPERTS + j] for x in range(X)], axis=1)
-        term = jnp.dot(rows, both, preferred_element_type=F32)
+    for j in range(0, len(rows), 2):
+        parts = [pl.ds(pl.multiple_of((where + i) * COLS + x * HD, HD), HD) for i in (j, j + 1)]
+        both = jnp.concatenate(
+            [jnp.concatenate([gate_ref[p, :], up_ref[p, :]], axis=1) for p in parts], axis=0
+        )
+        term = jnp.dot(
+            jnp.concatenate(rows[j : j + 2], axis=1), both, preferred_element_type=F32
+        )
         total = term if total is None else total + term
+    return total
+
+
+def near_kernel(own_ref, left_ref, right_ref, gate_ref, up_ref, out_ref):
+    total = None
+    for step, ref in ((0, own_ref), (1, right_ref), (X - 1, left_ref)):
+        rows = [ref[e] for e in range(EXPERTS)]
+        term = share_of_hidden(rows, 0, step, gate_ref, up_ref)
+        total = term if total is None else total + term
+    out_ref[...] = total
+
+
+def expert_kernel(sum_ref, first_ref, second_ref, gate_ref, up_ref, down_ref, out_ref):
+    half = EXPERTS // 2
+    total = sum_ref[...]
+    for where, ref in ((0, first_ref), (half, second_ref)):
+        rows = [ref[e] for e in range(half)]
+        total = total + share_of_hidden(rows, where, 2, gate_ref, up_ref)
     width = gate_ref.shape[1]
     gate, up = total[:, :width], total[:, width:]
     hidden = (gate / (1.0 + jnp.exp(-gate)) * up).astype(BF16)
@@ -366,6 +388,10 @@
 
 def swap(array, axis):
     return lax.all_to_all(array, axis, 0, 0, tiled=True)
+
+
+def shift(array, step):
+    return lax.ppermute(array, "x", [(x, (x + step) % X) for x in range(X)])
 
 
 def body(
@@ -388,7 +414,7 @@
             pltpu.VMEM((8, HD), F32),
             pltpu.SemaphoreType.DMA((6,)),
         ],
-        True,
+        [True] * 6,
     )(decay, queries, keys, values, expert_ids.T, gate_weights.T)
     message = swap(message, "x")
     groups = call(group_kernel, shape((Z, PART + 24, HD), BF16), "group")(message)
@@ -401,18 +427,26 @@
     back = swap(back, "z")
     states, slots = call(
         expand_kernel,
-        (shape((X, OWN * HD, HD), BF16), shape((X * EXPERTS, X * SLOTS, HD), BF16)),
+        (shape((X, OWN * HD, HD), BF16), shape((EXPERTS, X * SLOTS, HD), BF16)),
         "expand",
     )(back, message, gain, facts)
-    slots = swap(slots, ("x", "y", "core"))
-    states = lax.all_gather(states, "x", axis=0)
+    slots = swap(slots, ("y", "core"))
+    slots, states = lax.optimization_barrier((slots, states))
+    left, right = shift(slots, 1), shift(slots, -1)
+    states = swap(states, "x")
+    left, right, states = lax.optimization_barrier((left, right, states))
+    half = EXPERTS // 2
+    first, second = shift(right[:half], -1), shift(left[half:], 1)
+    weights = (w_gate[0], w_up[0])
+    near = call(near_kernel, shape((X * SLOTS, 2 * HD), F32), "near")(slots, left, right, *weights)
+    parts = call(expert_kernel, shape((X * EXPERTS, SLOTS, COLS), BF16), "experts")(
+        near, first, second, *weights, w_down[0]
+    )
     attn_out = call(attention_kernel, shape((2, TOK, COLS), BF16), "attention")(
         queries, keys, values, running, states, gain
     )
-    parts = call(expert_kernel, shape((X * EXPERTS, SLOTS, COLS), BF16), "experts")(
-        slots, w_gate[0], w_up[0], w_down[0]
-    )
     parts = swap(parts, ("x", "y", "core"))
+    parts, attn_out = lax.optimization_barrier((parts, attn_out))
     share = call(combine_kernel, shape((GROUP, COLS), BF16), "combine")(parts, facts)
     share = swap(share.reshape(Z, MROWS, COLS), "z")
     moe_out = call(sum_kernel, shape((MROWS, COLS), BF16), "sum_z")(share)

time: 176 us -> 171 us (0.972)
  starting transfers between devices: 7.51 us -> 22.2 us
  between operations: 14.1 us -> 0.81 us
  waiting for transfers between devices: 40.4 us -> 30.1 us
  blocking collectives: 95 us -> 103 us
  Pallas kernels: 14.2 us -> 12 us
    all_to_all x2 -> x1, waiting for transfers between devices: 39.7 us -> 24.3 us  [swap(): return lax.all_to_all(array, axis, 0, 0, tiled=True)]
    ppermute x0 -> x4, starting transfers between devices: none -> 14 us  [shift(): return lax.ppermute(array, 'x', [(x, (x + step) % X) for x in range(X)])]
    all_to_all x4 -> x6, blocking collectives: 95 us -> 103 us  [swap(): return lax.all_to_all(array, axis, 0, 0, tiled=True)]
    ppermute x0 -> x4, waiting for transfers between devices: none -> 5.79 us  [shift(): return lax.ppermute(array, 'x', [(x, (x + step) % X) for x in range(X)])]
    all_to_all x2 -> x1, starting transfers between devices: 7.47 us -> 8.17 us  [swap(): return lax.all_to_all(array, axis, 0, 0, tiled=True)]
  transfers between devices with their start and end apart: 3 -> 5, of which waited for: 2 -> 3; matrix products, arithmetic and copies ran while one was open for 0% -> 0% of each run, Pallas kernels for 2% -> 2%
where the time goes in v7:
time: 171 us; the launch traced here: 169 us
  blocking collectives  103 us (60%)
  waiting for transfers between devices  30.1 us (18%)
  starting transfers between devices  22.2 us (13%)
  Pallas kernels  12 us (7%)
    all_to_all x6, blocking collectives, swap(): return lax.all_to_all(array, axis, 0, 0, tiled=True)  103 us
    all_to_all x1, waiting for transfers between devices, swap(): return lax.all_to_all(array, axis, 0, 0, tiled=True)  24.3 us
    ppermute x4, starting transfers between devices, shift(): return lax.ppermute(array, 'x', [(x, (x + step) % X) for x in range(X)])  14 us
    all_to_all x1, starting transfers between devices, swap(): return lax.all_to_all(array, axis, 0, 0, tiled=True)  8.17 us
    ppermute x4, waiting for transfers between devices, shift(): return lax.ppermute(array, 'x', [(x, (x + step) % X) for x in range(X)])  5.79 us
  transfers between devices with their start and end apart: 5, of which 3 were waited for; matrix products, arithmetic and copies ran while one was open for 0% of the time, Pallas kernels for 2%

profile of v7, /device:TPU:1, one launch (start us, length us, event | category | flops | bytes accessed | tf_op | source)
XLA Modules:
  0.0 169.1 jit_solution(11225111704724186501)
XLA Ops:
  0.6 0.0 copy-start.7
  0.6 3.4 %update.1 = (f32[8,256]{1,0:T(8,128)}, bf16[4,296,128]{2,1,0:T(8,128)(2,1)}) custom-call(f32[2,4,256]{2,1,0:T(4,128)} %bitcast.16, bf16[2,256,512]{2,1,0:T(8,128)(2,1)} %q_ref.1, bf16[2,256,512]{2,1,0:T(8,128)(2,1)} %k_ref.1, bf16[2,256,512]{2,1,0:T(8,128)(2,1)} %v_ref.1, s32[2,8]{1,0:T(2,128)} %bitcast.17, f32[2,8]{1,0:T(2,128)} %bitcast.18), custom_call_target="tpu_custom_call" | custom-call | tf_op jit(solution)/shard_map/update/pallas_call | solution.py:403
  4.0 10.6 %all_to_all.35.msg_ref = bf16[4,296,128]{2,1,0:T(8,128)(2,1)S(1)} all-to-all(bf16[4,296,128]{2,1,0:T(8,128)(2,1)} %get-tuple-element.15), channel_id=1, replica_groups=mesh['z'=16,'x'=4,'y'=4,'core'=2] {'x'}, dimensions={0} | all-to-all | bytes 606208 | tf_op jit(solution)/shard_map/all_to_all | solution.py:390
  14.6 0.3 group.1
  15.0 0.0 copy-start
  15.0 0.0 copy-start.1
  15.0 27.2 %all_to_all.36.msg_ref = bf16[16,40,128]{2,1,0:T(8,128)(2,1)S(1)} all-to-all(bf16[16,40,128]{2,1,0:T(8,128)(2,1)S(1)} %group.1), channel_id=1, replica_groups=mesh['z'=16,'x'=4,'y'=4,'core'=2] {'z'}, dimensions={0} | all-to-all | bytes 327680 | tf_op jit(solution)/shard_map/all_to_all | solution.py:390
  42.2 0.3 scan.1
  42.5 18.2 %all_to_all.37.back_ref = bf16[16,48,128]{2,1,0:T(8,128)(2,1)S(1)} all-to-all(bf16[16,48,128]{2,1,0:T(8,128)(2,1)S(1)} %get-tuple-element.16), channel_id=1, replica_groups=mesh['z'=16,'x'=4,'y'=4,'core'=2] {'z'}, dimensions={0} | all-to-all | bytes 393216 | tf_op jit(solution)/shard_map/all_to_all | solution.py:390
  60.7 0.0 copy-done.7
  60.7 0.7 expand.1
  61.5 19.2 %all_to_all.38.own_ref = bf16[8,256,128]{2,1,0:T(8,128)(2,1)S(1)} all-to-all(bf16[8,256,128]{2,1,0:T(8,128)(2,1)S(1)} %get-tuple-element.18), channel_id=1, replica_groups=mesh['z'=16,'x'=4,'y'=4,'core'=2] {'y','core'}, dimensions={0} | all-to-all | bytes 1048576 | tf_op jit(solution)/shard_map/all_to_all | solution.py:390
  80.7 2.2 %collective-permute-start = (bf16[8,256,128]{2,1,0:T(8,128)(2,1)S(1)}, bf16[8,256,128]{2,1,0:T(8,128)(2,1)S(1)}, u32[]{:S(2)}, u32[]{:S(2)}) collective-permute-start(bf16[8,256,128]{2,1,0:T(8,128)(2,1)S(1)} %all_to_all.38.own_ref), channel_id=1, source_target_pairs={{0,8},{8,16},{16,24},{24,0},{1,9},{9,17},{17,25},{25,1},{2,10},{10... | collective-permute-start | bytes 1572872 | tf_op jit(solution)/shard_map/ppermute | solution.py:394
  82.9 4.3 %collective-permute-start.1 = (bf16[8,256,128]{2,1,0:T(8,128)(2,1)S(1)}, bf16[8,256,128]{2,1,0:T(8,128)(2,1)S(1)}, u32[]{:S(2)}, u32[]{:S(2)}) collective-permute-start(bf16[8,256,128]{2,1,0:T(8,128)(2,1)S(1)} %all_to_all.38.own_ref), channel_id=1, source_target_pairs={{0,24},{8,0},{16,8},{24,16},{1,25},{9,1},{17,9},{25,17},{2,26},{10... | collective-permute-start | bytes 1572872 | tf_op jit(solution)/shard_map/ppermute | solution.py:394
  87.2 11.8 %all_to_all.39.state_ref = bf16[4,256,128]{2,1,0:T(8,128)(2,1)S(1)} all-to-all(bf16[4,256,128]{2,1,0:T(8,128)(2,1)S(1)} %get-tuple-element.21), channel_id=1, replica_groups=mesh['z'=16,'x'=4,'y'=4,'core'=2] {'x'}, dimensions={0} | all-to-all | bytes 524288 | tf_op jit(solution)/shard_map/all_to_all | solution.py:390
  99.0 0.0 collective-permute-done.left_ref
  99.0 0.0 collective-permute-done.1.right_ref
  99.1 5.5 %collective-permute-start.2 = (bf16[4,256,128]{2,1,0:T(8,128)(2,1)S(1)}, bf16[4,256,128]{2,1,0:T(8,128)(2,1)S(1)}, u32[]{:S(2)}, u32[]{:S(2)}) collective-permute-start(bf16[4,256,128]{2,1,0:T(8,128)(2,1)S(1)} %slice.6), channel_id=1, source_target_pairs={{0,24},{8,0},{16,8},{24,16},{1,25},{9,1},{17,9},{25,17},{2,26},{10... | collective-permute-start | bytes 786440 | tf_op jit(solution)/shard_map/ppermute | solution.py:394
  104.6 0.0 copy-start.5
  104.6 2.1 %collective-permute-start.3 = (bf16[4,256,128]{2,1,0:T(8,128)(2,1)S(1)}, bf16[4,256,128]{2,1,0:T(8,128)(2,1)S(1)}, u32[]{:S(2)}, u32[]{:S(2)}) collective-permute-start(bf16[4,256,128]{2,1,0:T(8,128)(2,1)S(1)} %slice.7), channel_id=1, source_target_pairs={{0,8},{8,16},{16,24},{24,0},{1,9},{9,17},{17,25},{25,1},{2,10},{10... | collective-permute-start | bytes 786440 | tf_op jit(solution)/shard_map/ppermute | solution.py:394
  106.7 0.6 near.1.sum_ref
  107.3 0.6 collective-permute-done.2.first_ref
  107.8 5.2 %collective-permute-done.3.second_ref = bf16[4,256,128]{2,1,0:T(8,128)(2,1)S(1)} collective-permute-done((bf16[4,256,128]{2,1,0:T(8,128)(2,1)S(1)}, bf16[4,256,128]{2,1,0:T(8,128)(2,1)S(1)}, u32[]{:S(2)}, u32[]{:S(2)}) %collective-permute-start.3) | collective-permute-done | bytes 262176 | tf_op jit(solution)/shard_map/ppermute | solution.py:394
  113.0 2.5 %experts.1 = bf16[32,64,512]{2,1,0:T(8,128)(2,1)} custom-call(f32[256,256]{1,0:T(8,128)S(1)} %near.1.sum_ref, bf16[4,256,128]{2,1,0:T(8,128)(2,1)S(1)} %collective-permute-done.2.first_ref, bf16[4,256,128]{2,1,0:T(8,128)(2,1)S(1)} %collective-permute-done.3.second_ref, bf16[4096,128]{1,0:T(8,128)(2,1)S(1)} %bitcast.9, bf16[4096,128]{1,0:T(8,128)(2,1)S(1)} %bitcast.11, ...), custom_call_target="tpu_custom_call" | custom-call | tf_op jit(solution)/shard_map/experts/pallas_call | solution.py:442
  115.6 8.2 %all-to-all-start.5 = ((bf16[32,64,512]{2,1,0:T(8,128)(2,1)}), bf16[32,64,512]{2,1,0:T(8,128)(2,1)S(1)}, u32[]{:S(2)}, u32[]{:S(2)}) async-start(bf16[32,64,512]{2,1,0:T(8,128)(2,1)} %experts.1), calls=%async_computation.5 | async-start | bytes 4194304 | tf_op jit(solution)/shard_map/all_to_all | solution.py:390
  123.8 0.0 copy-start.4
  123.8 1.0 copy-done.4
  124.8 3.0 %attention.1 = bf16[2,256,512]{2,1,0:T(8,128)(2,1)} custom-call(bf16[2,256,512]{2,1,0:T(8,128)(2,1)S(1)} %copy-done.2, bf16[2,256,512]{2,1,0:T(8,128)(2,1)S(1)} %copy-done.3, bf16[2,256,512]{2,1,0:T(8,128)(2,1)S(1)} %copy-done.4, f32[8,256]{1,0:T(8,128)S(1)} %copy-done.6, bf16[4,256,128]{2,1,0:T(8,128)(2,1)S(1)} %all_to_all.39.state_ref, f32[1,512]{1,0:T(1,128)S(1)} %bitcast.15), custom_call_target="tpu_custom_call" | custom-call | tf_op jit(solution)/shard_map/attention/pallas_call | solution.py:445
  127.8 24.3 %all-to-all-done.5.parts_ref = bf16[32,64,512]{2,1,0:T(8,128)(2,1)S(1)} async-done(((bf16[32,64,512]{2,1,0:T(8,128)(2,1)}), bf16[32,64,512]{2,1,0:T(8,128)(2,1)S(1)}, u32[]{:S(2)}, u32[]{:S(2)}) %all-to-all-start.5) | async-done | bytes 2097184 | tf_op jit(solution)/shard_map/all_to_all | solution.py:390
  152.1 0.5 combine.1
  152.6 15.9 %all_to_all.40.parts_ref = bf16[16,8,512]{2,1,0:T(8,128)(2,1)S(1)} all-to-all(bf16[16,8,512]{2,1,0:T(8,128)(2,1)S(1)} %bitcast.13), channel_id=1, replica_groups=mesh['z'=16,'x'=4,'y'=4,'core'=2] {'z'}, dimensions={0} | all-to-all | bytes 262144 | tf_op jit(solution)/shard_map/all_to_all | solution.py:390
  168.5 0.6 sum_z.1
  (11 shorter events, 0.1 us)
Async XLA Ops:
  0.6 60.1 %copy-start.7 = (f32[512]{0:T(512)S(1)}, f32[512]{0:T(512)}, u32[]{:S(2)}) copy-start(f32[512]{0:T(512)} %param.14) | copy-start | bytes 6148
  15.0 91.7 %copy-start = (bf16[1,4096,128]{2,1,0:T(8,128)(2,1)S(1)}, bf16[1,4096,128]{2,1,0:T(8,128)(2,1)}, u32[]{:S(2)}) copy-start(bf16[1,4096,128]{2,1,0:T(8,128)(2,1)} %param.17) | copy-start | bytes 3145732
  15.0 91.7 %copy-start.1 = (bf16[1,4096,128]{2,1,0:T(8,128)(2,1)S(1)}, bf16[1,4096,128]{2,1,0:T(8,128)(2,1)}, u32[]{:S(2)}) copy-start(bf16[1,4096,128]{2,1,0:T(8,128)(2,1)} %param.18) | copy-start | bytes 3145732
  80.7 18.3 %collective-permute-start = (bf16[8,256,128]{2,1,0:T(8,128)(2,1)S(1)}, bf16[8,256,128]{2,1,0:T(8,128)(2,1)S(1)}, u32[]{:S(2)}, u32[]{:S(2)}) collective-permute-start(bf16[8,256,128]{2,1,0:T(8,128)(2,1)S(1)} %all_to_all.38.own_ref), channel_id=1, source_target_pairs={{0,8},{8,16},{16,24},{24,0},{1,9},{9,17},{17,25},{25,1},{2,10},{10... | collective-permute-start | bytes 1572872 | tf_op jit(solution)/shard_map/ppermute | solution.py:394
  82.9 16.1 %collective-permute-start.1 = (bf16[8,256,128]{2,1,0:T(8,128)(2,1)S(1)}, bf16[8,256,128]{2,1,0:T(8,128)(2,1)S(1)}, u32[]{:S(2)}, u32[]{:S(2)}) collective-permute-start(bf16[8,256,128]{2,1,0:T(8,128)(2,1)S(1)} %all_to_all.38.own_ref), channel_id=1, source_target_pairs={{0,24},{8,0},{16,8},{24,16},{1,25},{9,1},{17,9},{25,17},{2,26},{10... | collective-permute-start | bytes 1572872 | tf_op jit(solution)/shard_map/ppermute | solution.py:394
  99.1 8.8 %collective-permute-start.2 = (bf16[4,256,128]{2,1,0:T(8,128)(2,1)S(1)}, bf16[4,256,128]{2,1,0:T(8,128)(2,1)S(1)}, u32[]{:S(2)}, u32[]{:S(2)}) collective-permute-start(bf16[4,256,128]{2,1,0:T(8,128)(2,1)S(1)} %slice.6), channel_id=1, source_target_pairs={{0,24},{8,0},{16,8},{24,16},{1,25},{9,1},{17,9},{25,17},{2,26},{10... | collective-permute-start | bytes 786440 | tf_op jit(solution)/shard_map/ppermute | solution.py:394
  104.6 8.5 %copy-start.5 = (bf16[1,128,4096]{2,1,0:T(8,128)(2,1)S(1)}, bf16[1,128,4096]{2,1,0:T(8,128)(2,1)}, u32[]{:S(2)}) copy-start(bf16[1,128,4096]{2,1,0:T(8,128)(2,1)} %param.19) | copy-start | bytes 3145732
  104.6 8.5 %collective-permute-start.3 = (bf16[4,256,128]{2,1,0:T(8,128)(2,1)S(1)}, bf16[4,256,128]{2,1,0:T(8,128)(2,1)S(1)}, u32[]{:S(2)}, u32[]{:S(2)}) collective-permute-start(bf16[4,256,128]{2,1,0:T(8,128)(2,1)S(1)} %slice.7), channel_id=1, source_target_pairs={{0,8},{8,16},{16,24},{24,0},{1,9},{9,17},{17,25},{25,1},{2,10},{10... | collective-permute-start | bytes 786440 | tf_op jit(solution)/shard_map/ppermute | solution.py:394
  115.6 8.2 %copy-start.2 = (bf16[2,256,512]{2,1,0:T(8,128)(2,1)S(1)}, bf16[2,256,512]{2,1,0:T(8,128)(2,1)}, u32[]{:S(2)}) copy-start(bf16[2,256,512]{2,1,0:T(8,128)(2,1)} %q_ref.1) | copy-start | bytes 1572868
  115.6 8.2 %copy-start.3 = (bf16[2,256,512]{2,1,0:T(8,128)(2,1)S(1)}, bf16[2,256,512]{2,1,0:T(8,128)(2,1)}, u32[]{:S(2)}) copy-start(bf16[2,256,512]{2,1,0:T(8,128)(2,1)} %k_ref.1) | copy-start | bytes 1572868
  115.6 8.2 %copy-start.6 = (f32[8,256]{1,0:T(8,128)S(1)}, f32[8,256]{1,0:T(8,128)}, u32[]{:S(2)}) copy-start(f32[8,256]{1,0:T(8,128)} %get-tuple-element.24.run_ref) | copy-start | bytes 24580
  115.6 36.6 %all-to-all-start.5 = ((bf16[32,64,512]{2,1,0:T(8,128)(2,1)}), bf16[32,64,512]{2,1,0:T(8,128)(2,1)S(1)}, u32[]{:S(2)}, u32[]{:S(2)}) async-start(bf16[32,64,512]{2,1,0:T(8,128)(2,1)} %experts.1), calls=%async_computation.5 | async-start | bytes 4194304 | tf_op jit(solution)/shard_map/all_to_all | solution.py:390
  123.8 1.0 copy-start.4

commit v8 on v4

--- a/solution.py
+++ b/solution.py
@@ -18,6 +18,7 @@
 OWN = PAIRS // X
 PART = OWN * HD // Z
 SLOTS = Z * CAP
+PIECE = OWN * HD // (X * EXPERTS)
 HALF = MROWS // 2
 FEW = 16
 GROUP = Z * MROWS
@@ -31,15 +32,17 @@
 BF16 = jnp.bfloat16
 
 
-def call(kernel, out, name, scratch=(), fetch=False):
+def call(kernel, out, name, scratch=(), places=None):
     vmem = pl.BlockSpec(memory_space=pltpu.VMEM)
-    specs = {"in_specs": [pl.BlockSpec(memory_space=pl.ANY)] * 6} if fetch else {}
+    specs = {}
+    if places:
+        specs["in_specs"] = [pl.BlockSpec(memory_space=pl.ANY) if p else vmem for p in places]
     return pl.pallas_call(
         kernel,
         out_shape=out,
         out_specs=jax.tree.map(lambda _: vmem, out),
         scratch_shapes=scratch,
-        compiler_params=pltpu.CompilerParams(vmem_limit_bytes=(60 if fetch else 40) * 2**20),
+        compiler_params=pltpu.CompilerParams(vmem_limit_bytes=(56 if places else 40) * 2**20),
         name=name,
         **specs,
     )
@@ -121,15 +124,17 @@
         copies.append(pltpu.make_async_copy(part, target, semaphores.at[i]))
     for copy in copies:
         copy.start()
-    for copy in copies:
-        copy.wait()
     decay_ref, q_ref, k_ref, v_ref, ids_ref, gates_ref = fetched
+    for i in (0, 4, 5):
+        copies[i].wait()
     running = prefix_sums(jnp.concatenate([decay_ref[0], decay_ref[1]], axis=0))
     run_ref[...] = running
     end = running[:, TOK - 1 :]
     to_end = jnp.exp(end - running).T
     columns = running.T[:FEW]
     route_facts(ids_ref, gates_ref, facts_ref)
+    for i in (1, 2, 3):
+        copies[i].wait()
     for owner in range(X):
         parts, logs, qs, locals_ = [], [], [], []
         for i in range(OWN):
@@ -253,7 +258,7 @@
     facts_ref[...] = jnp.concatenate(facts, axis=1)
 
 
-def expand_kernel(back_ref, msg_ref, gain_ref, facts_ref, state_ref, slots_ref):
+def expand_kernel(back_ref, msg_ref, gain_ref, facts_ref, slots_ref):
     gain = gain_ref[:, :HD]
     for x in range(1, X):
         gain = jnp.where(lax.axis_index("x") == x, gain_ref[:, x * HD : (x + 1) * HD], gain)
@@ -285,23 +290,31 @@
                     slots_ref[target * EXPERTS + e, pl.ds(x * SLOTS + half * 32, 32)] = sent[
                         at : at + 32
                     ]
+    entering = []
     for x in range(X):
-        state_ref[x] = jnp.concatenate(state, axis=0).astype(BF16)
+        entering.append(jnp.concatenate(state, axis=0))
         if x < X - 1:
             part = msg_ref[x].astype(F32)
             for i in range(OWN):
                 factor = jnp.exp(joined_log(part, AT_LOGS + 4 * i))
                 state[i] = factor * state[i] + part[i * HD : (i + 1) * HD]
-
-
-def attention_kernel(q_ref, k_ref, v_ref, run_ref, state_ref, gain_ref, out_ref):
-    here = lax.axis_index("x")
+    for m in range(X * EXPERTS):
+        pieces = [own[m * PIECE : (m + 1) * PIECE] for own in entering]
+        slots_ref[m, pl.ds(X * SLOTS, X * PIECE)] = jnp.concatenate(pieces, axis=0).astype(BF16)
+
+
+def attention_kernel(q_ref, k_ref, v_ref, run_ref, parts_ref, gain_ref, out_ref):
     running = run_ref[...]
     columns = running.T
+    pieces = [parts_ref[m].astype(F32)[SLOTS:] for m in range(X * EXPERTS)]
+    each = len(pieces) // 2
+    states = [
+        jnp.concatenate(pieces[b * each : (b + 1) * each], axis=0).astype(BF16) for b in range(2)
+    ]
     for pair in range(PAIRS):
         b, cols = pair // HEADS, pl.ds(pair % HEADS * HD, HD)
         q, column = q_ref[b, :, cols], columns[:, pair : pair + 1]
-        state = state_ref[pair % HEADS, here, b * HD : (b + 1) * HD]
+        state = states[b][:, pair % HEADS * HD : (pair % HEADS + 1) * HD]
         weights = fading_scores(q, k_ref[b, :, cols], column, running[pair : pair + 1])
         decayed = (q.astype(F32) * jnp.exp(column)).astype(BF16)
         o = jnp.dot(
@@ -326,16 +339,21 @@
     for j in range(EXPERTS):
         part = pl.ds(j * COLS, COLS)
         both = jnp.concatenate([gate_ref[part, :], up_ref[part, :]], axis=1)
-        rows = jnp.concatenate([rows_ref[x * EXPERTS + j] for x in range(X)], axis=1)
-        term = jnp.dot(rows, both, preferred_element_type=F32)
+        rows = [rows_ref[x * EXPERTS + j, : X * SLOTS] for x in range(X)]
+        term = jnp.dot(jnp.concatenate(rows, axis=1), both, preferred_element_type=F32)
         total = term if total is None else total + term
     width = gate_ref.shape[1]
     gate, up = total[:, :width], total[:, width:]
     hidden = (gate / (1.0 + jnp.exp(-gate)) * up).astype(BF16)
     for j in range(EXPERTS):
         out = jnp.dot(hidden, down_ref[:, pl.ds(j * COLS, COLS)], preferred_element_type=F32)
+        passing = jnp.concatenate(
+            [rows_ref[x * EXPERTS + j, X * SLOTS :].astype(F32) for x in range(X)], axis=1
+        )
         for x in range(X):
-            out_ref[x * EXPERTS + j] = out[x * SLOTS : (x + 1) * SLOTS].astype(BF16)
+            out_ref[x * EXPERTS + j] = jnp.concatenate(
+                [out[x * SLOTS : (x + 1) * SLOTS], passing[x * PIECE : (x + 1) * PIECE]], axis=0
+            ).astype(BF16)
 
 
 def combine_kernel(parts_ref, facts_ref, out_ref):
@@ -345,9 +363,9 @@
     mix = jnp.where(index == first, gates[0], 0.0) + jnp.where(index == second, gates[1], 0.0)
     rows = []
     for e in range(EXPERTS):
-        total = parts_ref[e].astype(F32)
+        total = parts_ref[e, :SLOTS].astype(F32)
         for x in range(1, X):
-            total = total + parts_ref[x * EXPERTS + e].astype(F32)
+            total = total + parts_ref[x * EXPERTS + e, :SLOTS].astype(F32)
         rows.append(total.astype(BF16))
     out_ref[...] = lax.dot_general(
         mix.astype(BF16),
@@ -388,7 +406,7 @@
             pltpu.VMEM((8, HD), F32),
             pltpu.SemaphoreType.DMA((6,)),
         ],
-        True,
+        [True] * 6,
     )(decay, queries, keys, values, expert_ids.T, gate_weights.T)
     message = swap(message, "x")
     groups = call(group_kernel, shape((Z, PART + 24, HD), BF16), "group")(message)
@@ -399,20 +417,17 @@
         "scan",
     )(groups)
     back = swap(back, "z")
-    states, slots = call(
-        expand_kernel,
-        (shape((X, OWN * HD, HD), BF16), shape((X * EXPERTS, X * SLOTS, HD), BF16)),
-        "expand",
+    slots = call(
+        expand_kernel, shape((X * EXPERTS, X * SLOTS + X * PIECE, HD), BF16), "expand"
     )(back, message, gain, facts)
     slots = swap(slots, ("x", "y", "core"))
-    states = lax.all_gather(states, "x", axis=0)
+    parts = call(expert_kernel, shape((X * EXPERTS, SLOTS + PIECE, COLS), BF16), "experts")(
+        slots, w_gate[0], w_up[0], w_down[0]
+    )
+    parts = swap(parts, ("x", "y", "core"))
     attn_out = call(attention_kernel, shape((2, TOK, COLS), BF16), "attention")(
-        queries, keys, values, running, states, gain
-    )
-    parts = call(expert_kernel, shape((X * EXPERTS, SLOTS, COLS), BF16), "experts")(
-        slots, w_gate[0], w_up[0], w_down[0]
-    )
-    parts = swap(parts, ("x", "y", "core"))
+        queries, keys, values, running, parts, gain
+    )
     share = call(combine_kernel, shape((GROUP, COLS), BF16), "combine")(parts, facts)
     share = swap(share.reshape(Z, MROWS, COLS), "z")
     moe_out = call(sum_kernel, shape((MROWS, COLS), BF16), "sum_z")(share)

time: 176 us -> 160 us (0.909); the launches traced: 174 us -> 159 us
  blocking collectives: 95 us -> 133 us
  waiting for transfers between devices: 40.4 us -> 8.1 us
  between operations: 14.1 us -> 0.75 us
  starting transfers between devices: 7.51 us -> 4.21 us
  Pallas kernels: 14.2 us -> 11.9 us
    all_to_all x4 -> x5, blocking collectives: 95 us -> 133 us  [swap(): return lax.all_to_all(array, axis, 0, 0, tiled=True)]
    all_to_all x2 -> x1, waiting for transfers between devices: 39.7 us -> 8.1 us  [swap(): return lax.all_to_all(array, axis, 0, 0, tiled=True)]
    all_to_all x2 -> x1, starting transfers between devices: 7.47 us -> 4.21 us  [swap(): return lax.all_to_all(array, axis, 0, 0, tiled=True)]
    pallas_call x2, Pallas kernels: 5.18 us -> 3.14 us  [the longest x1 2.39 us: body(): call(expert_kernel, shape((X * EXPERTS, SLOTS + PIECE, COLS), BF16), 'exp...]
  transfers between devices with their start and end apart: 3 -> 1, of which waited for: 2 -> 1; matrix products, arithmetic and copies ran while one was open for 0% -> 0% of each run, Pallas kernels for 2% -> 2%
where the time goes in v8:
time: 160 us; the launch traced here: 159 us
  blocking collectives  133 us (83%)
  Pallas kernels  11.9 us (7%)
  waiting for transfers between devices  8.1 us (5%)
  starting transfers between devices  4.21 us (3%)
    all_to_all x5, blocking collectives, swap(): return lax.all_to_all(array, axis, 0, 0, tiled=True)  133 us
    all_to_all x1, waiting for transfers between devices, swap(): return lax.all_to_all(array, axis, 0, 0, tiled=True)  8.1 us
    all_to_all x1, starting transfers between devices, swap(): return lax.all_to_all(array, axis, 0, 0, tiled=True)  4.21 us
    pallas_call x1, Pallas kernels, body(): call(update_kernel, (shape((PAIRS, TOK), F32), shape((X, AT_FACTS + 8, HD...  3.38 us
  transfers between devices with their start and end apart: 1, of which 1 were waited for; matrix products, arithmetic and copies ran while one was open for 0% of the time, Pallas kernels for 2%

profile of v8, /device:TPU:1, one launch (start us, length us, event | category | flops | bytes accessed | tf_op | source)
XLA Modules:
  0.0 159.3 jit_solution(14534134177716009832)
XLA Ops:
  0.6 0.0 copy-start.7
  0.6 3.4 %update.1 = (f32[8,256]{1,0:T(8,128)}, bf16[4,296,128]{2,1,0:T(8,128)(2,1)}) custom-call(f32[2,4,256]{2,1,0:T(4,128)} %bitcast.13, bf16[2,256,512]{2,1,0:T(8,128)(2,1)} %q_ref.1, bf16[2,256,512]{2,1,0:T(8,128)(2,1)} %k_ref.1, bf16[2,256,512]{2,1,0:T(8,128)(2,1)} %v_ref.1, s32[2,8]{1,0:T(2,128)} %bitcast.14, f32[2,8]{1,0:T(2,128)} %bitcast.15), custom_call_target="tpu_custom_call" | custom-call | tf_op jit(solution)/shard_map/update/pallas_call | solution.py:395
  4.0 10.6 %all_to_all.30.msg_ref = bf16[4,296,128]{2,1,0:T(8,128)(2,1)S(1)} all-to-all(bf16[4,296,128]{2,1,0:T(8,128)(2,1)} %get-tuple-element.7), channel_id=1, replica_groups=mesh['z'=16,'x'=4,'y'=4,'core'=2] {'x'}, dimensions={0} | all-to-all | bytes 606208 | tf_op jit(solution)/shard_map/all_to_all | solution.py:386
  14.6 0.3 group.1
  15.0 27.1 %all_to_all.31.msg_ref = bf16[16,40,128]{2,1,0:T(8,128)(2,1)S(1)} all-to-all(bf16[16,40,128]{2,1,0:T(8,128)(2,1)S(1)} %group.1), channel_id=1, replica_groups=mesh['z'=16,'x'=4,'y'=4,'core'=2] {'z'}, dimensions={0} | all-to-all | bytes 327680 | tf_op jit(solution)/shard_map/all_to_all | solution.py:386
  42.0 0.3 scan.1
  42.4 18.2 %all_to_all.32.back_ref = bf16[16,48,128]{2,1,0:T(8,128)(2,1)S(1)} all-to-all(bf16[16,48,128]{2,1,0:T(8,128)(2,1)S(1)} %get-tuple-element.8), channel_id=1, replica_groups=mesh['z'=16,'x'=4,'y'=4,'core'=2] {'z'}, dimensions={0} | all-to-all | bytes 393216 | tf_op jit(solution)/shard_map/all_to_all | solution.py:386
  60.6 0.0 copy-done.7
  60.6 0.8 expand.1
  61.3 0.0 copy-start.3
  61.4 0.0 copy-start.4
  61.4 0.0 copy-start.5
  61.4 42.5 %all_to_all.33.rows_ref = bf16[32,288,128]{2,1,0:T(8,128)(2,1)S(1)} all-to-all(bf16[32,288,128]{2,1,0:T(8,128)(2,1)S(1)} %expand.1), channel_id=1, replica_groups=mesh['z'=16,'x'=4,'y'=4,'core'=2] {'x','y','core'}, dimensions={0} | all-to-all | bytes 4718592 | tf_op jit(solution)/shard_map/all_to_all | solution.py:386
  103.9 0.0 copy-done.3
  103.9 0.0 copy-done.4
  103.9 0.0 copy-done.5
  103.9 2.4 %experts.1 = bf16[32,72,512]{2,1,0:T(8,128)(2,1)S(1)} custom-call(bf16[32,288,128]{2,1,0:T(8,128)(2,1)S(1)} %all_to_all.33.rows_ref, bf16[4096,128]{1,0:T(8,128)(2,1)S(1)} %bitcast.8, bf16[4096,128]{1,0:T(8,128)(2,1)S(1)} %bitcast.9, bf16[128,4096]{1,0:T(8,128)(2,1)S(1)} %bitcast.10), custom_call_target="tpu_custom_call" | custom-call | tf_op jit(solution)/shard_map/experts/pallas_call | solution.py:424
  106.3 34.9 %all_to_all.34.parts_ref = bf16[32,72,512]{2,1,0:T(8,128)(2,1)S(1)} all-to-all(bf16[32,72,512]{2,1,0:T(8,128)(2,1)S(1)} %experts.1), channel_id=1, replica_groups=mesh['z'=16,'x'=4,'y'=4,'core'=2] {'x','y','core'}, dimensions={0} | all-to-all | bytes 4718592 | tf_op jit(solution)/shard_map/all_to_all | solution.py:386
  141.2 0.0 copy-start
  141.2 0.0 copy-start.1
  141.2 0.0 copy-start.6
  141.2 1.1 combine.1
  142.3 4.2 %all-to-all-start.5 = ((bf16[16,8,512]{2,1,0:T(8,128)(2,1)}), bf16[16,8,512]{2,1,0:T(8,128)(2,1)S(1)}, u32[]{:S(2)}, u32[]{:S(2)}) async-start(bf16[16,8,512]{2,1,0:T(8,128)(2,1)} %bitcast.7), calls=%async_computation.5 | async-start | bytes 262144 | tf_op jit(solution)/shard_map/all_to_all | solution.py:386
  146.5 0.0 copy-done
  146.5 0.0 copy-done.1
  146.6 0.0 copy-done.6
  146.6 0.0 copy-start.2
  146.6 1.0 copy-done.2
  147.6 3.0 %attention.1 = bf16[2,256,512]{2,1,0:T(8,128)(2,1)} custom-call(bf16[2,256,512]{2,1,0:T(8,128)(2,1)S(1)} %copy-done, bf16[2,256,512]{2,1,0:T(8,128)(2,1)S(1)} %copy-done.1, bf16[2,256,512]{2,1,0:T(8,128)(2,1)S(1)} %copy-done.2, f32[8,256]{1,0:T(8,128)S(1)} %copy-done.6, bf16[32,72,512]{2,1,0:T(8,128)(2,1)S(1)} %all_to_all.34.parts_ref, f32[1,512]{1,0:T(1,128)S(1)} %bitcast.12), custom_call_target="tpu_custom_call" | custom-call | tf_op jit(solution)/shard_map/attention/pallas_call | solution.py:428
  150.6 8.1 %all-to-all-done.5.parts_ref = bf16[16,8,512]{2,1,0:T(8,128)(2,1)S(1)} async-done(((bf16[16,8,512]{2,1,0:T(8,128)(2,1)}), bf16[16,8,512]{2,1,0:T(8,128)(2,1)S(1)}, u32[]{:S(2)}, u32[]{:S(2)}) %all-to-all-start.5) | async-done | bytes 131104 | tf_op jit(solution)/shard_map/all_to_all | solution.py:386
  158.7 0.6 sum_z.1
Async XLA Ops:
  0.6 60.0 %copy-start.7 = (f32[512]{0:T(512)S(1)}, f32[512]{0:T(512)}, u32[]{:S(2)}) copy-start(f32[512]{0:T(512)} %param.14) | copy-start | bytes 6148
  61.3 42.5 %copy-start.3 = (bf16[1,4096,128]{2,1,0:T(8,128)(2,1)S(1)}, bf16[1,4096,128]{2,1,0:T(8,128)(2,1)}, u32[]{:S(2)}) copy-start(bf16[1,4096,128]{2,1,0:T(8,128)(2,1)} %param.17) | copy-start | bytes 3145732
  61.4 42.5 %copy-start.4 = (bf16[1,4096,128]{2,1,0:T(8,128)(2,1)S(1)}, bf16[1,4096,128]{2,1,0:T(8,128)(2,1)}, u32[]{:S(2)}) copy-start(bf16[1,4096,128]{2,1,0:T(8,128)(2,1)} %param.18) | copy-start | bytes 3145732
  61.4 42.5 %copy-start.5 = (bf16[1,128,4096]{2,1,0:T(8,128)(2,1)S(1)}, bf16[1,128,4096]{2,1,0:T(8,128)(2,1)}, u32[]{:S(2)}) copy-start(bf16[1,128,4096]{2,1,0:T(8,128)(2,1)} %param.19) | copy-start | bytes 3145732
  141.2 5.4 %copy-start = (bf16[2,256,512]{2,1,0:T(8,128)(2,1)S(1)}, bf16[2,256,512]{2,1,0:T(8,128)(2,1)}, u32[]{:S(2)}) copy-start(bf16[2,256,512]{2,1,0:T(8,128)(2,1)} %q_ref.1) | copy-start | bytes 1572868
  141.2 5.4 %copy-start.1 = (bf16[2,256,512]{2,1,0:T(8,128)(2,1)S(1)}, bf16[2,256,512]{2,1,0:T(8,128)(2,1)}, u32[]{:S(2)}) copy-start(bf16[2,256,512]{2,1,0:T(8,128)(2,1)} %k_ref.1) | copy-start | bytes 1572868
  141.2 5.4 %copy-start.6 = (f32[8,256]{1,0:T(8,128)S(1)}, f32[8,256]{1,0:T(8,128)}, u32[]{:S(2)}) copy-start(f32[8,256]{1,0:T(8,128)} %get-tuple-element.6.run_ref) | copy-start | bytes 24580
  142.3 16.4 %all-to-all-start.5 = ((bf16[16,8,512]{2,1,0:T(8,128)(2,1)}), bf16[16,8,512]{2,1,0:T(8,128)(2,1)S(1)}, u32[]{:S(2)}, u32[]{:S(2)}) async-start(bf16[16,8,512]{2,1,0:T(8,128)(2,1)} %bitcast.7), calls=%async_computation.5 | async-start | bytes 262144 | tf_op jit(solution)/shard_map/all_to_all | solution.py:386
  146.6 1.0 copy-start.2

commit v9 on v8

--- a/solution.py
+++ b/solution.py
@@ -26,21 +26,23 @@
 AT_Q = AT_LOGS + 8
 AT_LOCAL = AT_Q + 8
 AT_FACTS = AT_LOCAL + 16
+MSG = AT_FACTS + 16
 AT_ROUTE = 64
 AT_MINE = 96
 F32 = jnp.float32
 BF16 = jnp.bfloat16
 
 
-def call(kernel, out, name, scratch=(), places=None):
-    vmem = pl.BlockSpec(memory_space=pltpu.VMEM)
-    specs = {}
+def call(kernel, out, name, scratch=(), places=None, results=None):
+    vmem, own = pl.BlockSpec(memory_space=pltpu.VMEM), pl.BlockSpec(memory_space=pl.ANY)
+    specs = {"out_specs": jax.tree.map(lambda _: vmem, out)}
     if places:
-        specs["in_specs"] = [pl.BlockSpec(memory_space=pl.ANY) if p else vmem for p in places]
+        specs["in_specs"] = [own if p else vmem for p in places]
+    if results:
+        specs["out_specs"] = tuple(own if p else vmem for p in results)
     return pl.pallas_call(
         kernel,
         out_shape=out,
-        out_specs=jax.tree.map(lambda _: vmem, out),
         scratch_shapes=scratch,
         compiler_params=pltpu.CompilerParams(vmem_limit_bytes=(56 if places else 40) * 2**20),
         name=name,
@@ -116,47 +118,68 @@
 
 
 def update_kernel(*refs):
-    sources, (run_ref, msg_ref), fetched = refs[:6], refs[6:8], refs[8:14]
-    facts_ref, semaphores = refs[14:]
-    copies = []
-    for i, (source, target) in enumerate(zip(sources, fetched)):
-        part = source.at[:, pl.ds(0, FEW)] if i == 1 else source
-        copies.append(pltpu.make_async_copy(part, target, semaphores.at[i]))
-    for copy in copies:
-        copy.start()
+    sources, (run_ref, msg_hbm), fetched = refs[:6], refs[6:8], refs[8:14]
+    msg_ref, facts_ref, semaphores = refs[14:]
+
+    def copy(i, source, target):
+        return pltpu.make_async_copy(source, target, semaphores.at[i])
+
     decay_ref, q_ref, k_ref, v_ref, ids_ref, gates_ref = fetched
-    for i in (0, 4, 5):
-        copies[i].wait()
+    first = [copy(i, sources[i], fetched[i]) for i in (0, 4, 5)]
+    first.append(copy(1, sources[1].at[:, pl.ds(0, FEW)], q_ref))
+    halves = [
+        [copy(6 + 2 * b + j, sources[2 + j].at[b], fetched[2 + j].at[b]) for j in range(2)]
+        for b in range(2)
+    ]
+    for fetch in first + halves[0] + halves[1]:
+        fetch.start()
+    for fetch in first:
+        fetch.wait()
     running = prefix_sums(jnp.concatenate([decay_ref[0], decay_ref[1]], axis=0))
     run_ref[...] = running
     end = running[:, TOK - 1 :]
     to_end = jnp.exp(end - running).T
     columns = running.T[:FEW]
     route_facts(ids_ref, gates_ref, facts_ref)
-    for i in (1, 2, 3):
-        copies[i].wait()
-    for owner in range(X):
-        parts, logs, qs, locals_ = [], [], [], []
-        for i in range(OWN):
-            b, pair, cols = i, i * HEADS + owner, pl.ds(owner * HD, HD)
+    logs, qs, locals_ = ([[] for _ in range(X)] for _ in range(3))
+    sent = []
+    for b in range(OWN):
+        for fetch in halves[b]:
+            fetch.wait()
+        for owner in range(X):
+            pair, cols = b * HEADS + owner, pl.ds(owner * HD, HD)
             decayed = (k_ref[b, :, cols].astype(F32) * to_end[:, pair : pair + 1]).astype(BF16)
-            parts.append(
-                lax.dot_general(
-                    v_ref[b, :, cols], decayed, (((0,), (0,)), ((), ())), preferred_element_type=F32
-                )
-            )
-            logs += [jnp.broadcast_to(p, (1, HD)) for p in split_log(end[pair : pair + 1])]
-            q, column = q_ref[b, :FEW, cols], columns[:, pair : pair + 1]
+            msg_ref[owner, pl.ds(b * HD, HD)] = lax.dot_general(
+                v_ref[b, :, cols], decayed, (((0,), (0,)), ((), ())), preferred_element_type=F32
+            ).astype(BF16)
+            logs[owner] += [jnp.broadcast_to(p, (1, HD)) for p in split_log(end[pair : pair + 1])]
+            q, column = q_ref[b, :, cols], columns[:, pair : pair + 1]
             weights = fading_scores(
                 q, k_ref[b, :FEW, cols], column, running[pair : pair + 1, :FEW]
             )
             local = jnp.dot(weights, v_ref[b, :FEW, cols], preferred_element_type=F32)
-            locals_.append(local[:8])
-            qs.append((q.astype(F32) * jnp.exp(column))[:8])
-        local = two_parts(beside(*locals_))
-        msg_ref[owner] = jnp.concatenate(
-            parts + [stacked_rows(logs), beside(*qs), local[0], local[1], facts_ref[...]], axis=0
-        ).astype(BF16)
+            locals_[owner].append(local[:8])
+            qs[owner].append((q.astype(F32) * jnp.exp(column))[:8])
+        if b == OWN - 1:
+            for owner in range(X):
+                local = two_parts(beside(*locals_[owner]))
+                facts = facts_ref[...]
+                msg_ref[owner, pl.ds(AT_LOGS, MSG - AT_LOGS)] = jnp.concatenate(
+                    [
+                        stacked_rows(logs[owner]),
+                        beside(*qs[owner]),
+                        local[0],
+                        local[1],
+                        facts,
+                        jnp.zeros_like(facts),
+                    ],
+                    axis=0,
+                ).astype(BF16)
+        rows = pl.ds(b * HD, HD if b < OWN - 1 else MSG - b * HD)
+        sent.append(copy(10 + b, msg_ref.at[:, rows], msg_hbm.at[:, rows]))
+        sent[-1].start()
+    for send in sent:
+        send.wait()
 
 
 def placed(rows, i, x):
@@ -175,7 +198,7 @@
     lane = lax.broadcasted_iota(jnp.int32, (8, HD), 1)
     facts = jnp.zeros((8, HD), F32)
     for x in range(X):
-        own = msg_ref[x].astype(F32)[AT_FACTS:]
+        own = msg_ref[x].astype(F32)[AT_FACTS : AT_FACTS + 8]
         for b in range(2):
             only = jnp.where(lane // HALF == b, own, 0.0)
             shift = b * 16 + x * HALF - b * HALF
@@ -394,7 +417,7 @@
     gain = norm_gain.reshape(1, COLS)
     running, message = call(
         update_kernel,
-        (shape((PAIRS, TOK), F32), shape((X, AT_FACTS + 8, HD), BF16)),
+        (shape((PAIRS, TOK), F32), shape((X, MSG, HD), BF16)),
         "update",
         [
             pltpu.VMEM((2, HEADS, TOK), F32),
@@ -403,10 +426,12 @@
             pltpu.VMEM((2, TOK, COLS), BF16),
             pltpu.VMEM((2, MROWS), jnp.int32),
             pltpu.VMEM((2, MROWS), F32),
+            pltpu.VMEM((X, MSG, HD), BF16),
             pltpu.VMEM((8, HD), F32),
-            pltpu.SemaphoreType.DMA((6,)),
+            pltpu.SemaphoreType.DMA((12,)),
         ],
         [True] * 6,
+        [False, True],
     )(decay, queries, keys, values, expert_ids.T, gate_weights.T)
     message = swap(message, "x")
     groups = call(group_kernel, shape((Z, PART + 24, HD), BF16), "group")(message)

time: 160 us -> 161 us (level)
  no operation moved by 1% of the time
where the time goes in v9:
time: 161 us; the launch traced here: 160 us
  blocking collectives  133 us (83%)
  Pallas kernels  12.5 us (8%)
  waiting for transfers between devices  8.11 us (5%)
  starting transfers between devices  4.18 us (3%)
    all_to_all x5, blocking collectives, swap(): return lax.all_to_all(array, axis, 0, 0, tiled=True)  133 us
    all_to_all x1, waiting for transfers between devices, swap(): return lax.all_to_all(array, axis, 0, 0, tiled=True)  8.11 us
    all_to_all x1, starting transfers between devices, swap(): return lax.all_to_all(array, axis, 0, 0, tiled=True)  4.18 us
    pallas_call x1, Pallas kernels, body(): call(update_kernel, (shape((PAIRS, TOK), F32), shape((X, MSG, HD), BF16))...  3.99 us
  transfers between devices with their start and end apart: 1, of which 1 were waited for; matrix products, arithmetic and copies ran while one was open for 0% of the time, Pallas kernels for 2%

profile of v9, /device:TPU:1, one launch (start us, length us, event | category | flops | bytes accessed | tf_op | source)
XLA Modules:
  0.0 159.9 jit_solution(15972909642642206774)
XLA Ops:
  0.6 0.0 copy-start.7
  0.6 4.0 %update.1 = (f32[8,256]{1,0:T(8,128)}, bf16[4,304,128]{2,1,0:T(8,128)(2,1)}) custom-call(f32[2,4,256]{2,1,0:T(4,128)} %bitcast.13, bf16[2,256,512]{2,1,0:T(8,128)(2,1)} %q_ref.1, bf16[2,256,512]{2,1,0:T(8,128)(2,1)} %k_ref.1, bf16[2,256,512]{2,1,0:T(8,128)(2,1)} %v_ref.1, s32[2,8]{1,0:T(2,128)} %bitcast.14, f32[2,8]{1,0:T(2,128)} %bitcast.15), custom_call_target="tpu_custom_call" | custom-call | tf_op jit(solution)/shard_map/update/pallas_call | solution.py:418
  4.6 10.6 %all_to_all.30.msg_ref = bf16[4,304,128]{2,1,0:T(8,128)(2,1)S(1)} all-to-all(bf16[4,304,128]{2,1,0:T(8,128)(2,1)} %get-tuple-element.7), channel_id=1, replica_groups=mesh['z'=16,'x'=4,'y'=4,'core'=2] {'x'}, dimensions={0} | all-to-all | bytes 622592 | tf_op jit(solution)/shard_map/all_to_all | solution.py:409
  15.3 0.3 group.1
  15.6 27.1 %all_to_all.31.msg_ref = bf16[16,40,128]{2,1,0:T(8,128)(2,1)S(1)} all-to-all(bf16[16,40,128]{2,1,0:T(8,128)(2,1)S(1)} %group.1), channel_id=1, replica_groups=mesh['z'=16,'x'=4,'y'=4,'core'=2] {'z'}, dimensions={0} | all-to-all | bytes 327680 | tf_op jit(solution)/shard_map/all_to_all | solution.py:409
  42.7 0.3 scan.1
  43.1 18.2 %all_to_all.32.back_ref = bf16[16,48,128]{2,1,0:T(8,128)(2,1)S(1)} all-to-all(bf16[16,48,128]{2,1,0:T(8,128)(2,1)S(1)} %get-tuple-element.8), channel_id=1, replica_groups=mesh['z'=16,'x'=4,'y'=4,'core'=2] {'z'}, dimensions={0} | all-to-all | bytes 393216 | tf_op jit(solution)/shard_map/all_to_all | solution.py:409
  61.3 0.0 copy-done.7
  61.3 0.8 expand.1
  62.1 0.0 copy-start.3
  62.1 0.0 copy-start.4
  62.1 0.0 copy-start.5
  62.1 42.3 %all_to_all.33.rows_ref = bf16[32,288,128]{2,1,0:T(8,128)(2,1)S(1)} all-to-all(bf16[32,288,128]{2,1,0:T(8,128)(2,1)S(1)} %expand.1), channel_id=1, replica_groups=mesh['z'=16,'x'=4,'y'=4,'core'=2] {'x','y','core'}, dimensions={0} | all-to-all | bytes 4718592 | tf_op jit(solution)/shard_map/all_to_all | solution.py:409
  104.4 0.0 copy-done.3
  104.4 0.0 copy-done.4
  104.4 0.0 copy-done.5
  104.4 2.4 %experts.1 = bf16[32,72,512]{2,1,0:T(8,128)(2,1)S(1)} custom-call(bf16[32,288,128]{2,1,0:T(8,128)(2,1)S(1)} %all_to_all.33.rows_ref, bf16[4096,128]{1,0:T(8,128)(2,1)S(1)} %bitcast.8, bf16[4096,128]{1,0:T(8,128)(2,1)S(1)} %bitcast.9, bf16[128,4096]{1,0:T(8,128)(2,1)S(1)} %bitcast.10), custom_call_target="tpu_custom_call" | custom-call | tf_op jit(solution)/shard_map/experts/pallas_call | solution.py:449
  106.8 34.9 %all_to_all.34.parts_ref = bf16[32,72,512]{2,1,0:T(8,128)(2,1)S(1)} all-to-all(bf16[32,72,512]{2,1,0:T(8,128)(2,1)S(1)} %experts.1), channel_id=1, replica_groups=mesh['z'=16,'x'=4,'y'=4,'core'=2] {'x','y','core'}, dimensions={0} | all-to-all | bytes 4718592 | tf_op jit(solution)/shard_map/all_to_all | solution.py:409
  141.8 0.0 copy-start
  141.8 0.0 copy-start.1
  141.8 0.0 copy-start.6
  141.8 1.1 combine.1
  142.9 4.2 %all-to-all-start.5 = ((bf16[16,8,512]{2,1,0:T(8,128)(2,1)}), bf16[16,8,512]{2,1,0:T(8,128)(2,1)S(1)}, u32[]{:S(2)}, u32[]{:S(2)}) async-start(bf16[16,8,512]{2,1,0:T(8,128)(2,1)} %bitcast.7), calls=%async_computation.5 | async-start | bytes 262144 | tf_op jit(solution)/shard_map/all_to_all | solution.py:409
  147.1 0.0 copy-done
  147.1 0.0 copy-done.1
  147.1 0.0 copy-done.6
  147.1 0.0 copy-start.2
  147.1 1.0 copy-done.2
  148.2 3.0 %attention.1 = bf16[2,256,512]{2,1,0:T(8,128)(2,1)} custom-call(bf16[2,256,512]{2,1,0:T(8,128)(2,1)S(1)} %copy-done, bf16[2,256,512]{2,1,0:T(8,128)(2,1)S(1)} %copy-done.1, bf16[2,256,512]{2,1,0:T(8,128)(2,1)S(1)} %copy-done.2, f32[8,256]{1,0:T(8,128)S(1)} %copy-done.6, bf16[32,72,512]{2,1,0:T(8,128)(2,1)S(1)} %all_to_all.34.parts_ref, f32[1,512]{1,0:T(1,128)S(1)} %bitcast.12), custom_call_target="tpu_custom_call" | custom-call | tf_op jit(solution)/shard_map/attention/pallas_call | solution.py:453
  151.1 8.1 %all-to-all-done.5.parts_ref = bf16[16,8,512]{2,1,0:T(8,128)(2,1)S(1)} async-done(((bf16[16,8,512]{2,1,0:T(8,128)(2,1)}), bf16[16,8,512]{2,1,0:T(8,128)(2,1)S(1)}, u32[]{:S(2)}, u32[]{:S(2)}) %all-to-all-start.5) | async-done | bytes 131104 | tf_op jit(solution)/shard_map/all_to_all | solution.py:409
  159.2 0.6 sum_z.1
Async XLA Ops:
  0.6 60.7 %copy-start.7 = (f32[512]{0:T(512)S(1)}, f32[512]{0:T(512)}, u32[]{:S(2)}) copy-start(f32[512]{0:T(512)} %param.14) | copy-start | bytes 6148
  62.1 42.4 %copy-start.3 = (bf16[1,4096,128]{2,1,0:T(8,128)(2,1)S(1)}, bf16[1,4096,128]{2,1,0:T(8,128)(2,1)}, u32[]{:S(2)}) copy-start(bf16[1,4096,128]{2,1,0:T(8,128)(2,1)} %param.17) | copy-start | bytes 3145732
  62.1 42.3 %copy-start.4 = (bf16[1,4096,128]{2,1,0:T(8,128)(2,1)S(1)}, bf16[1,4096,128]{2,1,0:T(8,128)(2,1)}, u32[]{:S(2)}) copy-start(bf16[1,4096,128]{2,1,0:T(8,128)(2,1)} %param.18) | copy-start | bytes 3145732
  62.1 42.3 %copy-start.5 = (bf16[1,128,4096]{2,1,0:T(8,128)(2,1)S(1)}, bf16[1,128,4096]{2,1,0:T(8,128)(2,1)}, u32[]{:S(2)}) copy-start(bf16[1,128,4096]{2,1,0:T(8,128)(2,1)} %param.19) | copy-start | bytes 3145732
  141.8 5.3 %copy-start = (bf16[2,256,512]{2,1,0:T(8,128)(2,1)S(1)}, bf16[2,256,512]{2,1,0:T(8,128)(2,1)}, u32[]{:S(2)}) copy-start(bf16[2,256,512]{2,1,0:T(8,128)(2,1)} %q_ref.1) | copy-start | bytes 1572868
  141.8 5.3 %copy-start.1 = (bf16[2,256,512]{2,1,0:T(8,128)(2,1)S(1)}, bf16[2,256,512]{2,1,0:T(8,128)(2,1)}, u32[]{:S(2)}) copy-start(bf16[2,256,512]{2,1,0:T(8,128)(2,1)} %k_ref.1) | copy-start | bytes 1572868
  141.8 5.3 %copy-start.6 = (f32[8,256]{1,0:T(8,128)S(1)}, f32[8,256]{1,0:T(8,128)}, u32[]{:S(2)}) copy-start(f32[8,256]{1,0:T(8,128)} %get-tuple-element.6.run_ref) | copy-start | bytes 24580
  142.9 16.3 %all-to-all-start.5 = ((bf16[16,8,512]{2,1,0:T(8,128)(2,1)}), bf16[16,8,512]{2,1,0:T(8,128)(2,1)S(1)}, u32[]{:S(2)}, u32[]{:S(2)}) async-start(bf16[16,8,512]{2,1,0:T(8,128)(2,1)} %bitcast.7), calls=%async_computation.5 | async-start | bytes 262144 | tf_op jit(solution)/shard_map/all_to_all | solution.py:409
  147.1 1.0 copy-start.2

commit v10 on v8

--- a/solution.py
+++ b/solution.py
@@ -287,7 +287,7 @@
             for x in range(X):
                 at = e * HD + x * 32
                 for target in range(X):
-                    slots_ref[target * EXPERTS + e, pl.ds(x * SLOTS + half * 32, 32)] = sent[
+                    slots_ref[e * X + target, pl.ds(x * SLOTS + half * 32, 32)] = sent[
                         at : at + 32
                     ]
     entering = []
@@ -339,7 +339,7 @@
     for j in range(EXPERTS):
         part = pl.ds(j * COLS, COLS)
         both = jnp.concatenate([gate_ref[part, :], up_ref[part, :]], axis=1)
-        rows = [rows_ref[x * EXPERTS + j, : X * SLOTS] for x in range(X)]
+        rows = [rows_ref[j * X + x, : X * SLOTS] for x in range(X)]
         term = jnp.dot(jnp.concatenate(rows, axis=1), both, preferred_element_type=F32)
         total = term if total is None else total + term
     width = gate_ref.shape[1]
@@ -348,10 +348,10 @@
     for j in range(EXPERTS):
         out = jnp.dot(hidden, down_ref[:, pl.ds(j * COLS, COLS)], preferred_element_type=F32)
         passing = jnp.concatenate(
-            [rows_ref[x * EXPERTS + j, X * SLOTS :].astype(F32) for x in range(X)], axis=1
+            [rows_ref[j * X + x, X * SLOTS :].astype(F32) for x in range(X)], axis=1
         )
         for x in range(X):
-            out_ref[x * EXPERTS + j] = jnp.concatenate(
+            out_ref[j * X + x] = jnp.concatenate(
                 [out[x * SLOTS : (x + 1) * SLOTS], passing[x * PIECE : (x + 1) * PIECE]], axis=0
             ).astype(BF16)
 
@@ -363,9 +363,9 @@
     mix = jnp.where(index == first, gates[0], 0.0) + jnp.where(index == second, gates[1], 0.0)
     rows = []
     for e in range(EXPERTS):
-        total = parts_ref[e, :SLOTS].astype(F32)
+        total = parts_ref[e * X, :SLOTS].astype(F32)
         for x in range(1, X):
-            total = total + parts_ref[x * EXPERTS + e, :SLOTS].astype(F32)
+            total = total + parts_ref[e * X + x, :SLOTS].astype(F32)
         rows.append(total.astype(BF16))
     out_ref[...] = lax.dot_general(
         mix.astype(BF16),
@@ -420,11 +420,11 @@
     slots = call(
         expand_kernel, shape((X * EXPERTS, X * SLOTS + X * PIECE, HD), BF16), "expand"
     )(back, message, gain, facts)
-    slots = swap(slots, ("x", "y", "core"))
+    slots = swap(slots, ("y", "core", "x"))
     parts = call(expert_kernel, shape((X * EXPERTS, SLOTS + PIECE, COLS), BF16), "experts")(
         slots, w_gate[0], w_up[0], w_down[0]
     )
-    parts = swap(parts, ("x", "y", "core"))
+    parts = swap(parts, ("y", "core", "x"))
     attn_out = call(attention_kernel, shape((2, TOK, COLS), BF16), "attention")(
         queries, keys, values, running, parts, gain
     )

time: 160 us -> 161 us (level)
  no operation moved by 1% of the time
where the time goes in v10:
time: 161 us; the launch traced here: 160 us
  blocking collectives  134 us (83%)
  Pallas kernels  11.9 us (7%)
  waiting for transfers between devices  8.11 us (5%)
  starting transfers between devices  4.21 us (3%)
    all_to_all x5, blocking collectives, swap(): return lax.all_to_all(array, axis, 0, 0, tiled=True)  134 us
    all_to_all x1, waiting for transfers between devices, swap(): return lax.all_to_all(array, axis, 0, 0, tiled=True)  8.11 us
    all_to_all x1, starting transfers between devices, swap(): return lax.all_to_all(array, axis, 0, 0, tiled=True)  4.21 us
    pallas_call x1, Pallas kernels, body(): call(update_kernel, (shape((PAIRS, TOK), F32), shape((X, AT_FACTS + 8, HD...  3.38 us
  transfers between devices with their start and end apart: 1, of which 1 were waited for; matrix products, arithmetic and copies ran while one was open for 0% of the time, Pallas kernels for 2%

profile of v10, /device:TPU:1, one launch (start us, length us, event | category | flops | bytes accessed | tf_op | source)
XLA Modules:
  0.0 159.6 jit_solution(11974981871115170754)
XLA Ops:
  0.6 0.0 copy-start.7
  0.6 3.4 %update.1 = (f32[8,256]{1,0:T(8,128)}, bf16[4,296,128]{2,1,0:T(8,128)(2,1)}) custom-call(f32[2,4,256]{2,1,0:T(4,128)} %bitcast.13, bf16[2,256,512]{2,1,0:T(8,128)(2,1)} %q_ref.1, bf16[2,256,512]{2,1,0:T(8,128)(2,1)} %k_ref.1, bf16[2,256,512]{2,1,0:T(8,128)(2,1)} %v_ref.1, s32[2,8]{1,0:T(2,128)} %bitcast.14, f32[2,8]{1,0:T(2,128)} %bitcast.15), custom_call_target="tpu_custom_call" | custom-call | tf_op jit(solution)/shard_map/update/pallas_call | solution.py:395
  4.0 10.6 %all_to_all.30.msg_ref = bf16[4,296,128]{2,1,0:T(8,128)(2,1)S(1)} all-to-all(bf16[4,296,128]{2,1,0:T(8,128)(2,1)} %get-tuple-element.7), channel_id=1, replica_groups=mesh['z'=16,'x'=4,'y'=4,'core'=2] {'x'}, dimensions={0} | all-to-all | bytes 606208 | tf_op jit(solution)/shard_map/all_to_all | solution.py:386
  14.6 0.3 group.1
  15.0 27.1 %all_to_all.31.msg_ref = bf16[16,40,128]{2,1,0:T(8,128)(2,1)S(1)} all-to-all(bf16[16,40,128]{2,1,0:T(8,128)(2,1)S(1)} %group.1), channel_id=1, replica_groups=mesh['z'=16,'x'=4,'y'=4,'core'=2] {'z'}, dimensions={0} | all-to-all | bytes 327680 | tf_op jit(solution)/shard_map/all_to_all | solution.py:386
  42.0 0.3 scan.1
  42.4 18.2 %all_to_all.32.back_ref = bf16[16,48,128]{2,1,0:T(8,128)(2,1)S(1)} all-to-all(bf16[16,48,128]{2,1,0:T(8,128)(2,1)S(1)} %get-tuple-element.8), channel_id=1, replica_groups=mesh['z'=16,'x'=4,'y'=4,'core'=2] {'z'}, dimensions={0} | all-to-all | bytes 393216 | tf_op jit(solution)/shard_map/all_to_all | solution.py:386
  60.6 0.0 copy-done.7
  60.6 0.8 expand.1
  61.3 0.0 copy-start.3
  61.4 0.0 copy-start.4
  61.4 0.0 copy-start.5
  61.4 42.4 %all_to_all.33.rows_ref = bf16[32,288,128]{2,1,0:T(8,128)(2,1)S(1)} all-to-all(bf16[32,288,128]{2,1,0:T(8,128)(2,1)S(1)} %expand.1), channel_id=1, replica_groups=mesh['z'=16,'x'=4,'y'=4,'core'=2] {'y','core','x'}, dimensions={0} | all-to-all | bytes 4718592 | tf_op jit(solution)/shard_map/all_to_all | solution.py:386
  103.8 0.0 copy-done.3
  103.8 0.0 copy-done.4
  103.8 0.0 copy-done.5
  103.8 2.4 %experts.1 = bf16[32,72,512]{2,1,0:T(8,128)(2,1)S(1)} custom-call(bf16[32,288,128]{2,1,0:T(8,128)(2,1)S(1)} %all_to_all.33.rows_ref, bf16[4096,128]{1,0:T(8,128)(2,1)S(1)} %bitcast.8, bf16[4096,128]{1,0:T(8,128)(2,1)S(1)} %bitcast.9, bf16[128,4096]{1,0:T(8,128)(2,1)S(1)} %bitcast.10), custom_call_target="tpu_custom_call" | custom-call | tf_op jit(solution)/shard_map/experts/pallas_call | solution.py:424
  106.2 35.3 %all_to_all.34.parts_ref = bf16[32,72,512]{2,1,0:T(8,128)(2,1)S(1)} all-to-all(bf16[32,72,512]{2,1,0:T(8,128)(2,1)S(1)} %experts.1), channel_id=1, replica_groups=mesh['z'=16,'x'=4,'y'=4,'core'=2] {'y','core','x'}, dimensions={0} | all-to-all | bytes 4718592 | tf_op jit(solution)/shard_map/all_to_all | solution.py:386
  141.4 0.0 copy-start
  141.4 0.0 copy-start.1
  141.4 0.0 copy-start.6
  141.4 1.1 combine.1
  142.6 4.2 %all-to-all-start.5 = ((bf16[16,8,512]{2,1,0:T(8,128)(2,1)}), bf16[16,8,512]{2,1,0:T(8,128)(2,1)S(1)}, u32[]{:S(2)}, u32[]{:S(2)}) async-start(bf16[16,8,512]{2,1,0:T(8,128)(2,1)} %bitcast.7), calls=%async_computation.5 | async-start | bytes 262144 | tf_op jit(solution)/shard_map/all_to_all | solution.py:386
  146.8 0.0 copy-done
  146.8 0.0 copy-done.1
  146.8 0.0 copy-done.6
  146.8 0.0 copy-start.2
  146.8 1.0 copy-done.2
  147.9 3.0 %attention.1 = bf16[2,256,512]{2,1,0:T(8,128)(2,1)} custom-call(bf16[2,256,512]{2,1,0:T(8,128)(2,1)S(1)} %copy-done, bf16[2,256,512]{2,1,0:T(8,128)(2,1)S(1)} %copy-done.1, bf16[2,256,512]{2,1,0:T(8,128)(2,1)S(1)} %copy-done.2, f32[8,256]{1,0:T(8,128)S(1)} %copy-done.6, bf16[32,72,512]{2,1,0:T(8,128)(2,1)S(1)} %all_to_all.34.parts_ref, f32[1,512]{1,0:T(1,128)S(1)} %bitcast.12), custom_call_target="tpu_custom_call" | custom-call | tf_op jit(solution)/shard_map/attention/pallas_call | solution.py:428
  150.8 8.1 %all-to-all-done.5.parts_ref = bf16[16,8,512]{2,1,0:T(8,128)(2,1)S(1)} async-done(((bf16[16,8,512]{2,1,0:T(8,128)(2,1)}), bf16[16,8,512]{2,1,0:T(8,128)(2,1)S(1)}, u32[]{:S(2)}, u32[]{:S(2)}) %all-to-all-start.5) | async-done | bytes 131104 | tf_op jit(solution)/shard_map/all_to_all | solution.py:386
  158.9 0.6 sum_z.1
Async XLA Ops:
  0.6 60.0 %copy-start.7 = (f32[512]{0:T(512)S(1)}, f32[512]{0:T(512)}, u32[]{:S(2)}) copy-start(f32[512]{0:T(512)} %param.14) | copy-start | bytes 6148
  61.3 42.4 %copy-start.3 = (bf16[1,4096,128]{2,1,0:T(8,128)(2,1)S(1)}, bf16[1,4096,128]{2,1,0:T(8,128)(2,1)}, u32[]{:S(2)}) copy-start(bf16[1,4096,128]{2,1,0:T(8,128)(2,1)} %param.17) | copy-start | bytes 3145732
  61.4 42.4 %copy-start.4 = (bf16[1,4096,128]{2,1,0:T(8,128)(2,1)S(1)}, bf16[1,4096,128]{2,1,0:T(8,128)(2,1)}, u32[]{:S(2)}) copy-start(bf16[1,4096,128]{2,1,0:T(8,128)(2,1)} %param.18) | copy-start | bytes 3145732
  61.4 42.4 %copy-start.5 = (bf16[1,128,4096]{2,1,0:T(8,128)(2,1)S(1)}, bf16[1,128,4096]{2,1,0:T(8,128)(2,1)}, u32[]{:S(2)}) copy-start(bf16[1,128,4096]{2,1,0:T(8,128)(2,1)} %param.19) | copy-start | bytes 3145732
  141.4 5.4 %copy-start = (bf16[2,256,512]{2,1,0:T(8,128)(2,1)S(1)}, bf16[2,256,512]{2,1,0:T(8,128)(2,1)}, u32[]{:S(2)}) copy-start(bf16[2,256,512]{2,1,0:T(8,128)(2,1)} %q_ref.1) | copy-start | bytes 1572868
  141.4 5.4 %copy-start.1 = (bf16[2,256,512]{2,1,0:T(8,128)(2,1)S(1)}, bf16[2,256,512]{2,1,0:T(8,128)(2,1)}, u32[]{:S(2)}) copy-start(bf16[2,256,512]{2,1,0:T(8,128)(2,1)} %k_ref.1) | copy-start | bytes 1572868
  141.4 5.4 %copy-start.6 = (f32[8,256]{1,0:T(8,128)S(1)}, f32[8,256]{1,0:T(8,128)}, u32[]{:S(2)}) copy-start(f32[8,256]{1,0:T(8,128)} %get-tuple-element.6.run_ref) | copy-start | bytes 24580
  142.6 16.4 %all-to-all-start.5 = ((bf16[16,8,512]{2,1,0:T(8,128)(2,1)}), bf16[16,8,512]{2,1,0:T(8,128)(2,1)S(1)}, u32[]{:S(2)}, u32[]{:S(2)}) async-start(bf16[16,8,512]{2,1,0:T(8,128)(2,1)} %bitcast.7), calls=%async_computation.5 | async-start | bytes 262144 | tf_op jit(solution)/shard_map/all_to_all | solution.py:386
  146.8 1.0 copy-start.2

commit v11 on v8

--- a/solution.py
+++ b/solution.py
@@ -258,7 +258,7 @@
     facts_ref[...] = jnp.concatenate(facts, axis=1)
 
 
-def expand_kernel(back_ref, msg_ref, gain_ref, facts_ref, slots_ref):
+def expand_kernel(back_ref, msg_ref, gain_ref, facts_ref, own_ref, slots_ref):
     gain = gain_ref[:, :HD]
     for x in range(1, X):
         gain = jnp.where(lax.axis_index("x") == x, gain_ref[:, x * HD : (x + 1) * HD], gain)
@@ -298,14 +298,28 @@
             for i in range(OWN):
                 factor = jnp.exp(joined_log(part, AT_LOGS + 4 * i))
                 state[i] = factor * state[i] + part[i * HD : (i + 1) * HD]
+    here = lax.axis_index("x")
+
+    def state_on(step):
+        there = lax.rem(here + step, X)
+        found = entering[0]
+        for x in range(1, X):
+            found = jnp.where(there == x, entering[x], found)
+        return found
+
+    own_ref[...] = state_on(0).astype(BF16)
+    others = [state_on(step) for step in range(1, X)]
     for m in range(X * EXPERTS):
-        pieces = [own[m * PIECE : (m + 1) * PIECE] for own in entering]
-        slots_ref[m, pl.ds(X * SLOTS, X * PIECE)] = jnp.concatenate(pieces, axis=0).astype(BF16)
-
-
-def attention_kernel(q_ref, k_ref, v_ref, run_ref, parts_ref, gain_ref, out_ref):
+        pieces = [other[m * PIECE : (m + 1) * PIECE] for other in others]
+        slots_ref[m, pl.ds(X * SLOTS, (X - 1) * PIECE)] = jnp.concatenate(pieces, axis=0).astype(
+            BF16
+        )
+
+
+def attention_kernel(q_ref, k_ref, v_ref, run_ref, parts_ref, own_ref, gain_ref, out_ref):
     running = run_ref[...]
     columns = running.T
+    here = lax.axis_index("x")
     pieces = [parts_ref[m].astype(F32)[SLOTS:] for m in range(X * EXPERTS)]
     each = len(pieces) // 2
     states = [
@@ -314,7 +328,9 @@
     for pair in range(PAIRS):
         b, cols = pair // HEADS, pl.ds(pair % HEADS * HD, HD)
         q, column = q_ref[b, :, cols], columns[:, pair : pair + 1]
-        state = states[b][:, pair % HEADS * HD : (pair % HEADS + 1) * HD]
+        head = pair % HEADS
+        state = states[b][:, head * HD : (head + 1) * HD]
+        state = jnp.where(here == head, own_ref[b * HD : (b + 1) * HD], state)
         weights = fading_scores(q, k_ref[b, :, cols], column, running[pair : pair + 1])
         decayed = (q.astype(F32) * jnp.exp(column)).astype(BF16)
         o = jnp.dot(
@@ -347,12 +363,15 @@
     hidden = (gate / (1.0 + jnp.exp(-gate)) * up).astype(BF16)
     for j in range(EXPERTS):
         out = jnp.dot(hidden, down_ref[:, pl.ds(j * COLS, COLS)], preferred_element_type=F32)
-        passing = jnp.concatenate(
-            [rows_ref[x * EXPERTS + j, X * SLOTS :].astype(F32) for x in range(X)], axis=1
-        )
+        parts = [rows_ref[x * EXPERTS + j, X * SLOTS :].astype(F32) for x in range(X)]
         for x in range(X):
+            passing = []
+            for source in range(X):
+                at = (x - source - 1) % X * PIECE
+                piece = parts[source][at : at + PIECE] if source != x else jnp.zeros((PIECE, HD), F32)
+                passing.append(piece)
             out_ref[x * EXPERTS + j] = jnp.concatenate(
-                [out[x * SLOTS : (x + 1) * SLOTS], passing[x * PIECE : (x + 1) * PIECE]], axis=0
+                [out[x * SLOTS : (x + 1) * SLOTS], jnp.concatenate(passing, axis=1)], axis=0
             ).astype(BF16)
 
 
@@ -361,18 +380,15 @@
     place = lax.broadcasted_iota(jnp.int32, (1, GROUP), 1) // MROWS * CAP
     (first, second), gates = slot_rows(facts_ref[:, 4 * HD :], place, SLOTS)
     mix = jnp.where(index == first, gates[0], 0.0) + jnp.where(index == second, gates[1], 0.0)
-    rows = []
-    for e in range(EXPERTS):
-        total = parts_ref[e, :SLOTS].astype(F32)
-        for x in range(1, X):
-            total = total + parts_ref[x * EXPERTS + e, :SLOTS].astype(F32)
-        rows.append(total.astype(BF16))
-    out_ref[...] = lax.dot_general(
-        mix.astype(BF16),
-        jnp.concatenate(rows, axis=0),
-        (((0,), (0,)), ((), ())),
-        preferred_element_type=F32,
-    ).astype(BF16)
+    mix = mix.astype(BF16)
+    total = None
+    for x in range(X):
+        rows = jnp.concatenate(
+            [parts_ref[x * EXPERTS + e, :SLOTS] for e in range(EXPERTS)], axis=0
+        )
+        term = lax.dot_general(mix, rows, (((0,), (0,)), ((), ())), preferred_element_type=F32)
+        total = term if total is None else total + term
+    out_ref[...] = total.astype(BF16)
 
 
 def sum_kernel(parts_ref, out_ref):
@@ -417,8 +433,13 @@
         "scan",
     )(groups)
     back = swap(back, "z")
-    slots = call(
-        expand_kernel, shape((X * EXPERTS, X * SLOTS + X * PIECE, HD), BF16), "expand"
+    own, slots = call(
+        expand_kernel,
+        (
+            shape((OWN * HD, HD), BF16),
+            shape((X * EXPERTS, X * SLOTS + (X - 1) * PIECE, HD), BF16),
+        ),
+        "expand",
     )(back, message, gain, facts)
     slots = swap(slots, ("x", "y", "core"))
     parts = call(expert_kernel, shape((X * EXPERTS, SLOTS + PIECE, COLS), BF16), "experts")(
@@ -426,7 +447,7 @@
     )
     parts = swap(parts, ("x", "y", "core"))
     attn_out = call(attention_kernel, shape((2, TOK, COLS), BF16), "attention")(
-        queries, keys, values, running, parts, gain
+        queries, keys, values, running, parts, own, gain
     )
     share = call(combine_kernel, shape((GROUP, COLS), BF16), "combine")(parts, facts)
     share = swap(share.reshape(Z, MROWS, COLS), "z")

time: 160 us -> 161 us (level)
  no operation moved by 1% of the time
where the time goes in v11:
time: 161 us; the launch traced here: 159 us
  blocking collectives  133 us (83%)
  Pallas kernels  12 us (7%)
  waiting for transfers between devices  7.27 us (5%)
  starting transfers between devices  4.21 us (3%)
  local copies, waits for them, and re-layouts  2.53 us (2%)
    all_to_all x5, blocking collectives, swap(): return lax.all_to_all(array, axis, 0, 0, tiled=True)  133 us
    all_to_all x1, waiting for transfers between devices, swap(): return lax.all_to_all(array, axis, 0, 0, tiled=True)  7.27 us
    all_to_all x1, starting transfers between devices, swap(): return lax.all_to_all(array, axis, 0, 0, tiled=True)  4.21 us
    pallas_call x1, Pallas kernels, body(): call(update_kernel, (shape((PAIRS, TOK), F32), shape((X, AT_FACTS + 8, HD...  3.38 us
  transfers between devices with their start and end apart: 1, of which 1 were waited for; matrix products, arithmetic and copies ran while one was open for 0% of the time, Pallas kernels for 2%

profile of v11, /device:TPU:1, one launch (start us, length us, event | category | flops | bytes accessed | tf_op | source)
XLA Modules:
  0.0 159.4 jit_solution(17302989217265691774)
XLA Ops:
  0.6 0.0 copy-start.9
  0.6 3.4 %update.1 = (f32[8,256]{1,0:T(8,128)}, bf16[4,296,128]{2,1,0:T(8,128)(2,1)}) custom-call(f32[2,4,256]{2,1,0:T(4,128)} %bitcast.13, bf16[2,256,512]{2,1,0:T(8,128)(2,1)} %q_ref.1, bf16[2,256,512]{2,1,0:T(8,128)(2,1)} %k_ref.1, bf16[2,256,512]{2,1,0:T(8,128)(2,1)} %v_ref.1, s32[2,8]{1,0:T(2,128)} %bitcast.14, f32[2,8]{1,0:T(2,128)} %bitcast.15), custom_call_target="tpu_custom_call" | custom-call | tf_op jit(solution)/shard_map/update/pallas_call | solution.py:411
  4.0 10.6 %all_to_all.30.msg_ref = bf16[4,296,128]{2,1,0:T(8,128)(2,1)S(1)} all-to-all(bf16[4,296,128]{2,1,0:T(8,128)(2,1)} %get-tuple-element.9), channel_id=1, replica_groups=mesh['z'=16,'x'=4,'y'=4,'core'=2] {'x'}, dimensions={0} | all-to-all | bytes 606208 | tf_op jit(solution)/shard_map/all_to_all | solution.py:402
  14.6 0.3 group.1
  15.0 27.1 %all_to_all.31.msg_ref = bf16[16,40,128]{2,1,0:T(8,128)(2,1)S(1)} all-to-all(bf16[16,40,128]{2,1,0:T(8,128)(2,1)S(1)} %group.1), channel_id=1, replica_groups=mesh['z'=16,'x'=4,'y'=4,'core'=2] {'z'}, dimensions={0} | all-to-all | bytes 327680 | tf_op jit(solution)/shard_map/all_to_all | solution.py:402
  42.0 0.3 scan.1
  42.4 18.2 %all_to_all.32.back_ref = bf16[16,48,128]{2,1,0:T(8,128)(2,1)S(1)} all-to-all(bf16[16,48,128]{2,1,0:T(8,128)(2,1)S(1)} %get-tuple-element.10), channel_id=1, replica_groups=mesh['z'=16,'x'=4,'y'=4,'core'=2] {'z'}, dimensions={0} | all-to-all | bytes 393216 | tf_op jit(solution)/shard_map/all_to_all | solution.py:402
  60.6 0.0 copy-done.9
  60.6 0.9 expand.1
  61.5 0.0 copy-start.6
  61.5 0.6 copy-done.6
  62.1 0.0 copy-start.3
  62.1 0.0 copy-start.4
  62.1 0.0 copy-start.5
  62.1 41.8 %all_to_all.33.rows_ref = bf16[32,280,128]{2,1,0:T(8,128)(2,1)S(1)} all-to-all(bf16[32,280,128]{2,1,0:T(8,128)(2,1)S(1)} %get-tuple-element.12), channel_id=1, replica_groups=mesh['z'=16,'x'=4,'y'=4,'core'=2] {'x','y','core'}, dimensions={0} | all-to-all | bytes 4587520 | tf_op jit(solution)/shard_map/all_to_all | solution.py:402
  103.9 0.0 copy-done.3
  103.9 0.0 copy-done.4
  103.9 0.0 copy-done.5
  103.9 2.4 %experts.1 = bf16[32,72,512]{2,1,0:T(8,128)(2,1)S(1)} custom-call(bf16[32,280,128]{2,1,0:T(8,128)(2,1)S(1)} %all_to_all.33.rows_ref, bf16[4096,128]{1,0:T(8,128)(2,1)S(1)} %bitcast.8, bf16[4096,128]{1,0:T(8,128)(2,1)S(1)} %bitcast.9, bf16[128,4096]{1,0:T(8,128)(2,1)S(1)} %bitcast.10), custom_call_target="tpu_custom_call" | custom-call | tf_op jit(solution)/shard_map/experts/pallas_call | solution.py:445
  106.3 35.0 %all_to_all.34.parts_ref = bf16[32,72,512]{2,1,0:T(8,128)(2,1)S(1)} all-to-all(bf16[32,72,512]{2,1,0:T(8,128)(2,1)S(1)} %experts.1), channel_id=1, replica_groups=mesh['z'=16,'x'=4,'y'=4,'core'=2] {'x','y','core'}, dimensions={0} | all-to-all | bytes 4718592 | tf_op jit(solution)/shard_map/all_to_all | solution.py:402
  141.3 0.0 copy-start
  141.3 1.1 combine.1
  142.4 4.2 %all-to-all-start.5 = ((bf16[16,8,512]{2,1,0:T(8,128)(2,1)}), bf16[16,8,512]{2,1,0:T(8,128)(2,1)S(1)}, u32[]{:S(2)}, u32[]{:S(2)}) async-start(bf16[16,8,512]{2,1,0:T(8,128)(2,1)} %bitcast.7), calls=%async_computation.5 | async-start | bytes 262144 | tf_op jit(solution)/shard_map/all_to_all | solution.py:402
  146.7 0.0 copy-done
  146.7 0.0 copy-done.1
  146.7 0.0 copy-done.8
  146.7 0.0 copy-start.2
  146.7 1.0 copy-done.2
  147.7 0.8 copy-done.7
  148.6 3.0 %attention.1 = bf16[2,256,512]{2,1,0:T(8,128)(2,1)} custom-call(bf16[2,256,512]{2,1,0:T(8,128)(2,1)S(1)} %copy-done, bf16[2,256,512]{2,1,0:T(8,128)(2,1)S(1)} %copy-done.1, bf16[2,256,512]{2,1,0:T(8,128)(2,1)S(1)} %copy-done.2, f32[8,256]{1,0:T(8,128)S(1)} %copy-done.8, bf16[32,72,512]{2,1,0:T(8,128)(2,1)S(1)} %all_to_all.34.parts_ref, ...), custom_call_target="tpu_custom_call" | custom-call | tf_op jit(solution)/shard_map/attention/pallas_call | solution.py:449
  151.5 7.3 %all-to-all-done.5.parts_ref = bf16[16,8,512]{2,1,0:T(8,128)(2,1)S(1)} async-done(((bf16[16,8,512]{2,1,0:T(8,128)(2,1)}), bf16[16,8,512]{2,1,0:T(8,128)(2,1)S(1)}, u32[]{:S(2)}, u32[]{:S(2)}) %all-to-all-start.5) | async-done | bytes 131104 | tf_op jit(solution)/shard_map/all_to_all | solution.py:402
  158.8 0.6 sum_z.1
  (3 shorter events, 0.0 us)
Async XLA Ops:
  0.6 60.0 %copy-start.9 = (f32[512]{0:T(512)S(1)}, f32[512]{0:T(512)}, u32[]{:S(2)}) copy-start(f32[512]{0:T(512)} %param.14) | copy-start | bytes 6148
  61.5 0.6 copy-start.6
  62.1 41.8 %copy-start.3 = (bf16[1,4096,128]{2,1,0:T(8,128)(2,1)S(1)}, bf16[1,4096,128]{2,1,0:T(8,128)(2,1)}, u32[]{:S(2)}) copy-start(bf16[1,4096,128]{2,1,0:T(8,128)(2,1)} %param.17) | copy-start | bytes 3145732
  62.1 41.8 %copy-start.4 = (bf16[1,4096,128]{2,1,0:T(8,128)(2,1)S(1)}, bf16[1,4096,128]{2,1,0:T(8,128)(2,1)}, u32[]{:S(2)}) copy-start(bf16[1,4096,128]{2,1,0:T(8,128)(2,1)} %param.18) | copy-start | bytes 3145732
  62.1 41.8 %copy-start.5 = (bf16[1,128,4096]{2,1,0:T(8,128)(2,1)S(1)}, bf16[1,128,4096]{2,1,0:T(8,128)(2,1)}, u32[]{:S(2)}) copy-start(bf16[1,128,4096]{2,1,0:T(8,128)(2,1)} %param.19) | copy-start | bytes 3145732
  141.3 5.4 %copy-start = (bf16[2,256,512]{2,1,0:T(8,128)(2,1)S(1)}, bf16[2,256,512]{2,1,0:T(8,128)(2,1)}, u32[]{:S(2)}) copy-start(bf16[2,256,512]{2,1,0:T(8,128)(2,1)} %q_ref.1) | copy-start | bytes 1572868
  141.3 5.4 %copy-start.1 = (bf16[2,256,512]{2,1,0:T(8,128)(2,1)S(1)}, bf16[2,256,512]{2,1,0:T(8,128)(2,1)}, u32[]{:S(2)}) copy-start(bf16[2,256,512]{2,1,0:T(8,128)(2,1)} %k_ref.1) | copy-start | bytes 1572868
  141.3 5.4 %copy-start.8 = (f32[8,256]{1,0:T(8,128)S(1)}, f32[8,256]{1,0:T(8,128)}, u32[]{:S(2)}) copy-start(f32[8,256]{1,0:T(8,128)} %get-tuple-element.8.run_ref) | copy-start | bytes 24580
  142.4 16.4 %all-to-all-start.5 = ((bf16[16,8,512]{2,1,0:T(8,128)(2,1)}), bf16[16,8,512]{2,1,0:T(8,128)(2,1)S(1)}, u32[]{:S(2)}, u32[]{:S(2)}) async-start(bf16[16,8,512]{2,1,0:T(8,128)(2,1)} %bitcast.7), calls=%async_computation.5 | async-start | bytes 262144 | tf_op jit(solution)/shard_map/all_to_all | solution.py:402
  146.7 1.0 copy-start.2
  147.7 0.8 copy-start.7

commit v12 on v11

--- a/solution.py
+++ b/solution.py
@@ -122,8 +122,8 @@
     for i, (source, target) in enumerate(zip(sources, fetched)):
         part = source.at[:, pl.ds(0, FEW)] if i == 1 else source
         copies.append(pltpu.make_async_copy(part, target, semaphores.at[i]))
-    for copy in copies:
-        copy.start()
+    for i in (0, 4, 5, 2, 3, 1):
+        copies[i].start()
     decay_ref, q_ref, k_ref, v_ref, ids_ref, gates_ref = fetched
     for i in (0, 4, 5):
         copies[i].wait()

time: 161 us -> 161 us (level)
  no operation moved by 1% of the time
where the time goes in v12:
time: 161 us; the launch traced here: 159 us
  blocking collectives  133 us (83%)
  Pallas kernels  11.7 us (7%)
  waiting for transfers between devices  7.26 us (5%)
  starting transfers between devices  4.21 us (3%)
  local copies, waits for them, and re-layouts  2.53 us (2%)
    all_to_all x5, blocking collectives, swap(): return lax.all_to_all(array, axis, 0, 0, tiled=True)  133 us
    all_to_all x1, waiting for transfers between devices, swap(): return lax.all_to_all(array, axis, 0, 0, tiled=True)  7.26 us
    all_to_all x1, starting transfers between devices, swap(): return lax.all_to_all(array, axis, 0, 0, tiled=True)  4.21 us
  transfers between devices with their start and end apart: 1, of which 1 were waited for; matrix products, arithmetic and copies ran while one was open for 0% of the time, Pallas kernels for 2%

profile of v12, /device:TPU:1, one launch (start us, length us, event | category | flops | bytes accessed | tf_op | source)
XLA Modules:
  0.0 159.1 jit_solution(17477095590728251829)
XLA Ops:
  0.6 0.0 copy-start.9
  0.6 3.0 %update.1 = (f32[8,256]{1,0:T(8,128)}, bf16[4,296,128]{2,1,0:T(8,128)(2,1)}) custom-call(f32[2,4,256]{2,1,0:T(4,128)} %bitcast.13, bf16[2,256,512]{2,1,0:T(8,128)(2,1)} %q_ref.1, bf16[2,256,512]{2,1,0:T(8,128)(2,1)} %k_ref.1, bf16[2,256,512]{2,1,0:T(8,128)(2,1)} %v_ref.1, s32[2,8]{1,0:T(2,128)} %bitcast.14, f32[2,8]{1,0:T(2,128)} %bitcast.15), custom_call_target="tpu_custom_call" | custom-call | tf_op jit(solution)/shard_map/update/pallas_call | solution.py:411
  3.7 10.6 %all_to_all.30.msg_ref = bf16[4,296,128]{2,1,0:T(8,128)(2,1)S(1)} all-to-all(bf16[4,296,128]{2,1,0:T(8,128)(2,1)} %get-tuple-element.9), channel_id=1, replica_groups=mesh['z'=16,'x'=4,'y'=4,'core'=2] {'x'}, dimensions={0} | all-to-all | bytes 606208 | tf_op jit(solution)/shard_map/all_to_all | solution.py:402
  14.3 0.3 group.1
  14.6 27.1 %all_to_all.31.msg_ref = bf16[16,40,128]{2,1,0:T(8,128)(2,1)S(1)} all-to-all(bf16[16,40,128]{2,1,0:T(8,128)(2,1)S(1)} %group.1), channel_id=1, replica_groups=mesh['z'=16,'x'=4,'y'=4,'core'=2] {'z'}, dimensions={0} | all-to-all | bytes 327680 | tf_op jit(solution)/shard_map/all_to_all | solution.py:402
  41.7 0.3 scan.1
  42.0 18.2 %all_to_all.32.back_ref = bf16[16,48,128]{2,1,0:T(8,128)(2,1)S(1)} all-to-all(bf16[16,48,128]{2,1,0:T(8,128)(2,1)S(1)} %get-tuple-element.10), channel_id=1, replica_groups=mesh['z'=16,'x'=4,'y'=4,'core'=2] {'z'}, dimensions={0} | all-to-all | bytes 393216 | tf_op jit(solution)/shard_map/all_to_all | solution.py:402
  60.3 0.0 copy-done.9
  60.3 0.9 expand.1
  61.1 0.0 copy-start.6
  61.2 0.6 copy-done.6
  61.8 0.0 copy-start.3
  61.8 0.0 copy-start.4
  61.8 41.8 %all_to_all.33.rows_ref = bf16[32,280,128]{2,1,0:T(8,128)(2,1)S(1)} all-to-all(bf16[32,280,128]{2,1,0:T(8,128)(2,1)S(1)} %get-tuple-element.12), channel_id=1, replica_groups=mesh['z'=16,'x'=4,'y'=4,'core'=2] {'x','y','core'}, dimensions={0} | all-to-all | bytes 4587520 | tf_op jit(solution)/shard_map/all_to_all | solution.py:402
  103.6 0.0 copy-done.3
  103.6 0.0 copy-done.4
  103.6 0.0 copy-done.5
  103.6 2.4 %experts.1 = bf16[32,72,512]{2,1,0:T(8,128)(2,1)S(1)} custom-call(bf16[32,280,128]{2,1,0:T(8,128)(2,1)S(1)} %all_to_all.33.rows_ref, bf16[4096,128]{1,0:T(8,128)(2,1)S(1)} %bitcast.8, bf16[4096,128]{1,0:T(8,128)(2,1)S(1)} %bitcast.9, bf16[128,4096]{1,0:T(8,128)(2,1)S(1)} %bitcast.10), custom_call_target="tpu_custom_call" | custom-call | tf_op jit(solution)/shard_map/experts/pallas_call | solution.py:445
  106.0 35.0 %all_to_all.34.parts_ref = bf16[32,72,512]{2,1,0:T(8,128)(2,1)S(1)} all-to-all(bf16[32,72,512]{2,1,0:T(8,128)(2,1)S(1)} %experts.1), channel_id=1, replica_groups=mesh['z'=16,'x'=4,'y'=4,'core'=2] {'x','y','core'}, dimensions={0} | all-to-all | bytes 4718592 | tf_op jit(solution)/shard_map/all_to_all | solution.py:402
  141.0 0.0 copy-start
  141.0 0.0 copy-start.1
  141.0 1.1 combine.1
  142.1 4.2 %all-to-all-start.5 = ((bf16[16,8,512]{2,1,0:T(8,128)(2,1)}), bf16[16,8,512]{2,1,0:T(8,128)(2,1)S(1)}, u32[]{:S(2)}, u32[]{:S(2)}) async-start(bf16[16,8,512]{2,1,0:T(8,128)(2,1)} %bitcast.7), calls=%async_computation.5 | async-start | bytes 262144 | tf_op jit(solution)/shard_map/all_to_all | solution.py:402
  146.3 0.0 copy-done
  146.3 0.0 copy-done.1
  146.3 0.0 copy-done.8
  146.4 0.0 copy-start.2
  146.4 1.0 copy-done.2
  147.4 0.8 copy-done.7
  148.2 3.0 %attention.1 = bf16[2,256,512]{2,1,0:T(8,128)(2,1)} custom-call(bf16[2,256,512]{2,1,0:T(8,128)(2,1)S(1)} %copy-done, bf16[2,256,512]{2,1,0:T(8,128)(2,1)S(1)} %copy-done.1, bf16[2,256,512]{2,1,0:T(8,128)(2,1)S(1)} %copy-done.2, f32[8,256]{1,0:T(8,128)S(1)} %copy-done.8, bf16[32,72,512]{2,1,0:T(8,128)(2,1)S(1)} %all_to_all.34.parts_ref, ...), custom_call_target="tpu_custom_call" | custom-call | tf_op jit(solution)/shard_map/attention/pallas_call | solution.py:449
  151.2 7.3 %all-to-all-done.5.parts_ref = bf16[16,8,512]{2,1,0:T(8,128)(2,1)S(1)} async-done(((bf16[16,8,512]{2,1,0:T(8,128)(2,1)}), bf16[16,8,512]{2,1,0:T(8,128)(2,1)S(1)}, u32[]{:S(2)}, u32[]{:S(2)}) %all-to-all-start.5) | async-done | bytes 131104 | tf_op jit(solution)/shard_map/all_to_all | solution.py:402
  158.5 0.6 sum_z.1
  (3 shorter events, 0.0 us)
Async XLA Ops:
  0.6 59.6 %copy-start.9 = (f32[512]{0:T(512)S(1)}, f32[512]{0:T(512)}, u32[]{:S(2)}) copy-start(f32[512]{0:T(512)} %param.14) | copy-start | bytes 6148
  61.1 0.6 copy-start.6
  61.8 41.8 %copy-start.3 = (bf16[1,4096,128]{2,1,0:T(8,128)(2,1)S(1)}, bf16[1,4096,128]{2,1,0:T(8,128)(2,1)}, u32[]{:S(2)}) copy-start(bf16[1,4096,128]{2,1,0:T(8,128)(2,1)} %param.17) | copy-start | bytes 3145732
  61.8 41.8 %copy-start.4 = (bf16[1,4096,128]{2,1,0:T(8,128)(2,1)S(1)}, bf16[1,4096,128]{2,1,0:T(8,128)(2,1)}, u32[]{:S(2)}) copy-start(bf16[1,4096,128]{2,1,0:T(8,128)(2,1)} %param.18) | copy-start | bytes 3145732
  61.8 41.8 %copy-start.5 = (bf16[1,128,4096]{2,1,0:T(8,128)(2,1)S(1)}, bf16[1,128,4096]{2,1,0:T(8,128)(2,1)}, u32[]{:S(2)}) copy-start(bf16[1,128,4096]{2,1,0:T(8,128)(2,1)} %param.19) | copy-start | bytes 3145732
  141.0 5.4 %copy-start = (bf16[2,256,512]{2,1,0:T(8,128)(2,1)S(1)}, bf16[2,256,512]{2,1,0:T(8,128)(2,1)}, u32[]{:S(2)}) copy-start(bf16[2,256,512]{2,1,0:T(8,128)(2,1)} %q_ref.1) | copy-start | bytes 1572868
  141.0 5.4 %copy-start.1 = (bf16[2,256,512]{2,1,0:T(8,128)(2,1)S(1)}, bf16[2,256,512]{2,1,0:T(8,128)(2,1)}, u32[]{:S(2)}) copy-start(bf16[2,256,512]{2,1,0:T(8,128)(2,1)} %k_ref.1) | copy-start | bytes 1572868
  141.0 5.4 %copy-start.8 = (f32[8,256]{1,0:T(8,128)S(1)}, f32[8,256]{1,0:T(8,128)}, u32[]{:S(2)}) copy-start(f32[8,256]{1,0:T(8,128)} %get-tuple-element.8.run_ref) | copy-start | bytes 24580
  142.1 16.4 %all-to-all-start.5 = ((bf16[16,8,512]{2,1,0:T(8,128)(2,1)}), bf16[16,8,512]{2,1,0:T(8,128)(2,1)S(1)}, u32[]{:S(2)}, u32[]{:S(2)}) async-start(bf16[16,8,512]{2,1,0:T(8,128)(2,1)} %bitcast.7), calls=%async_computation.5 | async-start | bytes 262144 | tf_op jit(solution)/shard_map/all_to_all | solution.py:402
  146.4 1.0 copy-start.2
  147.4 0.8 copy-start.7
